TPU v7x, 32 devices: a whole 2x2x4 slice. The times are simulated.
32 devices in a mesh: dp: 16 (over z, y, x), tp: 2 (over core).
Axes of the slice: x: 2, y: 2, z: 4, core: 2. Of those that a mesh axis runs over, the one named last changes fastest.
Arguments:
- block_input: bfloat16 [128, 197, 768], P('dp'), may hold values from -6 to 6
- cotangent: float32 [128, 197, 768], P('dp'), may hold values from -6 to 6
- mask_patches: int32 [128, 75], P('dp'), may hold values from 0 to 195, as said below
- owners: int32 [48], replicated, may hold values from 0 to 15, as said below
- master_slots: float32 [48, 2, 384, 384], P('dp', 'tp'), may hold values from -0.21875 to 0.21875
- left_bases: float32 [48, 2, 384, 384], P('dp', 'tp'), as said below
- right_bases: float32 [48, 2, 384, 384], P('dp', 'tp'), as said below
- first_moment: float32 [48, 2, 384, 384], P('dp', 'tp'), may hold values from -0.00390625 to 0.00390625
- second_moment: float32 [48, 2, 384, 384], P('dp', 'tp'), may hold values from 7.064254e-08 to 2.8257017e-07
- shared_vectors: float32 [2, 6, 768], replicated
- shared_first: float32 [2, 6, 768], replicated, may hold values from -0.00390625 to 0.00390625
- shared_second: float32 [2, 6, 768], replicated, may hold values from 7.064254e-08 to 2.8257017e-07
- split_vectors: float32 [2, 6, 768], P(None, None, 'tp'), may hold values from -2 to 2
- split_first: float32 [2, 6, 768], P(None, None, 'tp'), may hold values from -0.00390625 to 0.00390625
- split_second: float32 [2, 6, 768], P(None, None, 'tp'), may hold values from 7.064254e-08 to 2.8257017e-07
Outputs:
- block_output: float32 [128, 197, 768], P('dp')
- input_grad: float32 [128, 197, 768], P('dp')
- new_master: float32 [48, 2, 384, 384], P('dp', 'tp')
- new_first: float32 [48, 2, 384, 384], P('dp', 'tp')
- new_second: float32 [48, 2, 384, 384], P('dp', 'tp')
- new_shared: float32 [2, 6, 768], replicated
- new_shared_first: float32 [2, 6, 768], replicated
- new_shared_second: float32 [2, 6, 768], replicated
- new_split: float32 [2, 6, 768], P(None, None, 'tp')
- new_split_first: float32 [2, 6, 768], P(None, None, 'tp')
- new_split_second: float32 [2, 6, 768], P(None, None, 'tp')
- layer_norms: float32 [2], replicated
- global_norm: float32 [], replicated
Inputs may be any that keep to these rules, and one draw needn't show every extreme that they name: `owners`: no index of dp owns more than 3 of the 48 blocks, and some index owns exactly 3. `mask_patches`: each row names 75 distinct patches. `left_bases`: each block's basis is orthogonal. `right_bases`: each block's basis is orthogonal.
All inputs are finite; a program needn't handle non-finite values.
Results may differ from a plain program's by a relative error of at most 0.022.
Values may be sent and summed in bfloat16 or wider, within the bound.
A program may use at most 320 MiB of HBM per device.

v0:
```python
import math

import jax
import jax.numpy as jnp
from jax import lax
from jax.sharding import PartitionSpec as P

DH = 64


HIGHEST = lax.Precision.HIGHEST
CLIP_NORM = 1.0
MOMENT_DECAY = 0.5
CORRECTION = 0.9375
ADAM_EPSILON = 1e-08
WEIGHT_DECAY = 0.05
LAYER_EPSILON = 1e-06
VECTOR_RATE = 0.2


def layer_norm(stream, gain, bias):
    center = jnp.mean(stream, axis=-1, keepdims=True)
    spread = stream - center
    second = jnp.mean(spread * spread, axis=-1, keepdims=True)
    return spread * lax.rsqrt(second + LAYER_EPSILON) * gain + bias


def exact_gelu(stream):
    return jax.nn.gelu(stream, approximate=False)


def row_mask(mask_patches, seq_length):
    row_ids = jnp.arange(seq_length, dtype=jnp.int32)
    hits = mask_patches[:, :, None] + 1 == row_ids[None, None, :]
    return jnp.any(hits, axis=1).astype(jnp.float32)


def positions(owners, slot_count):
    block_ids = jnp.arange(owners.shape[0], dtype=jnp.int32)
    same_owner = owners[None, :] == owners[:, None]
    earlier = block_ids[None, :] < block_ids[:, None]
    ranking = jnp.sum((same_owner & earlier).astype(jnp.int32), axis=1)
    return owners * slot_count + ranking


def to_blocks(w_project, w_output, w_upward, w_downward):
    layer_count = w_project.shape[0]
    model_width = w_project.shape[1]
    block_size = w_project.shape[3]
    piece_count = model_width // block_size
    mlp_ratio = w_upward.shape[2]
    first_part = (
        w_project.reshape(layer_count, piece_count, block_size, 3, block_size)
        .transpose(0, 1, 3, 2, 4)
        .reshape(layer_count, piece_count * 3, block_size, block_size)
    )
    second_part = w_output.reshape(layer_count, block_size, piece_count, block_size).transpose(
        0, 2, 1, 3
    )
    third_part = (
        w_upward.reshape(layer_count, piece_count, block_size, mlp_ratio, block_size)
        .transpose(0, 1, 3, 2, 4)
        .reshape(layer_count, piece_count * mlp_ratio, block_size, block_size)
    )
    fourth_part = (
        w_downward.reshape(layer_count, mlp_ratio, block_size, piece_count, block_size)
        .transpose(0, 1, 3, 2, 4)
        .reshape(layer_count, mlp_ratio * piece_count, block_size, block_size)
    )
    joined = jnp.concatenate([first_part, second_part, third_part, fourth_part], axis=1)
    return joined.reshape(-1, block_size, block_size)


def from_blocks(blocks, layer_count, piece_count, mlp_ratio):
    block_size = blocks.shape[-1]
    per_layer = piece_count * (4 + 2 * mlp_ratio)
    grouped = blocks.reshape(layer_count, per_layer, block_size, block_size)
    start_out = 3 * piece_count
    start_up = 4 * piece_count
    start_down = start_up + piece_count * mlp_ratio
    w_project = (
        grouped[:, :start_out]
        .reshape(layer_count, piece_count, 3, block_size, block_size)
        .transpose(0, 1, 3, 2, 4)
        .reshape(layer_count, piece_count * block_size, 3, block_size)
    )
    w_output = (
        grouped[:, start_out:start_up]
        .transpose(0, 2, 1, 3)
        .reshape(layer_count, block_size, piece_count * block_size)
    )
    w_upward = (
        grouped[:, start_up:start_down]
        .reshape(layer_count, piece_count, mlp_ratio, block_size, block_size)
        .transpose(0, 1, 3, 2, 4)
        .reshape(layer_count, piece_count * block_size, mlp_ratio, block_size)
    )
    w_downward = (
        grouped[:, start_down:]
        .reshape(layer_count, mlp_ratio, piece_count, block_size, block_size)
        .transpose(0, 1, 3, 2, 4)
        .reshape(layer_count, mlp_ratio, block_size, piece_count * block_size)
    )
    return (w_project, w_output, w_upward, w_downward)


def rotated_update(gradient, weight, first_state, second_state, left_basis, right_basis, step_rate):
    half_turn = jnp.einsum("nki,nkl->nil", left_basis, gradient, precision=HIGHEST)
    turned = jnp.einsum("nil,nlj->nij", half_turn, right_basis, precision=HIGHEST)
    first_new = MOMENT_DECAY * first_state + (1.0 - MOMENT_DECAY) * turned
    second_new = MOMENT_DECAY * second_state + (1.0 - MOMENT_DECAY) * turned * turned
    stepped = first_new / CORRECTION / (jnp.sqrt(second_new / CORRECTION) + ADAM_EPSILON)
    half_back = jnp.einsum("nik,nkl->nil", left_basis, stepped, precision=HIGHEST)
    rotated_back = jnp.einsum("nil,njl->nij", half_back, right_basis, precision=HIGHEST)
    return (weight - step_rate * (rotated_back + WEIGHT_DECAY * weight), first_new, second_new)


def plain_update(gradient, weight, first_state, second_state, step_rate):
    first_new = MOMENT_DECAY * first_state + (1.0 - MOMENT_DECAY) * gradient
    second_new = MOMENT_DECAY * second_state + (1.0 - MOMENT_DECAY) * gradient * gradient
    stepped = first_new / CORRECTION / (jnp.sqrt(second_new / CORRECTION) + ADAM_EPSILON)
    return (weight - step_rate * stepped, first_new, second_new)


def shards(
    block_input,
    cotangent,
    mask_patches,
    owners,
    master_slots,
    left_bases,
    right_bases,
    first_moment,
    second_moment,
    shared_vectors,
    shared_first,
    shared_second,
    split_vectors,
    split_first,
    split_second,
):
    slot_count = master_slots.shape[0]
    block_size = master_slots.shape[-1]
    layer_count = shared_vectors.shape[0]
    model_width = shared_vectors.shape[2]
    mlp_ratio = split_vectors.shape[1] - 2
    piece_count = model_width // block_size
    block_total = owners.shape[0]
    per_layer = block_total // layer_count
    head_count = block_size // DH
    scale = 1.0 / math.sqrt(DH)
    image_count = block_input.shape[0]
    seq_length = block_input.shape[1]
    dp_count = lax.axis_size("dp")
    slot_total = dp_count * slot_count
    slot_index = positions(owners, slot_count)
    copies = lax.all_gather(master_slots[:, 0].astype(jnp.bfloat16), "dp", axis=0, tiled=True)
    w_project, w_output, w_upward, w_downward = from_blocks(
        copies[slot_index], layer_count, piece_count, mlp_ratio
    )

    def feed_back(grad_stream, middle, normed_two, hidden, active, mixed, layer_index):
        gain_two = shared_vectors[layer_index, 3]
        bias_two = shared_vectors[layer_index, 4]
        grad_low = grad_stream.astype(jnp.bfloat16)
        grad_down = jnp.einsum(
            "gsje,gsd->jed", active, grad_low, preferred_element_type=jnp.float32
        )
        grad_active = jnp.einsum(
            "gsd,jed->gsje", grad_low, w_downward[layer_index], preferred_element_type=jnp.float32
        )
        _, gelu_back = jax.vjp(exact_gelu, hidden)
        grad_hidden = gelu_back(grad_active)[0].astype(jnp.bfloat16)
        grad_up_bias = jnp.sum(grad_hidden.astype(jnp.float32), axis=(0, 1))
        grad_up = jnp.einsum(
            "gsd,gsje->dje", normed_two, grad_hidden, preferred_element_type=jnp.float32
        )
        partial_grad = jnp.einsum(
            "gsje,dje->gsd", grad_hidden, w_upward[layer_index], preferred_element_type=jnp.float32
        )
        grad_normed_two = lax.psum(partial_grad.astype(jnp.bfloat16), "tp").astype(jnp.float32)
        _, second_back = jax.vjp(layer_norm, middle, gain_two, bias_two)
        grad_mid_norm, grad_gain_two, grad_bias_two = second_back(grad_normed_two)
        grad_middle = grad_stream + grad_mid_norm
        grad_down_bias = jnp.sum(grad_stream, axis=(0, 1))
        grad_out_bias = jnp.sum(grad_middle, axis=(0, 1))
        grad_branch = grad_middle.astype(jnp.bfloat16)
        grad_out = jnp.einsum("gse,gsd->ed", mixed, grad_branch, preferred_element_type=jnp.float32)
        grad_mixed = jnp.einsum(
            "gsd,ed->gse", grad_branch, w_output[layer_index], preferred_element_type=jnp.float32
        ).astype(jnp.bfloat16)
        return (
            grad_middle,
            grad_mixed,
            grad_down,
            grad_up,
            grad_up_bias,
            grad_gain_two,
            grad_bias_two,
            grad_down_bias,
            grad_out_bias,
            grad_out,
        )

    def backward_layer(grad_stream, kept, layer_index):
        (
            stream,
            normed,
            query,
            keyset,
            valueset,
            log_total,
            mixed,
            middle,
            normed_two,
            hidden,
            active,
        ) = kept
        gain_one = shared_vectors[layer_index, 0]
        bias_one = shared_vectors[layer_index, 1]
        pieces = feed_back(grad_stream, middle, normed_two, hidden, active, mixed, layer_index)
        grad_middle, grad_mixed = (pieces[0], pieces[1])
        (
            grad_down,
            grad_up,
            grad_up_bias,
            grad_gain_two,
            grad_bias_two,
            grad_down_bias,
            grad_out_bias,
            grad_out,
        ) = pieces[2:]
        grad_mixed = grad_mixed.reshape(image_count, seq_length, head_count, DH)
        scores = jnp.einsum("gqhe,gkhe->ghqk", query, keyset, preferred_element_type=jnp.float32)
        weights = jnp.exp(scores - log_total)
        grad_values = jnp.einsum(
            "ghqk,gqhe->gkhe",
            weights.astype(jnp.bfloat16),
            grad_mixed,
            preferred_element_type=jnp.float32,
        ).astype(jnp.bfloat16)
        grad_weights = jnp.einsum(
            "gqhe,gkhe->ghqk", grad_mixed, valueset, preferred_element_type=jnp.float32
        )
        grad_scores = (
            weights * (grad_weights - jnp.sum(weights * grad_weights, axis=-1, keepdims=True))
        ).astype(jnp.bfloat16)
        grad_query = jnp.einsum(
            "ghqk,gkhe->gqhe", grad_scores, keyset, preferred_element_type=jnp.float32
        ).astype(jnp.bfloat16)
        grad_keys = jnp.einsum(
            "ghqk,gqhe->gkhe", grad_scores, query, preferred_element_type=jnp.float32
        ).astype(jnp.bfloat16)
        grad_query_in = (grad_query.astype(jnp.float32) * scale).astype(jnp.bfloat16)
        stacked = jnp.stack([grad_query_in, grad_keys, grad_values], axis=2).reshape(
            image_count, seq_length, 3, block_size
        )
        grad_query_bias = jnp.sum(grad_query_in.astype(jnp.float32), axis=(0, 1)).reshape(
            block_size
        )
        grad_value_bias = jnp.sum(grad_values.astype(jnp.float32), axis=(0, 1)).reshape(block_size)
        grad_project = jnp.einsum(
            "gsd,gsje->dje", normed, stacked, preferred_element_type=jnp.float32
        )
        grad_normed = lax.psum(
            jnp.einsum(
                "gsje,dje->gsd", stacked, w_project[layer_index], preferred_element_type=jnp.float32
            ).astype(jnp.bfloat16),
            "tp",
        ).astype(jnp.float32)
        _, first_back = jax.vjp(layer_norm, stream, gain_one, bias_one)
        grad_first_norm, grad_gain_one, grad_bias_one = first_back(grad_normed)
        grad_input = grad_middle + grad_first_norm
        shared_grad = jnp.stack(
            [
                grad_gain_one,
                grad_bias_one,
                grad_out_bias,
                grad_gain_two,
                grad_bias_two,
                grad_down_bias,
            ]
        )
        split_grad = jnp.concatenate(
            [grad_query_bias[None], grad_value_bias[None], grad_up_bias], axis=0
        )
        return (grad_input, (grad_project, grad_out, grad_up, grad_down), shared_grad, split_grad)

    stream = block_input.astype(jnp.float32)
    kept_layers = []
    for layer_index in range(layer_count):
        (
            forward_gain_one,
            forward_bias_one,
            out_bias,
            forward_gain_two,
            forward_bias_two,
            down_bias,
        ) = [shared_vectors[layer_index, entry] for entry in range(6)]
        query_bias = split_vectors[layer_index, 0]
        value_bias = split_vectors[layer_index, 1]
        up_bias = split_vectors[layer_index, 2:]
        forward_normed = layer_norm(stream, forward_gain_one, forward_bias_one).astype(jnp.bfloat16)
        project = jnp.einsum(
            "gsd,dje->gsje",
            forward_normed,
            w_project[layer_index],
            preferred_element_type=jnp.float32,
        )
        forward_query = (
            ((project[:, :, 0] + query_bias) * scale)
            .astype(jnp.bfloat16)
            .reshape(image_count, seq_length, head_count, DH)
        )
        forward_keyset = (
            project[:, :, 1].astype(jnp.bfloat16).reshape(image_count, seq_length, head_count, DH)
        )
        forward_valueset = (
            (project[:, :, 2] + value_bias)
            .astype(jnp.bfloat16)
            .reshape(image_count, seq_length, head_count, DH)
        )
        forward_scores = jnp.einsum(
            "gqhe,gkhe->ghqk", forward_query, forward_keyset, preferred_element_type=jnp.float32
        )
        highest = jnp.max(forward_scores, axis=-1, keepdims=True)
        powered = jnp.exp(forward_scores - highest)
        total_mass = jnp.sum(powered, axis=-1, keepdims=True)
        forward_weights = (powered / total_mass).astype(jnp.bfloat16)
        forward_mixed = jnp.einsum(
            "ghqk,gkhe->gqhe", forward_weights, forward_valueset, preferred_element_type=jnp.float32
        )
        forward_mixed = forward_mixed.astype(jnp.bfloat16).reshape(
            image_count, seq_length, block_size
        )
        branch = lax.psum(
            jnp.einsum(
                "gse,ed->gsd",
                forward_mixed,
                w_output[layer_index],
                preferred_element_type=jnp.float32,
            ).astype(jnp.bfloat16),
            "tp",
        ).astype(jnp.float32)
        forward_middle = stream + branch + out_bias
        forward_normed_two = layer_norm(forward_middle, forward_gain_two, forward_bias_two).astype(
            jnp.bfloat16
        )
        forward_hidden = (
            jnp.einsum(
                "gsd,dje->gsje",
                forward_normed_two,
                w_upward[layer_index],
                preferred_element_type=jnp.float32,
            )
            + up_bias
        )
        forward_active = exact_gelu(forward_hidden).astype(jnp.bfloat16)
        branch_two = lax.psum(
            jnp.einsum(
                "gsje,jed->gsd",
                forward_active,
                w_downward[layer_index],
                preferred_element_type=jnp.float32,
            ).astype(jnp.bfloat16),
            "tp",
        ).astype(jnp.float32)
        result = forward_middle + branch_two + down_bias
        forward_log_total = highest + jnp.log(total_mass)
        stream, kept = (
            result,
            (
                stream,
                forward_normed,
                forward_query,
                forward_keyset,
                forward_valueset,
                forward_log_total,
                forward_mixed,
                forward_middle,
                forward_normed_two,
                forward_hidden,
                forward_active,
            ),
        )
        kept_layers.append(kept)
    grad_stream = cotangent * row_mask(mask_patches, seq_length)[:, :, None]
    layer_blocks = [None] * layer_count
    shared_grads = [None] * layer_count
    split_grads = [None] * layer_count
    for layer_index in reversed(range(layer_count)):
        grad_stream, matrices, shared_grad, split_grad = backward_layer(
            grad_stream, kept_layers[layer_index], layer_index
        )
        layer_blocks[layer_index] = to_blocks(*[member[None] for member in matrices])
        shared_grads[layer_index] = shared_grad
        split_grads[layer_index] = split_grad
    placed = (
        jnp.zeros((slot_total, block_size, block_size), jnp.float32)
        .at[slot_index]
        .set(jnp.concatenate(layer_blocks, axis=0))
    )
    reduced = lax.psum_scatter(placed, "dp", scatter_dimension=0, tiled=True)
    shared_sum, split_sum = lax.psum((jnp.stack(shared_grads), jnp.stack(split_grads)), "dp")
    my_rank = lax.axis_index("dp")
    tp_rank = lax.axis_index("tp")
    mine_ids = my_rank * slot_count + jnp.arange(slot_count, dtype=jnp.int32)
    matches = slot_index[None, :] == mine_ids[:, None]
    live = jnp.any(matches, axis=1)
    block_layer = jnp.arange(block_total, dtype=jnp.int32) // per_layer
    owned_layer = jnp.sum(jnp.where(matches, block_layer[None, :], 0), axis=1)
    block_squares = jnp.where(live, jnp.sum(reduced * reduced, axis=(1, 2)), 0.0)
    layer_pick = (owned_layer[:, None] == jnp.arange(layer_count, dtype=jnp.int32)[None, :]) & live[
        :, None
    ]
    matrix_squares = jnp.sum(jnp.where(layer_pick, block_squares[:, None], 0.0), axis=0)
    shared_squares = jnp.sum(shared_sum * shared_sum, axis=(1, 2))
    split_squares = jnp.sum(split_sum * split_sum, axis=(1, 2))
    vector_part = jnp.where(
        my_rank == 0, split_squares + jnp.where(tp_rank == 0, shared_squares, 0.0), 0.0
    )
    squares = lax.psum(matrix_squares + vector_part, ("dp", "tp"))
    layer_norms = jnp.sqrt(squares)
    global_norm = jnp.sqrt(jnp.sum(squares))
    factor = CLIP_NORM / jnp.maximum(global_norm, CLIP_NORM)
    step_rate = 0.5 / math.sqrt(model_width)
    weight, first_state, second_state = rotated_update(
        reduced * factor,
        master_slots[:, 0],
        first_moment[:, 0],
        second_moment[:, 0],
        left_bases[:, 0],
        right_bases[:, 0],
        step_rate,
    )
    keep_live = live[:, None, None]
    new_master = jnp.where(keep_live, weight, master_slots[:, 0])[:, None]
    new_first = jnp.where(keep_live, first_state, first_moment[:, 0])[:, None]
    new_second = jnp.where(keep_live, second_state, second_moment[:, 0])[:, None]
    new_shared, new_shared_first, new_shared_second = plain_update(
        shared_sum * factor, shared_vectors, shared_first, shared_second, VECTOR_RATE
    )
    new_split, new_split_first, new_split_second = plain_update(
        split_sum * factor, split_vectors, split_first, split_second, VECTOR_RATE
    )
    return (
        stream,
        grad_stream,
        new_master,
        new_first,
        new_second,
        new_shared,
        new_shared_first,
        new_shared_second,
        new_split,
        new_split_first,
        new_split_second,
        layer_norms,
        global_norm,
    )


def solution(mesh):
    return jax.shard_map(
        shards,
        mesh=mesh,
        in_specs=(
            P("dp", None, None),
            P("dp", None, None),
            P("dp", None),
            P(),
            P("dp", "tp", None, None),
            P("dp", "tp", None, None),
            P("dp", "tp", None, None),
            P("dp", "tp", None, None),
            P("dp", "tp", None, None),
            P(),
            P(),
            P(),
            P(None, None, "tp"),
            P(None, None, "tp"),
            P(None, None, "tp"),
        ),
        out_specs=(
            P("dp", None, None),
            P("dp", None, None),
            P("dp", "tp", None, None),
            P("dp", "tp", None, None),
            P("dp", "tp", None, None),
            P(),
            P(),
            P(),
            P(None, None, "tp"),
            P(None, None, "tp"),
            P(None, None, "tp"),
            P(),
            P(),
        ),
        check_vma=False,
    )
```

profile of v0, /device:TPU:0, one launch (start us, length us, event | category | flops | bytes accessed | tf_op | source)
XLA Modules:
  0.0 1408.3 jit_solution(2315307643869400102)
XLA Ops:
  20.7 160.3 %all-gather.2.cloned.1.call-done = bf16[48,384,384]{2,1,0:T(8,128)(2,1)} async-done(((bf16[3,384,384]{2,1,0:T(8,128)(2,1)}), bf16[48,384,384]{2,1,0:T(8,128)(2,1)}) %all-gather.2.cloned.1.call-update) | async-done | bytes 14155792 | tf_op jit(solution)/shard_map/all_gather | solution.py:157
  181.0 12.4 gather_fusion
  234.5 7.4 fusion.180
  247.8 6.7 reshape.378
  266.6 7.8 fusion.77
  274.5 23.9 %multiply_convert_fusion.3 = (bf16[8,197,4,384]{3,1,2,0:T(8,128)(2,1)S(1)}, f32[8,197,4,384]{3,1,2,0:T(8,128)}) fusion(f32[8,197,4,384]{3,1,2,0:T(8,128)S(1)} %get-tuple-element.168, f32[4,384]{1,0:T(4,128)S(1)} %bitcast.391, u8[197,4,384]{2,0,1:T(8,128)(4,1)S(1)} %get-tuple-element.81, u8[197,4,384]{2,0,1:T(8,128)(4,1)S(1)} %get-tuple-element.80), kind=kLoop, calls=%fused_computation.43 | loop fusion | flops 171872256 | bytes 24818688 | tf_op jit(solution)/shard_map/convert_element_type | solution.py:358
  300.6 5.2 bitcast_convert_fusion.5
  314.2 12.1 all-reduce.12.cloned.1.call-done
  372.2 6.6 reshape.385
  378.8 8.7 all-reduce.14.cloned.1.call-done
  395.1 7.2 fusion.78
  402.3 23.7 %multiply_convert_fusion.2 = (bf16[8,197,4,384]{3,1,2,0:T(8,128)(2,1)}, f32[8,197,4,384]{3,1,2,0:T(8,128)}) fusion(f32[8,197,4,384]{3,1,2,0:T(8,128)S(1)} %get-tuple-element.171, f32[4,384]{1,0:T(4,128)S(1)} %bitcast.394, u8[197,4,384]{2,0,1:T(8,128)(4,1)S(1)} %get-tuple-element.79, u8[197,4,384]{2,0,1:T(8,128)(4,1)S(1)} %get-tuple-element.78), kind=kLoop, calls=%fused_computation.28 | loop fusion | flops 171872256 | bytes 24818688 | tf_op jit(solution)/shard_map/convert_element_type | solution.py:358
  426.1 14.3 %convert_reduce_fusion = (f32[4,384]{1,0:T(4,128)}, bf16[8,197,4,384]{3,1,2,0:T(8,128)(2,1)}) fusion(f32[8,197,4,384]{3,1,2,0:T(8,128)} %get-tuple-element.131, bf16[4,384,768,1]{2,1,0,3:T(8,128)(2,1)S(1)} %copy-done.48, f32[8,197,768]{2,0,1:T(8,128)S(1)} %bitcast.369, f32[8,197]{1,0:T(8,128)S(1)} %convert_element_type.261, ...), kind=kOutput, calls=%fused_computation.18 | convolution fusion | flops 3761822208 | bytes 31426720 | tf_op jit(solution)/shard_map/gsd,jed->gsje/dot_general | solution.py:169
  440.4 8.7 bitcast_convert_fusion.3
  449.2 23.1 %all-reduce.16.cloned.1.call-done = bf16[8,197,768]{2,1,0:T(8,128)(2,1)} async-done(((bf16[8,197,768]{2,1,0:T(8,128)(2,1)}), bf16[8,197,768]{2,1,0:T(8,128)(2,1)}) %all-reduce.16.cloned.1.call-update) | async-done | bytes 2420752 | tf_op jit(solution)/shard_map/psum | solution.py:181
  472.3 5.7 convert_reduce_fusion.5
  478.8 5.3 fusion.36
  484.1 6.6 fusion.175
  498.1 8.0 convert_reduce_fusion.7
  506.1 7.4 multiply_reduce_fusion.1
  513.5 11.1 multiply_convert_fusion.1
  524.6 6.3 convolution_convert_fusion.4
  540.7 7.6 bitcast_convert_fusion.2
  550.0 21.6 %all-reduce.18.cloned.1.call-done = bf16[8,197,768]{2,1,0:T(8,128)(2,1)} async-done(((bf16[8,197,768]{2,1,0:T(8,128)(2,1)}), bf16[8,197,768]{2,1,0:T(8,128)(2,1)}) %all-reduce.18.cloned.1.call-update) | async-done | bytes 2420752 | tf_op jit(solution)/shard_map/psum | solution.py:265
  571.6 5.7 convert_reduce_fusion.4
  577.3 5.1 fusion.37
  582.5 9.2 fusion.173
  591.7 14.7 %convert_reduce_fusion.1 = (f32[4,384]{1,0:T(4,128)}, bf16[8,197,4,384]{3,1,2,0:T(8,128)(2,1)}) fusion(f32[8,197,4,384]{3,1,2,0:T(8,128)} %get-tuple-element.137, bf16[4,384,768,1]{2,1,0,3:T(8,128)(2,1)S(1)} %copy-done.45, f32[8,197,768]{2,1,0:T(8,128)S(1)} %get-tuple-element.125, f32[8,197,4,384]{3,1,2,0:T(8,128)} %copy-done.29, f32[4,384]{1,0:T(4,128)S(1)} %bitcast.392), kind=kOutput, calls=%fused_computation.19 | convolution fusion | flops 3760611840 | bytes 31420416 | tf_op jit(solution)/shard_map/gsd,jed->gsje/dot_general | solution.py:169
  606.5 8.0 bitcast_convert_fusion.1
  616.5 8.1 fusion.160
  629.5 5.3 bitcast_convert_fusion.4
  637.7 6.1 convert_reduce_fusion.3
  648.3 5.3 fusion.174
  660.2 7.5 convert_reduce_fusion.9
  667.7 7.5 multiply_reduce_fusion
  675.1 11.1 multiply_convert_fusion
  686.3 6.3 convolution_convert_fusion.2
  700.3 7.6 bitcast_convert_fusion
  708.6 11.7 convolution_bitcast_fusion
  720.3 6.8 reshape_broadcast_in_dim.19
  727.1 5.3 copy.344
  732.4 9.8 fusion.79
  742.2 7.1 reshape_broadcast_in_dim.17
  749.3 5.0 copy.335
  754.3 8.0 fusion.164
  764.9 5.5 reshape.413
  770.4 5.6 reshape.414
  780.2 5.7 fusion.52
  785.9 4.6 convert_reduce_fusion.2
  794.1 8.9 convert_bitcast_fusion
  803.0 5.5 reshape.412
  808.6 5.8 reshape.411
  814.4 8.0 fusion.54
  825.0 17.0 %maximum_bitcast_fusion = (f32[24,384,384]{2,1,0:T(8,128)}, f32[24,384,384]{2,1,0:T(8,128)}) fusion(f32[1,8,384,384]{3,2,1,0:T(8,128)} %bitcast.347, f32[1,8,384,384]{3,2,1,0:T(8,128)} %bitcast.348, f32[1,2,384,384]{3,2,1,0:T(8,128)} %fusion.115, f32[1,6,384,384]{3,2,1,0:T(8,128)} %bitcast.373, f32[1,8,384,384]{3,2,1,0:T(8,128)} %bitcast.346, ...), kind=kLoop, calls=%fused_computation.5 | loop fusion | flops 21233664 | bytes 56623104 | tf_op jit(solution)/shard_map/reshape | solution.py:71
  842.0 20.8 %pad_maximum_fusion = f32[48,384,384]{2,1,0:T(8,128)} fusion(f32[24,384,384]{2,1,0:T(8,128)} %get-tuple-element.189, f32[24,384,384]{2,1,0:T(8,128)} %get-tuple-element.188), kind=kLoop, calls=%fused_computation.2 | loop fusion | flops 7077888 | bytes 56623104 | tf_op jit(solution)/shard_map/concatenate | solution.py:401
  862.8 12.8 broadcast_in_dim.134
  875.6 48.0 %scatter_fusion = f32[48,384,384]{2,1,0:T(8,128)} fusion(f32[48,384,384]{2,1,0:T(8,128)} %broadcast_in_dim.134, s32[48]{0:T(128)S(1)} %copy-done.150, f32[48,384,384]{2,1,0:T(8,128)} %pad_maximum_fusion), kind=kCustom, calls=%fused_computation.1 | custom fusion | bytes 84934848 | tf_op jit(solution)/shard_map/scatter | solution.py:401
  932.6 84.2 %all-reduce = (f32[2,6,384]{2,1,0:T(8,128)S(1)}, f32[2,6,768]{2,1,0:T(8,128)S(1)}) all-reduce(f32[2,6,384]{2,1,0:T(8,128)S(1)} %pad_maximum_fusion.4, f32[2,6,768]{2,1,0:T(8,128)S(1)} %pad_maximum_fusion.3), channel_id=1, replica_groups=mesh['dp'=16,'tp'=2] {'dp'}, use_global_device_ids=true, to_apply=%region_44.0 | all-reduce | flops 13824 | bytes 110592 | tf_op jit(solution)/shard_map/psum | solution.py:404
  1017.0 309.0 %reduce-scatter.2.cloned.1.call-done = f32[3,384,384]{2,1,0:T(8,128)} async-done(((f32[48,384,384]{2,1,0:T(8,128)}), f32[3,384,384]{2,1,0:T(8,128)}) %reduce-scatter.2.cloned.1.call-update) | async-done | bytes 1769488 | tf_op jit(solution)/shard_map/reduce_scatter | solution.py:403
  1327.9 6.2 copy.356
  1334.1 39.5 %psum.87 = f32[2]{0:T(128)S(1)} all-reduce(f32[2]{0:T(128)S(1)} %fusion.151), channel_id=1, replica_groups=mesh['dp'=16,'tp'=2] {'dp','tp'}, use_global_device_ids=true, to_apply=%region_60.0 | all-reduce | flops 2 | bytes 16 | tf_op jit(solution)/shard_map/psum | solution.py:422
  1375.4 5.3 fusion.94
  1384.3 4.8 fusion.92
  1395.5 4.9 fusion.86
  (496 shorter events, 219.1 us)
Async XLA Ops:
  7.2 1368.2 %copy-start = (f32[3,1,384,384]{3,2,1,0:T(8,128)S(1)}, f32[3,1,384,384]{3,2,1,0:T(8,128)}, u32[]{:S(2)}) copy-start(f32[3,1,384,384]{3,2,1,0:T(8,128)} %param.20) | copy-start | bytes 5308420
  7.2 173.8 %all-gather.2.cloned.1.call-start = ((), (), s32[]{:S(2)}) async-start(), calls=%async_computation.1 | async-start | bytes 15040512 | tf_op jit(solution)/shard_map/all_gather | solution.py:157
  9.9 250.6 %all-reduce.10.cloned.1.call-start = ((), (), s32[]{:S(2)}) async-start(), calls=%async_computation.2 | async-start | bytes 4915200 | tf_op jit(solution)/shard_map/psum | solution.py:336
  11.4 208.1 %copy-start.110 = (f32[6,64]{1,0:T(8,128)}, f32[6,64]{1,0:T(8,128)S(1)}, u32[]{:S(2)}) copy-start(f32[6,64]{1,0:T(8,128)S(1)} %add.335) | copy-start | bytes 4612
  11.4 213.5 %copy-start.132 = (f32[6,64]{1,0:T(8,128)}, f32[6,64]{1,0:T(8,128)S(1)}, u32[]{:S(2)}) copy-start(f32[6,64]{1,0:T(8,128)S(1)} %add.332) | copy-start | bytes 4612
  15.6 183.3 %copy-start.106 = (f32[768]{0:T(1024)}, f32[768]{0:T(1024)S(1)}, u32[]{:S(2)}) copy-start(f32[768]{0:T(1024)S(1)} %get-tuple-element.109) | copy-start | bytes 9220
  15.6 183.4 %copy-start.143 = (f32[768]{0:T(1024)}, f32[768]{0:T(1024)S(1)}, u32[]{:S(2)}) copy-start(f32[768]{0:T(1024)S(1)} %get-tuple-element.108) | copy-start | bytes 9220
  15.6 251.0 %copy-start.102 = (f32[768]{0:T(1024)}, f32[768]{0:T(1024)S(1)}, u32[]{:S(2)}) copy-start(f32[768]{0:T(1024)S(1)} %get-tuple-element.106) | copy-start | bytes 9220
  15.6 251.0 %copy-start.152 = (f32[768]{0:T(1024)}, f32[768]{0:T(1024)S(1)}, u32[]{:S(2)}) copy-start(f32[768]{0:T(1024)S(1)} %get-tuple-element.105) | copy-start | bytes 9220
  15.6 310.7 %copy-start.75 = (f32[768]{0:T(1024)}, f32[768]{0:T(1024)S(1)}, u32[]{:S(2)}) copy-start(f32[768]{0:T(1024)S(1)} %get-tuple-element.107) | copy-start | bytes 9220
  15.6 316.6 %copy-start.104 = (f32[768]{0:T(1024)}, f32[768]{0:T(1024)S(1)}, u32[]{:S(2)}) copy-start(f32[768]{0:T(1024)S(1)} %get-tuple-element.103) | copy-start | bytes 9220
  18.0 180.9 %copy-start.71 = (f32[8,197]{1,0:T(8,128)}, f32[8,197]{1,0:T(8,128)S(1)}, u32[]{:S(2)}) copy-start(f32[8,197]{1,0:T(8,128)S(1)} %broadcast_multiply_fusion.3) | copy-start | bytes 18916
  20.7 172.7 %copy-start.84 = (f32[8,197]{1,0:T(8,128)}, f32[8,197]{1,0:T(8,128)S(1)}, u32[]{:S(2)}) copy-start(f32[8,197]{1,0:T(8,128)S(1)} %fusion.33) | copy-start | bytes 18916
  20.7 178.2 %copy-start.82 = (f32[8,197]{1,0:T(8,128)}, f32[8,197]{1,0:T(8,128)S(1)}, u32[]{:S(2)}) copy-start(f32[8,197]{1,0:T(8,128)S(1)} %fusion.145) | copy-start | bytes 18916
  233.9 92.4 %all-reduce.12.cloned.1.call-start = ((), (), s32[]{:S(2)}) async-start(), calls=%async_computation.3 | async-start | bytes 4915200 | tf_op jit(solution)/shard_map/psum | solution.py:359
  234.5 39.9 %copy-start.117 = (f32[1,4,384]{2,1,0:T(4,128)}, f32[1,4,384]{2,1,0:T(4,128)S(1)}, u32[]{:S(2)}) copy-start(f32[1,4,384]{2,1,0:T(4,128)S(1)} %copy.499) | copy-start | bytes 18436
  264.4 10.1 copy-start.73
  266.0 8.4 copy-start.93
  274.4 23.9 %copy-start.29 = (f32[8,197,4,384]{3,1,2,0:T(8,128)}, f32[8,197,4,384]{3,1,2,0:T(8,128)S(1)}, u32[]{:S(2)}) copy-start(f32[8,197,4,384]{3,1,2,0:T(8,128)S(1)} %get-tuple-element.168) | copy-start | bytes 29048836
  274.5 26.1 %copy-start.44 = (bf16[4,384,768,1]{2,1,0,3:T(8,128)(2,1)S(1)}, bf16[4,384,768,1]{2,1,0,3:T(8,128)(2,1)}, u32[]{:S(2)}) copy-start(bf16[4,384,768,1]{2,1,0,3:T(8,128)(2,1)} %reshape.378) | copy-start | bytes 7077892
  305.8 20.4 %copy-start.123 = (f32[768]{0:T(1024)S(1)}, f32[768]{0:T(1024)}, u32[]{:S(2)}) copy-start(f32[768]{0:T(1024)} %get-tuple-element.104) | copy-start | bytes 9220
  305.9 81.7 %all-reduce.14.cloned.1.call-start = ((), (), s32[]{:S(2)}) async-start(), calls=%async_computation.4 | async-start | bytes 4915200 | tf_op jit(solution)/shard_map/psum | solution.py:336
  307.3 42.8 %copy-start.112 = (f32[6,64]{1,0:T(8,128)}, f32[6,64]{1,0:T(8,128)S(1)}, u32[]{:S(2)}) copy-start(f32[6,64]{1,0:T(8,128)S(1)} %add.360) | copy-start | bytes 4612
  364.4 107.9 %all-reduce.16.cloned.1.call-start = ((), (), s32[]{:S(2)}) async-start(), calls=%async_computation.5 | async-start | bytes 4915200 | tf_op jit(solution)/shard_map/psum | solution.py:181
  364.8 61.3 %copy-start.114 = (f32[8,197]{1,0:T(8,128)}, f32[8,197]{1,0:T(8,128)S(1)}, u32[]{:S(2)}) copy-start(f32[8,197]{1,0:T(8,128)S(1)} %convert_element_type.261) | copy-start | bytes 18916
  368.2 19.4 %copy-start.122 = (f32[768]{0:T(1024)S(1)}, f32[768]{0:T(1024)}, u32[]{:S(2)}) copy-start(f32[768]{0:T(1024)} %get-tuple-element.101) | copy-start | bytes 9220
  387.6 38.5 %slice-start.6 = ((s8[4841472]{0:T(1024)(128)(4,1)}), s8[4194304]{0:T(1024)(128)(4,1)S(1)}, s32[]{:S(2)}) async-start(s8[4841472]{0:T(1024)(128)(4,1)} %bitcast.368), calls=%async_computation.16 | async-start | bytes 8388608
  391.6 10.6 copy-start.9
  392.4 9.9 copy-start.90
  392.4 9.9 copy-start.97
  395.1 31.0 %slice-start.7 = ((s8[4841472]{0:T(1024)(128)(4,1)}), s8[647168]{0:T(1024)(128)(4,1)S(1)}, s32[]{:S(2)}) async-start(s8[4841472]{0:T(1024)(128)(4,1)} %bitcast.368), calls=%async_computation.17 | async-start | bytes 1294336
  402.3 23.7 %copy-start.30 = (f32[8,197,4,384]{3,1,2,0:T(8,128)}, f32[8,197,4,384]{3,1,2,0:T(8,128)S(1)}, u32[]{:S(2)}) copy-start(f32[8,197,4,384]{3,1,2,0:T(8,128)S(1)} %get-tuple-element.171) | copy-start | bytes 29048836
  402.3 23.7 %copy-start.48 = (bf16[4,384,768,1]{2,1,0,3:T(8,128)(2,1)S(1)}, bf16[4,384,768,1]{2,1,0,3:T(8,128)(2,1)}, u32[]{:S(2)}) copy-start(bf16[4,384,768,1]{2,1,0,3:T(8,128)(2,1)} %reshape.385) | copy-start | bytes 7077892
  449.1 122.4 %all-reduce.18.cloned.1.call-start = ((), (), s32[]{:S(2)}) async-start(), calls=%async_computation.6 | async-start | bytes 4915200 | tf_op jit(solution)/shard_map/psum | solution.py:265
  484.1 8.9 copy-start.43
  513.5 11.2 copy-start.113
  548.3 23.2 %copy-start.105 = (f32[768]{0:T(1024)S(1)}, f32[768]{0:T(1024)}, u32[]{:S(2)}) copy-start(f32[768]{0:T(1024)} %copy-done.104) | copy-start | bytes 9220
  548.4 28.9 %copy-start.89 = (f32[8,197]{1,0:T(8,128)S(1)}, f32[8,197]{1,0:T(8,128)}, u32[]{:S(2)}) copy-start(f32[8,197]{1,0:T(8,128)} %copy-done.88) | copy-start | bytes 18916
  548.4 28.9 %copy-start.96 = (f32[8,197]{1,0:T(8,128)S(1)}, f32[8,197]{1,0:T(8,128)}, u32[]{:S(2)}) copy-start(f32[8,197]{1,0:T(8,128)} %copy-done.95) | copy-start | bytes 18916
  548.4 89.3 %all-reduce.20.cloned.1.call-start = ((), (), s32[]{:S(2)}) async-start(), calls=%async_computation.7 | async-start | bytes 4915200 | tf_op jit(solution)/shard_map/psum | solution.py:181
  582.5 9.2 copy-start.45
  582.5 9.2 copy-start.118
  591.7 14.8 %copy-start.23 = (f32[8,197,768]{2,1,0:T(8,128)}, f32[8,197,768]{2,1,0:T(8,128)S(1)}, u32[]{:S(2)}) copy-start(f32[8,197,768]{2,1,0:T(8,128)S(1)} %get-tuple-element.125) | copy-start | bytes 14524420
  591.7 14.8 %copy-start.47 = (bf16[1,2,384,4,384]{4,2,1,3,0:T(8,128)(2,1)S(1)}, bf16[1,2,384,4,384]{4,2,1,3,0:T(8,128)(2,1)}, u32[]{:S(2)}) copy-start(bf16[1,2,384,4,384]{4,2,1,3,0:T(8,128)(2,1)} %copy.300) | copy-start | bytes 7077892
  614.5 171.4 %all-reduce.22.cloned.1.call-start = ((), (), s32[]{:S(2)}) async-start(), calls=%async_computation.9 | async-start | bytes 9830400 | tf_op jit(solution)/shard_map/psum | solution.py:359
  629.5 8.1 copy-start.76
  629.5 8.1 copy-start.103
  634.8 8.9 copy-start.87
  634.8 8.9 copy-start.94
  675.1 11.1 copy-start.111
  707.9 618.1 %reduce-scatter.2.cloned.1.call-start = ((), (), s32[]{:S(2)}) async-start(), calls=%async_computation.8 | async-start | bytes 30081024 | tf_op jit(solution)/shard_map/reduce_scatter | solution.py:403
  720.3 12.1 slice-start
  764.9 11.1 copy-start.63
  780.2 10.4 copy-start.85
  785.9 8.1 copy-start.144
  803.0 11.3 copy-start.64
  803.0 21.7 %slice-start.2 = ((s8[4718592]{0:T(1024)(128)(4,1)}), s8[524288]{0:T(1024)(128)(4,1)S(1)}, s32[]{:S(2)}) async-start(s8[4718592]{0:T(1024)(128)(4,1)} %bitcast.343), calls=%async_computation.12 | async-start | bytes 1048576
  814.4 10.4 slice-start.3
  862.8 12.8 copy-start.150
  1016.8 311.1 %copy-start.77 = (f32[2,6,768]{2,1,0:T(8,128)}, f32[2,6,768]{2,1,0:T(8,128)S(1)}, u32[]{:S(2)}) copy-start(f32[2,6,768]{2,1,0:T(8,128)S(1)} %get-tuple-element.115) | copy-start | bytes 110596
  1016.8 311.1 %copy-start.80 = (f32[2,6,384]{2,1,0:T(8,128)}, f32[2,6,384]{2,1,0:T(8,128)S(1)}, u32[]{:S(2)}) copy-start(f32[2,6,384]{2,1,0:T(8,128)S(1)} %get-tuple-element.114) | copy-start | bytes 55300
  1334.1 46.7 %copy-start.34 = (f32[3,1,384,384]{3,2,1,0:T(8,128)S(1)}, f32[3,1,384,384]{3,2,1,0:T(8,128)}, u32[]{:S(2)}) copy-start(f32[3,1,384,384]{3,2,1,0:T(8,128)} %param.21) | copy-start | bytes 5308420
  1375.4 8.9 copy-start.53
  1375.4 8.9 copy-start.54
  (109 other events, 456.4 us)
Sparse Core Ops, SparseCore 0:
  11.4 169.5 all-gather.1
  234.0 20.0 all-reduce.9
  306.0 20.2 all-reduce.11
  364.5 23.0 all-reduce.13
  449.3 23.0 all-reduce.15
  548.5 23.0 all-reduce.17
  614.6 23.0 all-reduce.19
  708.0 30.7 all-reduce.21
  923.9 402.0 reduce-scatter.1
where the time goes:
time: 1420 us; the launch traced here: 1410 us
  waiting for transfers between devices  538 us (38%)
  local copies, waits for them, and re-layouts  270 us (19%)
  matrix products  241 us (17%)
  other arithmetic  218 us (15%)
  blocking collectives  124 us (9%)
  between operations  17.8 us (1%)
    reduce_scatter x1, waiting for transfers between devices, shards(): reduced = lax.psum_scatter(placed, 'dp', scatter_dimension=0, tiled=True)  309 us
    all_gather x1, waiting for transfers between devices, shards(): lax.all_gather(master_slots[:, 0].astype(jnp.bfloat16), 'dp', axis=0, til...  160 us
    psum x1, blocking collectives, shards(): lax.psum((jnp.stack(shared_grads), jnp.stack(split_grads)), 'dp')  84.2 us
    scatter x1, local copies, waits for them, and re-layouts, shards(): placed = jnp.zeros((slot_total, block_size, block_size), jnp.float32).at[...  48 us
    convert_element_type x2, other arithmetic, shards(): forward_active = exact_gelu(forward_hidden).astype(jnp.bfloat16)  47.6 us
    reduce_sum x8, other arithmetic, layer_norm(): return spread * lax.rsqrt(second + LAYER_EPSILON) * gain + bias  40.5 us
    psum x1, blocking collectives, shards(): squares = lax.psum(matrix_squares + vector_part, ('dp', 'tp'))  39.5 us
    unnamed x338, local copies, waits for them, and re-layouts  37.9 us
  transfers between devices with their start and end apart: 9, of which 7 were waited for; matrix products, arithmetic and copies ran while one was open for 12% of the time, Pallas kernels for 0%

commit v1 on v0

v1 whole, which is shorter than its diff:
```python
import functools
import math

import jax
import jax.numpy as jnp
from jax import lax
from jax.experimental import pallas as pl
from jax.experimental.pallas import tpu as pltpu
from jax.sharding import PartitionSpec as P

DH = 64
GROUP = 4
LANES = GROUP * DH
CLIP_NORM = 1.0
MOMENT_DECAY = 0.5
CORRECTION = 0.9375
ADAM_EPSILON = 1e-08
WEIGHT_DECAY = 0.05
LAYER_EPSILON = 1e-06
VECTOR_RATE = 0.2
VMEM_LIMIT = 60 * 1024 * 1024
F32 = jnp.float32
BF16 = jnp.bfloat16


def nn(a, b):
    return lax.dot_general(a, b, (((1,), (0,)), ((), ())), preferred_element_type=F32)


def nt(a, b):
    return lax.dot_general(a, b, (((1,), (1,)), ((), ())), preferred_element_type=F32)


def tn(a, b):
    return lax.dot_general(a, b, (((0,), (0,)), ((), ())), preferred_element_type=F32)


def round_up(number, step):
    return (number + step - 1) // step * step


def positions(owners, slot_count):
    block_ids = jnp.arange(owners.shape[0], dtype=jnp.int32)
    same_owner = owners[None, :] == owners[:, None]
    earlier = block_ids[None, :] < block_ids[:, None]
    ranking = jnp.sum((same_owner & earlier).astype(jnp.int32), axis=1)
    return owners * slot_count + ranking


def normalized(v):
    center = jnp.mean(v, axis=-1, keepdims=True)
    spread = v - center
    second = jnp.mean(spread * spread, axis=-1, keepdims=True)
    inverse = lax.rsqrt(second + LAYER_EPSILON)
    return spread * inverse, inverse


def norm_back(grad, unit, inverse, gain):
    scaled = grad * gain
    first = jnp.mean(scaled, axis=-1, keepdims=True)
    second = jnp.mean(scaled * unit, axis=-1, keepdims=True)
    return inverse * (scaled - first - unit * second)


def gelu_pair(u):
    bell = jnp.exp(u * u * -0.5)
    below = 1.0 + jnp.abs(u) * (0.3275911 * math.sqrt(0.5))
    t = pl.reciprocal(below, approx=True)
    t = t * (2.0 - below * t)
    poly = 0.5 * 1.061405429
    for factor in (-1.453152027, 1.421413741, -0.284496736, 0.254829592):
        poly = poly * t + 0.5 * factor
    tail = poly * t * bell
    mass = jnp.where(u >= 0, 1.0 - tail, tail)
    return u * mass, mass + u * bell * (1.0 / math.sqrt(2.0 * math.pi))


def weight_copies(meta, layer, blocks, wp, wo, wu, wd, sems):
    side = blocks.shape[-1]
    width = wo.shape[0]
    pieces = width // side
    ratio = wd.shape[0] // width
    per_layer = pieces * (4 + 2 * ratio)
    base = layer * per_layer
    jobs = [[], [], [], []]

    def add(kind, target, b, row, col):
        for t in range(blocks.shape[0]):
            r, c = row(t), col(t)
            jobs[kind].append(
                pltpu.make_async_copy(
                    blocks.at[t, meta[base + b]],
                    target.at[pl.ds(r, side), pl.ds(c, side)],
                    sems.at[kind],
                )
            )

    for r in range(pieces):
        for p in range(3):
            add(0, wp, r * 3 + p, lambda t: r * side, lambda t: p * width + t * side)
    for c in range(pieces):
        add(1, wo, 3 * pieces + c, lambda t: t * side, lambda t: c * side)
    for r in range(pieces):
        for j in range(ratio):
            add(
                2, wu, 4 * pieces + r * ratio + j, lambda t: r * side, lambda t: j * width + t * side
            )
    for j in range(ratio):
        for c in range(pieces):
            add(
                3,
                wd,
                (4 + ratio) * pieces + j * pieces + c,
                lambda t: j * width + t * side,
                lambda t: c * side,
            )
    return jobs


def start_weights(jobs, order):
    @pl.when(pl.program_id(0) == 0)
    def _():
        for kind in order:
            for job in jobs[kind]:
                job.start()


def wait_weights(target, sem):
    @pl.when(pl.program_id(0) == 0)
    def _():
        pltpu.make_async_copy(target, target, sem).wait()


def head_masks():
    lane = lax.broadcasted_iota(jnp.int32, (1, LANES), 1)
    return [(lane // DH) == h for h in range(GROUP)]


def spread_heads(masks, value):
    zero = jnp.zeros((), value.dtype)
    return jnp.concatenate([jnp.where(m, value, zero) for m in masks], axis=0)


def forward_kernel(
    layer, seq, rows, keys, meta, x_ref, shared_ref, split_ref, blocks,
    a_ref, q_ref, k_ref, v_ref, p_ref, mixed_ref, h_ref, c_ref, act_ref, slope_ref, y_ref,
    wp, wo, wu, wd, xs, sems,
):
    width = wo.shape[0]
    ratio = wd.shape[0] // width
    groups = width // LANES
    jobs = weight_copies(meta, layer, blocks, wp, wo, wu, wd, sems)
    start_weights(jobs, (0, 1, 2, 3))
    if x_ref.shape[1] == seq:
        tail = seq // 16 * 16
        xs[tail:rows, :] = jnp.zeros((rows - tail, width), F32)
        xs[0:seq, :] = x_ref[0].astype(F32)
        x = xs[...]
    else:
        x = x_ref[0]
    unit, _ = normalized(x)
    a = (unit * shared_ref[0:1, :] + shared_ref[1:2, :]).astype(BF16)
    a_ref[0] = a
    wait_weights(wp, sems.at[0])
    q = ((nn(a, wp[:, 0:width]) + split_ref[0:1, :]) * (1.0 / math.sqrt(DH))).astype(BF16)
    q_ref[0] = q
    k_ref[0, 0:rows, :] = nn(a, wp[:, width : 2 * width]).astype(BF16)
    v_ref[0, 0:rows, :] = (nn(a, wp[:, 2 * width :]) + split_ref[1:2, :]).astype(BF16)
    k_ref[0, rows:keys, :] = jnp.zeros((keys - rows, width), BF16)
    v_ref[0, rows:keys, :] = jnp.zeros((keys - rows, width), BF16)
    masks = head_masks()
    real = lax.broadcasted_iota(jnp.int32, (1, keys), 1) < seq
    for g in range(groups):
        cols = slice(g * LANES, (g + 1) * LANES)
        qs = spread_heads(masks, q[:, cols])
        scores = nt(qs, k_ref[0, :, cols])
        scores = jnp.where(real, scores, -1e30)
        top = jnp.max(scores, axis=-1, keepdims=True)
        power = jnp.exp(scores - top)
        total = jnp.sum(power, axis=-1, keepdims=True)
        probs = (power * (1.0 / total)).astype(BF16)
        p_ref[0, g * GROUP * rows : (g + 1) * GROUP * rows, :] = probs
        v4 = v_ref[0, :, cols]
        mix = None
        for h in range(GROUP):
            part = nn(
                probs[h * rows : (h + 1) * rows, :], jnp.where(masks[h], v4, jnp.zeros((), BF16))
            )
            mix = part if mix is None else mix + part
        mixed_ref[0, :, cols] = mix.astype(BF16)
    wait_weights(wo, sems.at[1])
    h = x + nn(mixed_ref[0], wo[...]) + shared_ref[2:3, :]
    h_ref[0] = h
    unit, _ = normalized(h)
    c = (unit * shared_ref[3:4, :] + shared_ref[4:5, :]).astype(BF16)
    c_ref[0] = c
    wait_weights(wu, sems.at[2])
    wait_weights(wd, sems.at[3])
    y = h + shared_ref[5:6, :]
    for j in range(ratio):
        cols = slice(j * width, (j + 1) * width)
        u = nn(c, wu[:, cols]) + split_ref[2 + j : 3 + j, :]
        act, slope = gelu_pair(u)
        act = act.astype(BF16)
        act_ref[0, :, cols] = act
        slope_ref[0, :, cols] = slope.astype(BF16)
        y = y + nn(act, wd[cols, :])
    y_ref[0] = y[0 : y_ref.shape[1], :]


def backward_kernel(
    layer, seq, rows, keys, last, meta, dy_ref, hits_ref, x_ref, h_ref, slope_ref, p_ref, q_ref,
    k_ref, v_ref, shared_ref, blocks,
    dyr_ref, du_ref, dhr_ref, dqkv_ref, vec_ref, dx_ref,
    wp, wo, wu, wd, xs, sems,
):
    width = wo.shape[0]
    ratio = wd.shape[0] // width
    groups = width // LANES
    jobs = weight_copies(meta, layer, blocks, wp, wo, wu, wd, sems)
    start_weights(jobs, (3, 2, 1, 0))

    @pl.when(pl.program_id(0) == 0)
    def _():
        vec_ref[...] = jnp.zeros_like(vec_ref)

    def collect(row, value):
        vec_ref[row : row + 1, :] += jnp.sum(value, axis=0, keepdims=True)

    tail = seq // 16 * 16
    if last:
        wanted = lax.broadcasted_iota(jnp.int32, (rows, 1), 0)
        hit = jnp.max(jnp.where(hits_ref[0] + 1 == wanted, 1.0, 0.0), axis=-1, keepdims=True)
        xs[tail:rows, :] = jnp.zeros((rows - tail, width), F32)
        xs[0:seq, :] = dy_ref[0]
        dy = xs[...] * hit
    else:
        dy = dy_ref[0]
    collect(5, dy)
    dyr = dy.astype(BF16)
    dyr_ref[0] = dyr
    wait_weights(wd, sems.at[3])
    wait_weights(wu, sems.at[2])
    dc = None
    for j in range(ratio):
        cols = slice(j * width, (j + 1) * width)
        du = (nt(dyr, wd[cols, :]) * slope_ref[0, :, cols].astype(F32)).astype(BF16)
        du_ref[0, :, cols] = du
        collect(8 + j, du.astype(F32))
        part = nt(du, wu[:, cols])
        dc = part if dc is None else dc + part
    unit, inverse = normalized(h_ref[0])
    collect(3, dc * unit)
    collect(4, dc)
    dh = dy + norm_back(dc, unit, inverse, shared_ref[3:4, :])
    collect(2, dh)
    dhr = dh.astype(BF16)
    dhr_ref[0] = dhr
    wait_weights(wo, sems.at[1])
    dmixed = nt(dhr, wo[...]).astype(BF16)
    masks = head_masks()
    zero = jnp.zeros((), BF16)
    for g in range(groups):
        cols = slice(g * LANES, (g + 1) * LANES)
        dm = spread_heads(masks, dmixed[:, cols])
        probs = p_ref[0, g * GROUP * rows : (g + 1) * GROUP * rows, :]
        k4 = k_ref[0, :, cols]
        dprobs = nt(dm, v_ref[0, :, cols])
        wide = probs.astype(F32)
        both = wide * dprobs
        ds = (both - wide * jnp.sum(both, axis=-1, keepdims=True)).astype(BF16)
        dv = tn(probs, dm)[0:rows, :].astype(BF16)
        dk = tn(ds, spread_heads(masks, q_ref[0, :, cols]))[0:rows, :].astype(BF16)
        dq = None
        for h in range(GROUP):
            part = nn(ds[h * rows : (h + 1) * rows, :], jnp.where(masks[h], k4, zero))
            dq = part if dq is None else dq + part
        dq = (dq.astype(BF16).astype(F32) * (1.0 / math.sqrt(DH))).astype(BF16)
        dqkv_ref[0, :, cols] = dq
        dqkv_ref[0, :, width + g * LANES : width + (g + 1) * LANES] = dk
        dqkv_ref[0, :, 2 * width + g * LANES : 2 * width + (g + 1) * LANES] = dv
    collect(6, dqkv_ref[0, :, 0:width].astype(F32))
    collect(7, dqkv_ref[0, :, 2 * width :].astype(F32))
    wait_weights(wp, sems.at[0])
    da = nt(dqkv_ref[0, :, 0:width], wp[:, 0:width])
    da = da + nt(dqkv_ref[0, :, width : 2 * width], wp[:, width : 2 * width])
    da = da + nt(dqkv_ref[0, :, 2 * width :], wp[:, 2 * width :])
    if x_ref.shape[1] == seq:
        xs[tail:rows, :] = jnp.zeros((rows - tail, width), F32)
        xs[0:seq, :] = x_ref[0].astype(F32)
        x = xs[...]
    else:
        x = x_ref[0]
    unit, inverse = normalized(x)
    collect(0, da * unit)
    collect(1, da)
    dx = dh + norm_back(da, unit, inverse, shared_ref[0:1, :])
    dx_ref[0] = dx[0 : dx_ref.shape[1], :]


def gradient_kernel(
    pieces, ratio, meta, a_ref, dqkv_ref, mixed_ref, dhr_ref, c_ref, du_ref, act_ref, dyr_ref,
    *rest,
):
    out_ref, turned, wide = rest[-3:]
    side = out_ref.shape[-1]
    step = pl.program_id(0)
    start_out = 3 * pieces
    start_up = 4 * pieces
    start_down = start_up + pieces * ratio

    def by_columns(lhs_ref, rhs_ref, first):
        @pl.when(first)
        def _():
            turned[...] = lhs_ref[...].T

        res = nn(turned[...], rhs_ref[...])
        for t in range(out_ref.shape[0]):
            out_ref[t, 0] = res[:, t * side : (t + 1) * side].astype(BF16)

    def by_rows(lhs_ref, rhs_ref, first):
        @pl.when(first)
        def _():
            wide[...] = lhs_ref[...].T

        res = nn(wide[...], rhs_ref[...])
        for t in range(out_ref.shape[0]):
            out_ref[t, 0] = res[t * side : (t + 1) * side, :].astype(BF16)

    @pl.when(step < start_out)
    def _():
        by_columns(a_ref, dqkv_ref, step % 3 == 0)

    @pl.when((step >= start_out) & (step < start_up))
    def _():
        by_rows(mixed_ref, dhr_ref, step == start_out)

    @pl.when((step >= start_up) & (step < start_down))
    def _():
        by_columns(c_ref, du_ref, (step - start_up) % ratio == 0)

    @pl.when(step >= start_down)
    def _():
        by_rows(act_ref, dyr_ref, (step - start_down) % pieces == 0)


def adam_kernel(live_ref, factor_ref, g_ref, w_ref, l_ref, r_ref, m_ref, s_ref, w_out, m_out, s_out):
    step_rate = factor_ref[1]
    high = lax.Precision.HIGHEST

    def dot(a, b, dims):
        return lax.dot_general(a, b, (dims, ((), ())), precision=high, preferred_element_type=F32)

    slot = pl.program_id(0)
    alive = live_ref[slot] > 0
    weight = w_ref[0, 0]
    left = l_ref[0, 0]
    right = r_ref[0, 0]
    gradient = g_ref[0].astype(F32) * factor_ref[0]
    turned = dot(dot(left, gradient, ((0,), (0,))), right, ((1,), (0,)))
    first = MOMENT_DECAY * m_ref[0, 0] + (1.0 - MOMENT_DECAY) * turned
    second = MOMENT_DECAY * s_ref[0, 0] + (1.0 - MOMENT_DECAY) * turned * turned
    stepped = first / CORRECTION / (jnp.sqrt(second / CORRECTION) + ADAM_EPSILON)
    back = dot(dot(left, stepped, ((1,), (0,))), right, ((1,), (1,)))
    w_out[0, 0] = jnp.where(alive, weight - step_rate * (back + WEIGHT_DECAY * weight), weight)
    m_out[0, 0] = jnp.where(alive, first, m_ref[0, 0])
    s_out[0, 0] = jnp.where(alive, second, s_ref[0, 0])


def plain_update(gradient, weight, first_state, second_state, step_rate):
    first_new = MOMENT_DECAY * first_state + (1.0 - MOMENT_DECAY) * gradient
    second_new = MOMENT_DECAY * second_state + (1.0 - MOMENT_DECAY) * gradient * gradient
    stepped = first_new / CORRECTION / (jnp.sqrt(second_new / CORRECTION) + ADAM_EPSILON)
    return (weight - step_rate * stepped, first_new, second_new)


def image_spec(shape):
    return pl.BlockSpec((1,) + tuple(shape[1:]), lambda i, meta: (i, 0, 0))


def shifted_spec(shape, count, place):
    return pl.BlockSpec((1,) + tuple(shape[1:]), lambda i, meta: (meta[place] * count + i, 0, 0))


def whole_spec(shape):
    return pl.BlockSpec(tuple(shape), lambda i, meta: (0,) * len(shape))


def params():
    return pltpu.CompilerParams(vmem_limit_bytes=VMEM_LIMIT, dimension_semantics=("arbitrary",))


def weight_scratch(width, ratio, rows):
    return [
        pltpu.VMEM((width, 3 * width), BF16),
        pltpu.VMEM((width, width), BF16),
        pltpu.VMEM((width, ratio * width), BF16),
        pltpu.VMEM((ratio * width, width), BF16),
        pltpu.VMEM((rows, width), F32),
        pltpu.SemaphoreType.DMA((4,)),
    ]


def forward_layer(layer, last, count, seq, rows, keys, meta, place, stream, shared, split, blocks):
    width = shared.shape[1]
    ratio = split.shape[0] - 2
    heads = width // DH
    sd = jax.ShapeDtypeStruct
    outs = [
        sd((count, rows, width), BF16),
        sd((count, rows, width), BF16),
        sd((count, keys, width), BF16),
        sd((count, keys, width), BF16),
        sd((count, heads * rows, keys), BF16),
        sd((count, rows, width), BF16),
        sd((count, rows, width), F32),
        sd((count, rows, width), BF16),
        sd((count, rows, ratio * width), BF16),
        sd((count, rows, ratio * width), BF16),
        sd((count, seq if last else rows, width), F32),
    ]
    x_spec = (
        shifted_spec(stream.shape, count, place) if stream.shape[0] != count else image_spec(stream.shape)
    )
    grid = pltpu.PrefetchScalarGridSpec(
        num_scalar_prefetch=1,
        grid=(count,),
        in_specs=[x_spec, whole_spec(shared.shape), whole_spec(split.shape), pl.BlockSpec(memory_space=pl.ANY)],
        out_specs=[image_spec(o.shape) for o in outs],
        scratch_shapes=weight_scratch(width, ratio, rows),
    )
    return pl.pallas_call(
        functools.partial(forward_kernel, layer, seq, rows, keys),
        grid_spec=grid,
        out_shape=outs,
        compiler_params=params(),
        name=f"forward{layer}",
    )(meta, stream, shared, split, blocks)


def backward_layer(
    layer, last, count, seq, rows, keys, meta, place, grad, hits, stream, kept, shared, blocks
):
    a, q, k, v, probs, mixed, h, c, act, slope, _ = kept
    width = shared.shape[1]
    ratio = act.shape[2] // width
    sd = jax.ShapeDtypeStruct
    first = stream.shape[0] != count
    outs = [
        sd((count, rows, width), BF16),
        sd((count, rows, ratio * width), BF16),
        sd((count, rows, width), BF16),
        sd((count, rows, 3 * width), BF16),
        sd((16, width), F32),
        sd((count, seq if first else rows, width), F32),
    ]
    out_specs = [image_spec(o.shape) if o.shape[0] == count else whole_spec(o.shape) for o in outs]
    x_spec = shifted_spec(stream.shape, count, place) if first else image_spec(stream.shape)
    dy_spec = shifted_spec(grad.shape, count, place) if last else image_spec(grad.shape)
    grid = pltpu.PrefetchScalarGridSpec(
        num_scalar_prefetch=1,
        grid=(count,),
        in_specs=[
            dy_spec,
            shifted_spec(hits.shape, count, place),
            x_spec,
            image_spec(h.shape),
            image_spec(slope.shape),
            image_spec(probs.shape),
            image_spec(q.shape),
            image_spec(k.shape),
            image_spec(v.shape),
            whole_spec(shared.shape),
            pl.BlockSpec(memory_space=pl.ANY),
        ],
        out_specs=out_specs,
        scratch_shapes=weight_scratch(width, ratio, rows),
    )
    return pl.pallas_call(
        functools.partial(backward_kernel, layer, seq, rows, keys, last),
        grid_spec=grid,
        out_shape=outs,
        compiler_params=params(),
        name=f"backward{layer}",
    )(meta, grad, hits, stream, h, slope, probs, q, k, v, shared, blocks)


def layer_gradients(layer, meta, kept, pieces_back, target, slot_total, side, share_count):
    a, q, k, v, probs, mixed, h, c, act, slope, _ = kept
    dyr, du, dhr, dqkv = pieces_back
    flat = lambda z: z.reshape(-1, z.shape[-1])
    ops = [flat(z) for z in (a, dqkv, mixed, dhr, c, du, act, dyr)]
    tokens, width = ops[0].shape
    ratio = ops[5].shape[1] // width
    pieces = width // side
    per_layer = pieces * (4 + 2 * ratio)
    start_out = 3 * pieces
    start_up = 4 * pieces
    start_down = start_up + pieces * ratio

    def clip(s, low, count):
        return jnp.minimum(jnp.maximum(s - low, 0), count - 1)

    maps = [
        ((tokens, side), lambda s, meta: (0, clip(s, 0, start_out) // 3)),
        ((tokens, width), lambda s, meta: (0, clip(s, 0, start_out) % 3)),
        ((tokens, width), lambda s, meta: (0, 0)),
        ((tokens, side), lambda s, meta: (0, clip(s, start_out, pieces))),
        ((tokens, side), lambda s, meta: (0, clip(s, start_up, pieces * ratio) // ratio)),
        ((tokens, width), lambda s, meta: (0, clip(s, start_up, pieces * ratio) % ratio)),
        ((tokens, width), lambda s, meta: (0, clip(s, start_down, pieces * ratio) // pieces)),
        ((tokens, side), lambda s, meta: (0, clip(s, start_down, pieces * ratio) % pieces)),
    ]
    in_specs = [pl.BlockSpec(shape, index) for shape, index in maps]
    alias = {}
    if target is not None:
        in_specs.append(pl.BlockSpec(memory_space=pl.ANY))
        ops.append(target)
        alias = {len(ops): 0}
    grid = pltpu.PrefetchScalarGridSpec(
        num_scalar_prefetch=1,
        grid=(per_layer,),
        in_specs=in_specs,
        out_specs=pl.BlockSpec(
            (share_count, 1, side, side), lambda s, meta: (0, meta[layer * per_layer + s], 0, 0)
        ),
        scratch_shapes=[pltpu.VMEM((side, tokens), BF16), pltpu.VMEM((width, tokens), BF16)],
    )
    return pl.pallas_call(
        functools.partial(gradient_kernel, pieces, ratio),
        grid_spec=grid,
        out_shape=jax.ShapeDtypeStruct((share_count, slot_total, side, side), BF16),
        input_output_aliases=alias,
        compiler_params=params(),
        name=f"gradients{layer}",
    )(meta, *ops)


def adam(live, scalars, gradient, weight, left, right, first, second):
    count, _, side, _ = weight.shape
    spec = pl.BlockSpec((1, 1, side, side), lambda i: (i, 0, 0, 0))
    smem = pl.BlockSpec(memory_space=pltpu.SMEM)
    out = jax.ShapeDtypeStruct(weight.shape, F32)
    return pl.pallas_call(
        adam_kernel,
        grid=(count,),
        in_specs=[smem, smem, pl.BlockSpec((1, side, side), lambda i: (i, 0, 0))] + [spec] * 5,
        out_specs=[spec] * 3,
        out_shape=[out] * 3,
        compiler_params=params(),
        name="adam",
    )(live, scalars, gradient, weight, left, right, first, second)


def shards(
    block_input,
    cotangent,
    mask_patches,
    owners,
    master_slots,
    left_bases,
    right_bases,
    first_moment,
    second_moment,
    shared_vectors,
    shared_first,
    shared_second,
    split_vectors,
    split_first,
    split_second,
):
    slot_count = master_slots.shape[0]
    side = master_slots.shape[-1]
    layer_count = shared_vectors.shape[0]
    width = shared_vectors.shape[2]
    half = split_vectors.shape[2]
    ratio = split_vectors.shape[1] - 2
    block_total = owners.shape[0]
    per_layer = block_total // layer_count
    image_total, seq = block_input.shape[:2]
    dp_count = lax.axis_size("dp")
    tp_count = lax.axis_size("tp")
    count = image_total // tp_count
    rows = round_up(seq, 16)
    keys = round_up(seq, 128)
    slot_total = dp_count * slot_count
    dp_rank = lax.axis_index("dp")
    tp_rank = lax.axis_index("tp")
    slot_index = positions(owners, slot_count)
    meta = jnp.concatenate([slot_index, tp_rank[None].astype(jnp.int32)])
    place = block_total

    blocks = lax.all_gather(master_slots[:, 0].astype(BF16), "dp", axis=0, tiled=True)
    blocks = lax.all_gather(blocks, "tp", axis=0)
    split_all = lax.all_gather(split_vectors, "tp", axis=2, tiled=True)
    hits = mask_patches[:, None, :]

    streams = [block_input]
    kept = []
    for layer in range(layer_count):
        last = layer == layer_count - 1
        saved = forward_layer(
            layer, last, count, seq, rows, keys, meta, place, streams[-1],
            shared_vectors[layer], split_all[layer], blocks,
        )
        kept.append(saved)
        streams.append(saved[-1])
    block_output = lax.all_gather(streams[-1], "tp", axis=0, tiled=True)
    grad = cotangent
    vectors = [None] * layer_count
    target = None
    for layer in reversed(range(layer_count)):
        last = layer == layer_count - 1
        dyr, du, dhr, dqkv, vectors[layer], grad = backward_layer(
            layer, last, count, seq, rows, keys, meta, place, grad, hits, streams[layer],
            kept[layer], shared_vectors[layer], blocks,
        )
        target = layer_gradients(
            layer, meta, kept[layer], (dyr, du, dhr, dqkv), target, slot_total, side, tp_count
        )
    input_grad = lax.all_gather(grad, "tp", axis=0, tiled=True)
    reduced = lax.psum_scatter(target, "tp", scatter_dimension=0, tiled=False)
    reduced = lax.psum_scatter(reduced, "dp", scatter_dimension=0, tiled=True).astype(F32)
    vector_sum = lax.psum(jnp.stack(vectors), ("dp", "tp"))
    shared_sum = vector_sum[:, :6]
    split_full = vector_sum[:, 6 : 8 + ratio]
    split_sum = lax.dynamic_slice_in_dim(split_full, tp_rank * half, half, axis=2)
    mine_ids = dp_rank * slot_count + jnp.arange(slot_count, dtype=jnp.int32)
    matches = slot_index[None, :] == mine_ids[:, None]
    live = jnp.any(matches, axis=1)
    block_layer = jnp.arange(block_total, dtype=jnp.int32) // per_layer
    owned_layer = jnp.sum(jnp.where(matches, block_layer[None, :], 0), axis=1)
    block_squares = jnp.where(live, jnp.sum(reduced * reduced, axis=(1, 2)), 0.0)
    layer_pick = (owned_layer[:, None] == jnp.arange(layer_count, dtype=jnp.int32)[None, :]) & live[
        :, None
    ]
    matrix_squares = jnp.sum(jnp.where(layer_pick, block_squares[:, None], 0.0), axis=0)
    vector_squares = jnp.sum(shared_sum * shared_sum, axis=(1, 2)) + jnp.sum(
        split_full * split_full, axis=(1, 2)
    )
    squares = lax.psum(matrix_squares, ("dp", "tp")) + vector_squares
    layer_norms = jnp.sqrt(squares)
    global_norm = jnp.sqrt(jnp.sum(squares))
    factor = CLIP_NORM / jnp.maximum(global_norm, CLIP_NORM)
    step_rate = 0.5 / math.sqrt(width)
    scalars = jnp.stack([factor, jnp.asarray(step_rate, F32)])
    new_master, new_first, new_second = adam(
        live.astype(jnp.int32), scalars, reduced, master_slots, left_bases, right_bases,
        first_moment, second_moment,
    )
    new_shared, new_shared_first, new_shared_second = plain_update(
        shared_sum * factor, shared_vectors, shared_first, shared_second, VECTOR_RATE
    )
    new_split, new_split_first, new_split_second = plain_update(
        split_sum * factor, split_vectors, split_first, split_second, VECTOR_RATE
    )
    return (
        block_output,
        input_grad,
        new_master,
        new_first,
        new_second,
        new_shared,
        new_shared_first,
        new_shared_second,
        new_split,
        new_split_first,
        new_split_second,
        layer_norms,
        global_norm,
    )


def solution(mesh):
    sharded = P("dp", None, None)
    slots = P("dp", "tp", None, None)
    split = P(None, None, "tp")
    return jax.shard_map(
        shards,
        mesh=mesh,
        in_specs=(sharded, sharded, P("dp", None), P())
        + (slots,) * 5
        + (P(),) * 3
        + (split,) * 3,
        out_specs=(sharded, sharded) + (slots,) * 3 + (P(),) * 3 + (split,) * 3 + (P(), P()),
        check_vma=False,
    )
```

time: 1420 us -> 972 us (0.68)
  Pallas kernels: 0 us -> 245 us
  matrix products: 241 us -> 0 us
  local copies, waits for them, and re-layouts: 270 us -> 29.9 us
  other arithmetic: 218 us -> 10.6 us
  blocking collectives: 124 us -> 42.6 us
  waiting for transfers between devices: 538 us -> 619 us
    pallas_call x0 -> x7, Pallas kernels: none -> 245 us  [the longest x2 80.7 us: backward_layer(): pl.pallas_call(functools.partial(backward_kernel, layer, seq, rows, keys,...]
    dot_general x40 -> x0, matrix products: 241 us -> none  [the longest x2 29.1 us: feed_back(): jnp.einsum('gsd,jed->gsje', grad_low, w_downward[layer_index], preferred_...]
    reduce_sum x23 -> x1, other arithmetic: 85.9 us -> 1 us  [shards(): jnp.sum(split_full * split_full, axis=(1, 2))]
    psum x2 -> x1, blocking collectives: 124 us -> 40.8 us  [shards(): squares = lax.psum(matrix_squares, ('dp', 'tp')) + vector_squares]
    all_gather x1 -> x4, waiting for transfers between devices: 160 us -> 231 us  [the longest x1 171 us: shards(): lax.all_gather(master_slots[:, 0].astype(BF16), 'dp', axis=0, tiled=True)]
    convert_element_type x6 -> x3, other arithmetic: 72.5 us -> 4.38 us  [the longest x1 2.49 us: shards(): master_slots[:, 0].astype(BF16)]
    slice x27 -> x0, local copies, waits for them, and re-layouts: 65.2 us -> none  [the longest x4 12.7 us: shards(): project[:, :, 2] + value_bias]
    psum x7 -> x1, waiting for transfers between devices: 68.4 us -> 126 us  [shards(): vector_sum = lax.psum(jnp.stack(vectors), ('dp', 'tp'))]
  transfers between devices with their start and end apart: 9 -> 7, of which waited for: 7 -> 7; matrix products, arithmetic and copies ran while one was open for 12% -> 2% of each run, Pallas kernels for 0% -> 0%
where the time goes in v1:
time: 972 us; the launch traced here: 964 us
  waiting for transfers between devices  619 us (64%)
  Pallas kernels  245 us (25%)
  blocking collectives  42.6 us (4%)
  local copies, waits for them, and re-layouts  29.9 us (3%)
  between operations  16.4 us (2%)
  other arithmetic  10.6 us (1%)
    reduce_scatter x1, waiting for transfers between devices, shards(): lax.psum_scatter(reduced, 'dp', scatter_dimension=0, tiled=True).astype(F32)  222 us
    all_gather x1, waiting for transfers between devices, shards(): lax.all_gather(master_slots[:, 0].astype(BF16), 'dp', axis=0, tiled=True)  171 us
    psum x1, waiting for transfers between devices, shards(): vector_sum = lax.psum(jnp.stack(vectors), ('dp', 'tp'))  126 us
    pallas_call x2, Pallas kernels, backward_layer(): pl.pallas_call(functools.partial(backward_kernel, layer, seq, rows, keys,...  80.7 us
    pallas_call x2, Pallas kernels, layer_gradients(): pl.pallas_call(functools.partial(gradient_kernel, pieces, ratio), grid_sp...  73.2 us
    pallas_call x2, Pallas kernels, forward_layer(): pl.pallas_call(functools.partial(forward_kernel, layer, seq, rows, keys),...  71.4 us
    psum x1, blocking collectives, shards(): squares = lax.psum(matrix_squares, ('dp', 'tp')) + vector_squares  40.8 us
    reduce_scatter x1, waiting for transfers between devices, shards(): reduced = lax.psum_scatter(target, 'tp', scatter_dimension=0, tiled=False)  38.2 us
  transfers between devices with their start and end apart: 7, of which 7 were waited for; matrix products, arithmetic and copies ran while one was open for 2% of the time, Pallas kernels for 0%

profile of v1, /device:TPU:0, one launch (start us, length us, event | category | flops | bytes accessed | tf_op | source)
XLA Modules:
  0.0 963.7 jit_solution(12112803829326181208)
XLA Ops:
  7.2 0.0 all-gather.11.cloned.1.call-start
  7.2 2.5 convert_element_type.16
  9.7 0.0 all-gather.11.cloned.1.call-update
  9.7 0.0 all-gather.13.cloned.1.call-start
  9.8 171.2 %all-gather.11.cloned.1.call-done = bf16[48,1,384,384]{3,2,1,0:T(8,128)(2,1)} async-done(((bf16[3,1,384,384]{3,2,1,0:T(8,128)(2,1)}), bf16[48,1,384,384]{3,2,1,0:T(8,128)(2,1)}) %all-gather.11.cloned.1.call-update) | async-done | bytes 14155792 | tf_op jit(solution)/shard_map/all_gather | solution.py:593
  181.0 0.0 all-gather.13.cloned.1.call-update
  181.0 0.0 reduce-scatter.3.cloned.1.call-start
  181.1 0.7 copy-done.3
  181.8 0.9 copy-done.1
  182.7 2.0 copy.71.x_ref
  184.7 8.1 copy.73.dy_ref
  192.8 1.8 all_gather.18
  194.6 0.2 convert_reduce_fusion
  194.8 0.6 pad_add_fusion.meta
  195.4 0.6 slice_bitcast_fusion.1
  196.0 0.6 slice_bitcast_fusion
  196.7 29.9 %all-gather.13.cloned.1.call-done = bf16[96,1,384,384]{3,2,1,0:T(8,128)(2,1)} async-done(((bf16[48,1,384,384]{3,2,1,0:T(8,128)(2,1)}), bf16[96,1,384,384]{3,2,1,0:T(8,128)(2,1)}) %all-gather.13.cloned.1.call-update) | async-done | bytes 28311568 | tf_op jit(solution)/shard_map/all_gather | solution.py:594
  226.6 35.2 %forward0.1 = (bf16[4,208,768]{2,1,0:T(8,128)(2,1)}, bf16[4,208,768]{2,1,0:T(8,128)(2,1)}, bf16[4,256,768]{2,1,0:T(8,128)(2,1)}, bf16[4,256,768]{2,1,0:T(8,128)(...) custom-call(s32[49]{0:T(128)} %pad_add_fusion.meta, ...), custom_call_target="tpu_custom_call" | custom-call | tf_op jit(solution)/shard_map/forward0/pallas_call | solution.py:432
  261.8 36.2 %forward1.1 = (bf16[4,208,768]{2,1,0:T(8,128)(2,1)}, bf16[4,208,768]{2,1,0:T(8,128)(2,1)}, bf16[4,256,768]{2,1,0:T(8,128)(2,1)}, bf16[4,256,768]{2,1,0:T(8,128)(...) custom-call(s32[49]{0:T(128)} %pad_add_fusion.meta, ...), custom_call_target="tpu_custom_call" | custom-call | tf_op jit(solution)/shard_map/forward1/pallas_call | solution.py:432
  298.0 40.1 %backward1.1 = (bf16[4,208,768]{2,1,0:T(8,128)(2,1)}, bf16[4,208,3072]{2,1,0:T(8,128)(2,1)}, bf16[4,208,768]{2,1,0:T(8,128)(2,1)}, bf16[4,208,2304]{2,1,0:T(8,12...) custom-call(s32[49]{0:T(128)} %pad_add_fusion.meta, f32[8,197,768]{2,1,0:T(8,128)} %copy.73.dy_ref, ...), custom_call_target="tpu_custom_call" | custom-call | tf_op jit(solution)/shard_map/backward1/pallas_call | solution.py:479
  338.1 40.6 %backward0.1 = (bf16[4,208,768]{2,1,0:T(8,128)(2,1)}, bf16[4,208,3072]{2,1,0:T(8,128)(2,1)}, bf16[4,208,768]{2,1,0:T(8,128)(2,1)}, bf16[4,208,2304]{2,1,0:T(8,12...) custom-call(s32[49]{0:T(128)} %pad_add_fusion.meta, f32[4,208,768]{2,1,0:T(8,128)} %get-tuple-element.58.dy_ref, ...), custom_call_target="tpu_custom_call" | custom-call | tf_op jit(solution)/shard_map/backward0/pallas_call | solution.py:479
  378.7 36.5 %gradients1.1.rest_0_ = bf16[2,48,384,384]{3,2,1,0:T(8,128)(2,1)} custom-call(s32[49]{0:T(128)} %pad_add_fusion.meta, bf16[832,768]{1,0:T(8,128)(2,1)} %bitcast.47, bf16[832,2304]{1,0:T(8,128)(2,1)} %bitcast.40, bf16[832,768]{1,0:T(8,128)(2,1)} %bitcast.48, bf16[832,768]{1,0:T(8,128)(2,1)} %bitcast.51, bf16[832,768]{1,0:T(8,128)(2,1)} %bitcast.49, ...), custom_call_target="tpu_custom_call" | custom-call | tf_op jit(solution)/shard_map/gradients1/pallas_call | solution.py:529
  415.1 36.7 %gradients0.1 = bf16[2,48,384,384]{3,2,1,0:T(8,128)(2,1)} custom-call(s32[49]{0:T(128)} %pad_add_fusion.meta, bf16[832,768]{1,0:T(8,128)(2,1)} %bitcast.42, bf16[832,2304]{1,0:T(8,128)(2,1)} %bitcast.41, bf16[832,768]{1,0:T(8,128)(2,1)} %bitcast.43, bf16[832,768]{1,0:T(8,128)(2,1)} %bitcast.46, ...), custom_call_target="tpu_custom_call", output_to_operand_aliasing={{}: (9, {})} | custom-call | tf_op jit(solution)/shard_map/gradients0/pallas_call | solution.py:529
  451.9 0.0 reduce-scatter.3.cloned.1.call-update
  451.9 0.0 all-reduce.2.cloned.1.call-start
  451.9 0.7 copy-done.5
  452.6 0.0 copy-done.6
  452.7 0.6 pad_maximum_fusion
  453.3 0.0 all-reduce.2.cloned.1.call-update
  453.3 0.0 all-gather.9.cloned.1.call-start
  453.4 0.5 all-gather.9.cloned.1.call-update
  453.9 0.0 reduce-scatter.5.cloned.1.call-start
  454.0 38.2 %reduce-scatter.3.cloned.1.call-done = bf16[1,48,384,384]{3,2,1,0:T(8,128)(2,1)} async-done(((bf16[2,48,384,384]{3,2,1,0:T(8,128)(2,1)}), bf16[1,48,384,384]{3,2,1,0:T(8,128)(2,1)}) %reduce-scatter.3.cloned.1.call-update) | async-done | bytes 14155792 | tf_op jit(solution)/shard_map/reduce_scatter | solution.py:622
  492.2 0.0 reduce-scatter.5.cloned.1.call-update
  492.2 0.0 all-gather.7.cloned.1.call-start
  492.3 0.7 all-gather.7.cloned.1.call-update
  493.0 0.2 compare_reduce_fusion
  493.2 0.5 convert_element_type.18.live_ref
  493.8 0.2 fusion.3
  493.9 126.1 %all-reduce.2.cloned.1.call-done = f32[2,16,768]{2,1,0:T(8,128)} async-done(((f32[2,16,768]{2,1,0:T(8,128)}), f32[2,16,768]{2,1,0:T(8,128)}) %all-reduce.2.cloned.1.call-update) | async-done | bytes 98320 | tf_op jit(solution)/shard_map/psum | solution.py:624
  620.1 1.0 multiply_reduce_fusion.1
  621.1 16.0 %all-gather.9.cloned.1.call-done = f32[8,197,768]{2,1,0:T(8,128)} async-done(((f32[4,197,768]{2,1,0:T(8,128)}), f32[8,197,768]{2,1,0:T(8,128)}) %all-gather.9.cloned.1.call-update) | async-done | bytes 4841488 | tf_op jit(solution)/shard_map/all_gather | solution.py:621
  637.1 6.2 copy.82
  643.2 221.9 %reduce-scatter.5.cloned.1.call-done = bf16[3,384,384]{2,1,0:T(8,128)(2,1)} async-done(((bf16[48,384,384]{2,1,0:T(8,128)(2,1)}), bf16[3,384,384]{2,1,0:T(8,128)(2,1)}) %reduce-scatter.5.cloned.1.call-update) | async-done | bytes 884752 | tf_op jit(solution)/shard_map/reduce_scatter | solution.py:623
  865.1 1.5 multiply_reduce_fusion
  866.6 0.1 fusion.4
  866.8 0.0 copy-start.7
  866.8 0.0 copy-start.8
  866.8 0.0 copy-start.9
  866.8 0.0 copy-start.10
  866.8 14.3 %all-gather.7.cloned.1.call-done = f32[8,197,768]{2,1,0:T(8,128)} async-done(((f32[4,197,768]{2,1,0:T(8,128)}), f32[8,197,768]{2,1,0:T(8,128)}) %all-gather.7.cloned.1.call-update) | async-done | bytes 4841488 | tf_op jit(solution)/shard_map/all_gather | solution.py:608
  881.1 6.2 copy.81
  887.3 40.8 %psum.14 = f32[2]{0:T(128)S(1)} all-reduce(f32[2]{0:T(128)S(1)} %fusion.4), channel_id=1, replica_groups=mesh['dp'=16,'tp'=2] {'dp','tp'}, use_global_device_ids=true, to_apply=%region_7.8 | all-reduce | flops 2 | bytes 16 | tf_op jit(solution)/shard_map/psum | solution.py:641
  928.1 1.1 fusion.5
  930.0 0.1 multiply_subtract_fusion
  930.1 0.6 copy.86
  930.7 0.6 copy.87
  931.3 0.6 copy.88
  931.9 0.6 copy.83
  932.6 0.6 copy.84
  933.2 0.6 copy.85
  933.8 0.6 pad_maximum_fusion.1.factor_ref
  934.4 1.3 convert_element_type.19.g_ref
  935.7 19.7 %adam.1 = (f32[3,1,384,384]{3,2,1,0:T(8,128)}, f32[3,1,384,384]{3,2,1,0:T(8,128)}, f32[3,1,384,384]{3,2,1,0:T(8,128)}) custom-call(s32[3]{0:T(128)} %convert_element_type.18.live_ref, f32[2]{0:T(128)} %pad_maximum_fusion.1.factor_ref, f32[3,384,384]{2,1,0:T(8,128)} %convert_element_type.19.g_ref, f32[3,1,384,384]{3,2,1,0:T(8,128)} %w_ref.1, ...), custom_call_target="tpu_custom_call" | custom-call | tf_op jit(solution)/shard_map/adam/pallas_call | solution.py:544
  (23 shorter events, 0.1 us)
Async XLA Ops:
  7.2 173.8 %all-gather.11.cloned.1.call-start = ((), (), s32[]{:S(2)}) async-start(), calls=%async_computation.7 | async-start | bytes 15040512 | tf_op jit(solution)/shard_map/all_gather | solution.py:593
  9.7 216.8 %all-gather.13.cloned.1.call-start = ((), (), s32[]{:S(2)}) async-start(), calls=%async_computation.8 | async-start | bytes 42467328 | tf_op jit(solution)/shard_map/all_gather | solution.py:594
  181.0 0.8 copy-start.3
  181.0 1.7 copy-start.1
  181.0 311.2 %reduce-scatter.3.cloned.1.call-start = ((), (), s32[]{:S(2)}) async-start(), calls=%async_computation.4 | async-start | bytes 42467328 | tf_op jit(solution)/shard_map/reduce_scatter | solution.py:622
  182.7 2.0 copy-start.4
  184.7 9.9 %copy-start.11 = (s32[48]{0:T(128)S(1)}, s32[48]{0:T(128)}, u32[]{:S(2)}) copy-start(s32[48]{0:T(128)} %param.18) | copy-start | bytes 580
  451.8 0.8 copy-start.5
  451.8 0.8 copy-start.6
  451.9 168.2 %all-reduce.2.cloned.1.call-start = ((), (), s32[]{:S(2)}) async-start(), calls=%async_computation.6 | async-start | bytes 196608 | tf_op jit(solution)/shard_map/psum | solution.py:624
  453.3 183.7 %all-gather.9.cloned.1.call-start = ((), (), s32[]{:S(2)}) async-start(), calls=%async_computation.3 | async-start | bytes 7372800 | tf_op jit(solution)/shard_map/all_gather | solution.py:621
  453.9 411.2 %reduce-scatter.5.cloned.1.call-start = ((), (), s32[]{:S(2)}) async-start(), calls=%async_computation.5 | async-start | bytes 15040512 | tf_op jit(solution)/shard_map/reduce_scatter | solution.py:623
  492.2 388.9 %all-gather.7.cloned.1.call-start = ((), (), s32[]{:S(2)}) async-start(), calls=%async_computation.2 | async-start | bytes 7372800 | tf_op jit(solution)/shard_map/all_gather | solution.py:608
  866.8 63.2 %copy-start.2 = (f32[2,16,768]{2,1,0:T(8,128)S(1)}, f32[2,16,768]{2,1,0:T(8,128)}, u32[]{:S(2)}) copy-start(f32[2,16,768]{2,1,0:T(8,128)} %all-reduce.2.cloned.1.call-done) | copy-start | bytes 294916
  866.8 63.2 %copy-start.7 = (f32[2,6,768]{2,0,1:T(2,128)S(1)}, f32[2,6,768]{2,0,1:T(2,128)}, u32[]{:S(2)}) copy-start(f32[2,6,768]{2,0,1:T(2,128)} %param.25) | copy-start | bytes 110596
  866.8 63.2 %copy-start.8 = (f32[2,6,768]{2,0,1:T(2,128)S(1)}, f32[2,6,768]{2,0,1:T(2,128)}, u32[]{:S(2)}) copy-start(f32[2,6,768]{2,0,1:T(2,128)} %param.26) | copy-start | bytes 110596
  866.8 63.2 %copy-start.9 = (f32[2,6,384]{2,0,1:T(2,128)S(1)}, f32[2,6,384]{2,0,1:T(2,128)}, u32[]{:S(2)}) copy-start(f32[2,6,384]{2,0,1:T(2,128)} %param.28) | copy-start | bytes 55300
  866.8 63.2 %copy-start.10 = (f32[2,6,384]{2,0,1:T(2,128)S(1)}, f32[2,6,384]{2,0,1:T(2,128)}, u32[]{:S(2)}) copy-start(f32[2,6,384]{2,0,1:T(2,128)} %param.29) | copy-start | bytes 55300
  866.8 67.6 %copy-start = (bf16[3,384,384]{2,1,0:T(8,128)(2,1)S(1)}, bf16[3,384,384]{2,1,0:T(8,128)(2,1)}, u32[]{:S(2)}) copy-start(bf16[3,384,384]{2,1,0:T(8,128)(2,1)} %reduce-scatter.5.cloned.1.call-done) | copy-start | bytes 2654212
Sparse Core Ops, SparseCore 0:
  11.4 169.5 all-gather.10
  182.5 43.9 all-gather.12
  452.0 40.1 reduce-scatter.2
  498.2 121.7 all-reduce.1
  621.4 15.5 all-gather.8
  642.7 222.4 reduce-scatter.4
  866.7 14.3 all-gather.6

commit v2 on v1

--- a/solution.py
+++ b/solution.py
@@ -367,6 +367,467 @@
     s_out[0, 0] = jnp.where(alive, second, s_ref[0, 0])
 
 
+def line_sizes(dp_count):
+    if dp_count == 16:
+        return (4, 2, 2)
+    if dp_count == 64:
+        return (4, 4, 4)
+    return (dp_count, 1, 1)
+
+
+def part_table(sizes, total_rows):
+    step = 16
+    if sizes[0] > sizes[1]:
+        large = int(total_rows * 0.39) // step * step
+        lengths = (total_rows - 2 * large, large, large)
+        orders = ((2, 1, 0), (0, 1, 2), (0, 2, 1))
+    else:
+        small = total_rows // 3 // step * step
+        lengths = (total_rows - 2 * small, small, small)
+        orders = ((2, 1, 0), (0, 2, 1), (1, 0, 2))
+    offsets = (0, lengths[0], lengths[0] + lengths[1])
+    return [(orders[i], offsets[i], lengths[i]) for i in range(3)]
+
+
+def gather_plan(sizes, parts):
+    ready, moves, plan = {}, [], []
+    free = [0.0] * 3
+    for p, (order, _, _) in enumerate(parts):
+        n = [sizes[d] for d in order]
+        ready[(p, (0, 0, 0))] = 0.0
+        for a in range(n[0]):
+            if a + 1 < n[0]:
+                moves.append((p, 0, (a, 0, 0)))
+            for b in range(n[1]):
+                if b + 1 < n[1]:
+                    moves.append((p, 1, (a, b, 0)))
+                for c in range(n[2] - 1):
+                    moves.append((p, 2, (a, b, c)))
+    while moves:
+        choices = []
+        for move in moves:
+            p, stage, unit = move
+            if (p, unit) in ready:
+                start = max(ready[(p, unit)], free[parts[p][0][stage]])
+                choices.append((start, stage, p, unit))
+        start, stage, p, unit = min(choices)
+        end = start + parts[p][2]
+        free[parts[p][0][stage]] = end
+        ready[(p, one_on(unit, stage))] = end + 60.0
+        plan.append((p, stage, unit))
+        moves.remove((p, stage, unit))
+    return plan
+
+
+def one_on(unit, stage):
+    return tuple(v + (1 if i == stage else 0) for i, v in enumerate(unit))
+
+
+class Place:
+    def __init__(self, sizes):
+        self.sizes = sizes
+        self.dp = lax.axis_index("dp")
+        self.tp = lax.axis_index("tp")
+        nz, ny, nx = sizes
+        self.at = (self.dp // (ny * nx), self.dp // nx % ny, self.dp % nx)
+
+    def shifted(self, offsets):
+        nz, ny, nx = self.sizes
+        z, y, x = [
+            lax.rem(self.at[d] + (offsets[d] + self.sizes[d]) % self.sizes[d], self.sizes[d])
+            for d in range(3)
+        ]
+        return (z * ny + y) * nx + x
+
+    def along(self, dim, step):
+        return self.shifted(tuple(step if d == dim else 0 for d in range(3)))
+
+    def behind(self, order, unit, sign):
+        offsets = [0, 0, 0]
+        for d, v in zip(order, unit):
+            offsets[d] = sign * v
+        return self.shifted(tuple(offsets))
+
+
+def greet(place):
+    barrier = pltpu.get_barrier_semaphore()
+    number = 1
+    pl.semaphore_signal(
+        barrier, inc=1, device_id=(place.dp, 1 - place.tp), device_id_type=pl.DeviceIdType.MESH
+    )
+    for d in range(3):
+        for step in range(1, place.sizes[d]):
+            number += 1
+            pl.semaphore_signal(
+                barrier,
+                inc=1,
+                device_id=(place.along(d, step), place.tp),
+                device_id_type=pl.DeviceIdType.MESH,
+            )
+    pl.semaphore_wait(barrier, number)
+
+
+def remote(src, dst, send, recv, dp, tp):
+    return pltpu.make_async_remote_copy(
+        src_ref=src,
+        dst_ref=dst,
+        send_sem=send,
+        recv_sem=recv,
+        device_id=(dp, tp),
+        device_id_type=pl.DeviceIdType.MESH,
+    )
+
+
+def gather_kernel(
+    sizes, parts, plan, master_ref, split_ref, out_ref, split_out,
+    own_ref, send, recv, over_send, over_recv, here,
+):
+    place = Place(sizes)
+    dp, tp = place.dp, place.tp
+    rows = own_ref.shape[0]
+    dims = [n for n in sizes]
+    numbers = {}
+    for p, (order, _, _) in enumerate(parts):
+        for a in range(dims[order[0]]):
+            for b in range(dims[order[1]]):
+                for c in range(dims[order[2]]):
+                    numbers[(p, (a, b, c))] = len(numbers)
+
+    def region(p, unit, share):
+        order, start, length = parts[p]
+        owner = place.behind(order, unit, -1)
+        return out_ref.at[share, pl.ds(pl.multiple_of(owner * rows + start, 16), length)]
+
+    def source(p, unit):
+        if unit == (0, 0, 0):
+            return own_ref.at[pl.ds(parts[p][1], parts[p][2])]
+        return region(p, unit, tp)
+
+    def pass_over(p, unit):
+        n = numbers[(p, unit)]
+        return remote(
+            source(p, unit), region(p, unit, tp), over_send.at[n], over_recv.at[n], dp, 1 - tp
+        )
+
+    def taken_over(p, unit):
+        n = numbers[(p, unit)]
+        piece = region(p, unit, 1 - tp)
+        return remote(piece, piece, over_send.at[n], over_recv.at[n], dp, 1 - tp)
+
+    def arriving(p, unit):
+        n = numbers[(p, unit)]
+        piece = region(p, unit, tp)
+        return remote(piece, piece, send.at[n], recv.at[n], dp, 1 - tp)
+
+    def sending(p, stage, unit):
+        n = numbers[(p, one_on(unit, stage))]
+        target = place.along(parts[p][0][stage], 1)
+        return remote(source(p, unit), region(p, unit, tp), send.at[n], recv.at[n], target, tp)
+
+    own_ref[...] = master_ref[...].astype(BF16)
+    greet(place)
+    started = []
+    arrived = set()
+
+    def need(p, unit):
+        if (p, unit) in arrived:
+            return
+        arrived.add((p, unit))
+        if unit != (0, 0, 0):
+            arriving(p, unit).wait_recv()
+        late.append((p, unit))
+
+    late = []
+    for p, stage, unit in plan:
+        need(p, unit)
+        move = sending(p, stage, unit)
+        move.start()
+        started.append(move)
+        while late:
+            item = late.pop()
+            move = pass_over(*item)
+            move.start()
+            started.append(move)
+    vector = remote(split_ref, split_out.at[tp], here.at[1], here.at[2], dp, 1 - tp)
+    vector.start()
+    mine = pltpu.make_async_copy(
+        own_ref, out_ref.at[tp, pl.ds(pl.multiple_of(dp * rows, 16), rows)], here.at[0]
+    )
+    mine.start()
+    split_out[tp] = split_ref[...]
+    for p, unit in numbers:
+        need(p, unit)
+        while late:
+            item = late.pop()
+            move = pass_over(*item)
+            move.start()
+            started.append(move)
+    for p, unit in numbers:
+        taken_over(p, unit).wait_recv()
+    for move in started:
+        move.wait_send()
+    remote(split_ref, split_out.at[1 - tp], here.at[1], here.at[2], dp, 1 - tp).wait()
+    mine.wait()
+
+
+def gather_weights(sizes, own, split):
+    dp_count = sizes[0] * sizes[1] * sizes[2]
+    rows, side = own.shape
+    parts = part_table(sizes, rows)
+    plan = gather_plan(sizes, parts)
+    count = 3 * dp_count
+    anyspace = pl.BlockSpec(memory_space=pl.ANY)
+    vmem = pl.BlockSpec(memory_space=pltpu.VMEM)
+    return pl.pallas_call(
+        functools.partial(gather_kernel, sizes, parts, plan),
+        in_specs=[vmem] * 2,
+        out_specs=[anyspace, vmem],
+        out_shape=[
+            jax.ShapeDtypeStruct((2, dp_count * rows, side), BF16),
+            jax.ShapeDtypeStruct((2,) + split.shape, split.dtype),
+        ],
+        scratch_shapes=[pltpu.VMEM((rows, side), BF16)]
+        + [pltpu.SemaphoreType.DMA((count,))] * 4
+        + [pltpu.SemaphoreType.DMA((3,))],
+        compiler_params=pltpu.CompilerParams(
+            collective_id=0, has_side_effects=True, vmem_limit_bytes=VMEM_LIMIT
+        ),
+        name="gather_weights",
+    )(own, split)
+
+
+def reduce_kernel(
+    sizes, parts, plan, layer_count, target_ref, vec_ref, live_ref, block_ref, grad_ref,
+    sum_ref, vec_out, square_out, block_out, grad_out,
+    own, other, pieces, vec_acc, vec_got, sq_acc, sq_got,
+    load, over_send, over_recv, send, recv, vec_send, vec_recv, sq_send, sq_recv, image_sems,
+):
+    place = Place(sizes)
+    dp, tp = place.dp, place.tp
+    rows, side = sum_ref.shape
+    moves = [(p, stage, one_on(unit, stage), unit) for p, stage, unit in reversed(plan)]
+    order_used = []
+    for p, stage, unit, _ in moves:
+        if (p, unit) not in order_used:
+            order_used.append((p, unit))
+    for p in range(len(parts)):
+        order_used.append((p, (0, 0, 0)))
+    numbers = {item: i for i, item in enumerate(order_used)}
+    landing = {}
+    offset = 0
+    inbound = {item: [] for item in order_used}
+    for i, (p, stage, unit, to) in enumerate(moves):
+        landing[i] = (offset, parts[p][2])
+        offset += parts[p][2]
+        inbound[(p, to)].append(i)
+
+    def row_range(p, unit):
+        order, start, length = parts[p]
+        owner = place.behind(order, unit, 1)
+        return pl.ds(pl.multiple_of(owner * rows + start, 16), length)
+
+    def loading(item):
+        span = row_range(*item)
+        n = numbers[item]
+        return pltpu.make_async_copy(target_ref.at[tp, span], own.at[span], load.at[n])
+
+    def passing(item):
+        span = row_range(*item)
+        n = numbers[item]
+        return remote(
+            target_ref.at[1 - tp, span], other.at[span], over_send.at[n], over_recv.at[n], dp, 1 - tp
+        )
+
+    def sending(i):
+        p, stage, unit, _ = moves[i]
+        start, length = landing[i]
+        return remote(
+            own.at[row_range(p, unit)],
+            pieces.at[pl.ds(start, length)],
+            send.at[i],
+            recv.at[i],
+            place.along(parts[p][0][stage], 1),
+            tp,
+        )
+
+    def combine(item, final):
+        p, unit = item
+        order, start, length = parts[p]
+        owner = place.behind(order, unit, 1)
+        base = owner * rows + start
+        froms = [landing[i][0] for i in inbound[item]]
+        step = math.gcd(length, 64)
+
+        def body(k, carry):
+            at = pl.ds(pl.multiple_of(base + k * step, 16), step)
+            total = own[at, :].astype(F32) + other[at, :].astype(F32)
+            for place_from in froms:
+                got = pieces[pl.ds(pl.multiple_of(place_from + k * step, 16), step), :]
+                total = total + got.astype(F32)
+            if final:
+                sum_ref[pl.ds(pl.multiple_of(start + k * step, 16), step), :] = total
+            else:
+                own[at, :] = total.astype(BF16)
+            return carry
+
+        lax.fori_loop(0, length // step, body, 0)
+
+    hops = [(place.dp, 1 - tp)]
+    hop_dims = [None]
+    for d in (2, 1, 0):
+        reach = 1
+        while reach < sizes[d]:
+            there = place.at[d] + reach * (1 - 2 * (place.at[d] // reach % 2))
+            full = [there if e == d else place.at[e] for e in range(3)]
+            hops.append(((full[0] * sizes[1] + full[1]) * sizes[2] + full[2], tp))
+            hop_dims.append(d)
+            reach *= 2
+
+    def vec_hop(k):
+        return remote(
+            vec_acc.at[k], vec_got.at[k], vec_send.at[k], vec_recv.at[k], hops[k][0], hops[k][1]
+        )
+
+    def sq_hop(k):
+        return remote(
+            sq_acc.at[k], sq_got.at[k], sq_send.at[k], sq_recv.at[k], hops[k][0], hops[k][1]
+        )
+
+    def vec_step(k):
+        if k > 0:
+            vec_hop(k - 1).wait_recv()
+            vec_acc[k] = vec_acc[k - 1] + vec_got[k - 1]
+        if k < len(hops):
+            vec_hop(k).start()
+
+    vec_acc[0] = vec_ref[...]
+    greet(place)
+    for item in order_used:
+        loading(item).start()
+        passing(item).start()
+    vec_step(0)
+    done = 0
+    since = 0
+    combined = set()
+    for i, (p, stage, unit, to) in enumerate(moves):
+        item = (p, unit)
+        if item not in combined:
+            combined.add(item)
+            loading(item).wait()
+            passing(item).wait_recv()
+            for j in inbound[item]:
+                sending(j).wait_recv()
+            combine(item, False)
+            dim = hop_dims[min(done, len(hops) - 1)]
+            behind = [
+                j
+                for j in inbound[item]
+                if j >= since and parts[moves[j][0]][0][moves[j][1]] == dim
+            ]
+            if done < len(hops) and (behind or dim is None):
+                done += 1
+                vec_step(done)
+                since = i
+        sending(i).start()
+    while done < len(hops):
+        done += 1
+        vec_step(done)
+    images = [
+        remote(src, dst, image_sems.at[2 * n], image_sems.at[2 * n + 1], dp, 1 - tp)
+        for n, (src, dst) in enumerate(((block_ref, block_out), (grad_ref, grad_out)))
+    ]
+    for image in images:
+        image.start()
+    vec_sum = vec_acc[len(hops)]
+    vec_out[...] = vec_sum
+    for p in range(len(parts)):
+        item = (p, (0, 0, 0))
+        loading(item).wait()
+        passing(item).wait_recv()
+        for j in inbound[item]:
+            sending(j).wait_recv()
+        combine(item, True)
+    slot_count = live_ref.shape[0]
+    tile = jnp.zeros(square_out.shape, F32)
+    lane = lax.broadcasted_iota(jnp.int32, square_out.shape, 1)
+    for s in range(slot_count):
+        block = sum_ref[s * side : (s + 1) * side, :]
+        square = jnp.sum(jnp.sum(block * block, axis=0, keepdims=True), axis=1, keepdims=True)
+        tile = tile + jnp.where(live_ref[s] > 0, square, 0.0)
+    sq_acc[0] = tile
+    for k in range(len(hops)):
+        sq_hop(k).start()
+        sq_hop(k).wait_recv()
+        sq_acc[k + 1] = sq_acc[k] + sq_got[k]
+    tile = sq_acc[len(hops)]
+    per_layer = vec_sum.shape[0] // layer_count
+    for layer in range(layer_count):
+        block = vec_sum[layer * per_layer : (layer + 1) * per_layer, :]
+        square = jnp.sum(jnp.sum(block * block, axis=0, keepdims=True), axis=1, keepdims=True)
+        tile = tile + jnp.where(lane == layer, square, 0.0)
+    square_out[...] = tile
+    for item in order_used:
+        passing(item).wait_send()
+    for i in range(len(moves)):
+        sending(i).wait_send()
+    for k in range(len(hops)):
+        vec_hop(k).wait_send()
+        sq_hop(k).wait_send()
+    for image in images:
+        image.wait()
+
+
+def reduce_gradients(sizes, layer_count, slot_count, target, vectors, live_tile, block_own, grad_own):
+    dp_count = sizes[0] * sizes[1] * sizes[2]
+    side = target.shape[-1]
+    rows = slot_count * side
+    target = target.reshape(2, dp_count * rows, side)
+    parts = part_table(sizes, rows)
+    plan = gather_plan(sizes, parts)
+    hops = 1 + sum(n.bit_length() - 1 for n in sizes)
+    units = 3 * dp_count
+    landing = sum(parts[p][2] for p, _, _ in plan)
+    anyspace = pl.BlockSpec(memory_space=pl.ANY)
+    vmem = pl.BlockSpec(memory_space=pltpu.VMEM)
+    sd = jax.ShapeDtypeStruct
+    dma = pltpu.SemaphoreType.DMA
+    return pl.pallas_call(
+        functools.partial(reduce_kernel, sizes, parts, plan, layer_count),
+        in_specs=[anyspace, vmem, vmem, anyspace, anyspace],
+        out_specs=[vmem, vmem, vmem, anyspace, anyspace],
+        out_shape=[
+            sd((rows, side), F32),
+            sd(vectors.shape, F32),
+            sd(live_tile.shape[1:], F32),
+            sd(block_own.shape, F32),
+            sd(block_own.shape, F32),
+        ],
+        scratch_shapes=[
+            pltpu.VMEM((dp_count * rows, side), BF16),
+            pltpu.VMEM((dp_count * rows, side), BF16),
+            pltpu.VMEM((landing, side), BF16),
+            pltpu.VMEM((hops + 1,) + vectors.shape, F32),
+            pltpu.VMEM((hops,) + vectors.shape, F32),
+            pltpu.VMEM((hops + 1,) + live_tile.shape[1:], F32),
+            pltpu.VMEM((hops,) + live_tile.shape[1:], F32),
+            dma((units,)),
+            dma((units,)),
+            dma((units,)),
+            dma((len(plan),)),
+            dma((len(plan),)),
+            dma((hops,)),
+            dma((hops,)),
+            dma((hops,)),
+            dma((hops,)),
+            dma((4,)),
+        ],
+        compiler_params=pltpu.CompilerParams(
+            collective_id=1, has_side_effects=True, vmem_limit_bytes=VMEM_LIMIT
+        ),
+        name="reduce_gradients",
+    )(target, vectors, live_tile, block_own, grad_own)
+
+
 def plain_update(gradient, weight, first_state, second_state, step_rate):
     first_new = MOMENT_DECAY * first_state + (1.0 - MOMENT_DECAY) * gradient
     second_new = MOMENT_DECAY * second_state + (1.0 - MOMENT_DECAY) * gradient * gradient
@@ -590,9 +1051,11 @@
     meta = jnp.concatenate([slot_index, tp_rank[None].astype(jnp.int32)])
     place = block_total
 
-    blocks = lax.all_gather(master_slots[:, 0].astype(BF16), "dp", axis=0, tiled=True)
-    blocks = lax.all_gather(blocks, "tp", axis=0)
-    split_all = lax.all_gather(split_vectors, "tp", axis=2, tiled=True)
+    sizes = line_sizes(dp_count)
+    own = master_slots.reshape(slot_count * side, side)
+    blocks, split_pair = gather_weights(sizes, own, split_vectors)
+    blocks = blocks.reshape(tp_count, slot_total, side, side)
+    split_all = jnp.concatenate([split_pair[t] for t in range(tp_count)], axis=2)
     hits = mask_patches[:, None, :]
 
     streams = [block_input]
@@ -605,7 +1068,6 @@
         )
         kept.append(saved)
         streams.append(saved[-1])
-    block_output = lax.all_gather(streams[-1], "tp", axis=0, tiled=True)
     grad = cotangent
     vectors = [None] * layer_count
     target = None
@@ -618,27 +1080,30 @@
         target = layer_gradients(
             layer, meta, kept[layer], (dyr, du, dhr, dqkv), target, slot_total, side, tp_count
         )
-    input_grad = lax.all_gather(grad, "tp", axis=0, tiled=True)
-    reduced = lax.psum_scatter(target, "tp", scatter_dimension=0, tiled=False)
-    reduced = lax.psum_scatter(reduced, "dp", scatter_dimension=0, tiled=True).astype(F32)
-    vector_sum = lax.psum(jnp.stack(vectors), ("dp", "tp"))
-    shared_sum = vector_sum[:, :6]
-    split_full = vector_sum[:, 6 : 8 + ratio]
-    split_sum = lax.dynamic_slice_in_dim(split_full, tp_rank * half, half, axis=2)
     mine_ids = dp_rank * slot_count + jnp.arange(slot_count, dtype=jnp.int32)
     matches = slot_index[None, :] == mine_ids[:, None]
     live = jnp.any(matches, axis=1)
     block_layer = jnp.arange(block_total, dtype=jnp.int32) // per_layer
     owned_layer = jnp.sum(jnp.where(matches, block_layer[None, :], 0), axis=1)
-    block_squares = jnp.where(live, jnp.sum(reduced * reduced, axis=(1, 2)), 0.0)
-    layer_pick = (owned_layer[:, None] == jnp.arange(layer_count, dtype=jnp.int32)[None, :]) & live[
-        :, None
-    ]
-    matrix_squares = jnp.sum(jnp.where(layer_pick, block_squares[:, None], 0.0), axis=0)
-    vector_squares = jnp.sum(shared_sum * shared_sum, axis=(1, 2)) + jnp.sum(
-        split_full * split_full, axis=(1, 2)
-    )
-    squares = lax.psum(matrix_squares, ("dp", "tp")) + vector_squares
+    lanes = lax.broadcasted_iota(jnp.int32, (slot_count, 8, 128), 2)
+    live_tile = jnp.where((lanes == owned_layer[:, None, None]) & live[:, None, None], 1.0, 0.0)
+    reduced, vector_sum, square_tile, block_far, grad_far = reduce_gradients(
+        sizes, layer_count, slot_count, target, jnp.concatenate(vectors), live_tile, streams[-1], grad
+    )
+
+    def both(near, far):
+        low = jnp.where(tp_rank == 0, near, far)
+        high = jnp.where(tp_rank == 0, far, near)
+        return jnp.concatenate([low, high], axis=0)
+
+    block_output = both(streams[-1], block_far)
+    input_grad = both(grad, grad_far)
+    reduced = reduced.reshape(slot_count, side, side)
+    vector_sum = vector_sum.reshape(layer_count, -1, width)
+    shared_sum = vector_sum[:, :6]
+    split_full = vector_sum[:, 6 : 8 + ratio]
+    split_sum = lax.dynamic_slice_in_dim(split_full, tp_rank * half, half, axis=2)
+    squares = square_tile[0, :layer_count]
     layer_norms = jnp.sqrt(squares)
     global_norm = jnp.sqrt(jnp.sum(squares))
     factor = CLIP_NORM / jnp.maximum(global_norm, CLIP_NORM)

time: 972 us -> 544 us (0.56)
  waiting for transfers between devices: 619 us -> 0 us
  Pallas kernels: 245 us -> 498 us
  blocking collectives: 42.6 us -> 0 us
  between operations: 16.4 us -> 2.94 us
    reduce_scatter x2 -> x0, waiting for transfers between devices: 260 us -> none  [the longest x1 222 us: shards(): lax.psum_scatter(reduced, 'dp', scatter_dimension=0, tiled=True).astype(F32)]
    pallas_call x0 -> x2, Pallas kernels: none -> 253 us  [the longest x1 138 us: reduce_gradients(): pl.pallas_call(functools.partial(reduce_kernel, sizes, parts, plan, layer...]
    all_gather x4 -> x0, waiting for transfers between devices: 231 us -> none  [the longest x1 171 us: shards(): lax.all_gather(master_slots[:, 0].astype(BF16), 'dp', axis=0, tiled=True)]
    psum x1 -> x0, waiting for transfers between devices: 126 us -> none  [shards(): vector_sum = lax.psum(jnp.stack(vectors), ('dp', 'tp'))]
    psum x1 -> x0, blocking collectives: 40.8 us -> none  [shards(): squares = lax.psum(matrix_squares, ('dp', 'tp')) + vector_squares]
    unnamed x36 -> x25, local copies, waits for them, and re-layouts: 28.6 us -> 18.5 us
  transfers between devices with their start and end apart: 7 -> 0, of which waited for: 7 -> 0; matrix products, arithmetic and copies ran while one was open for 2% -> 0% of each run, Pallas kernels for 0% -> 0%
where the time goes in v2:
time: 544 us; the launch traced here: 536 us
  Pallas kernels  498 us (92%)
  local copies, waits for them, and re-layouts  21.7 us (4%)
  other arithmetic  12.8 us (2%)
    pallas_call x1, Pallas kernels, reduce_gradients(): pl.pallas_call(functools.partial(reduce_kernel, sizes, parts, plan, layer...  138 us
    pallas_call x1, Pallas kernels, gather_weights(): pl.pallas_call(functools.partial(gather_kernel, sizes, parts, plan), in_s...  115 us
    pallas_call x2, Pallas kernels, backward_layer(): pl.pallas_call(functools.partial(backward_kernel, layer, seq, rows, keys,...  81.2 us
    pallas_call x2, Pallas kernels, layer_gradients(): pl.pallas_call(functools.partial(gradient_kernel, pieces, ratio), grid_sp...  73.2 us
    pallas_call x2, Pallas kernels, forward_layer(): pl.pallas_call(functools.partial(forward_kernel, layer, seq, rows, keys),...  71 us
    pallas_call x1, Pallas kernels, adam(): pl.pallas_call(adam_kernel, grid=(count,), in_specs=[smem, smem, pl.Block...  20.1 us
    unnamed x25, local copies, waits for them, and re-layouts  18.5 us

profile of v2, /device:TPU:0, one launch (start us, length us, event | category | flops | bytes accessed | tf_op | source)
XLA Modules:
  0.0 535.6 jit_solution(5196628935736759517)
XLA Ops:
  0.6 0.9 convert_reduce_fusion
  1.6 0.7 and_select_fusion
  2.2 0.6 pad_add_fusion.meta
  2.8 1.3 copy.40.split_ref
  4.1 115.1 %gather_weights.1 = (bf16[2,18432,384]{2,1,0:T(8,128)(2,1)}, f32[2,2,6,384]{3,2,1,0:T(8,128)}) custom-call(f32[1152,384]{1,0:T(8,128)} %bitcast.43, f32[2,6,384]{2,1,0:T(8,128)} %copy.40.split_ref), custom_call_target="tpu_custom_call" | custom-call | tf_op jit(solution)/shard_map/gather_weights/pallas_call | solution.py:581
  119.3 0.8 slice_bitcast_fusion
  120.0 0.6 fusion.3
  120.7 0.9 fusion.12
  121.5 0.6 copy_bitcast_fusion
  122.2 3.6 copy.41.x_ref
  125.8 35.1 %forward0.1 = (bf16[4,208,768]{2,1,0:T(8,128)(2,1)}, bf16[4,208,768]{2,1,0:T(8,128)(2,1)}, bf16[4,256,768]{2,1,0:T(8,128)(2,1)}, bf16[4,256,768]{2,1,0:T(8,128)(...) custom-call(s32[49]{0:T(128)} %pad_add_fusion.meta, ...), custom_call_target="tpu_custom_call" | custom-call | tf_op jit(solution)/shard_map/forward0/pallas_call | solution.py:893
  160.9 35.9 %forward1.1 = (bf16[4,208,768]{2,1,0:T(8,128)(2,1)}, bf16[4,208,768]{2,1,0:T(8,128)(2,1)}, bf16[4,256,768]{2,1,0:T(8,128)(2,1)}, bf16[4,256,768]{2,1,0:T(8,128)(...) custom-call(s32[49]{0:T(128)} %pad_add_fusion.meta, ...), custom_call_target="tpu_custom_call" | custom-call | tf_op jit(solution)/shard_map/forward1/pallas_call | solution.py:893
  196.8 6.1 %copy.43.dy_ref = f32[8,197,768]{2,1,0:T(8,128)} copy(f32[8,197,768]{2,0,1:T(8,128)} %param.16) | data formatting | bytes 9682944 | tf_op args[1]
  202.9 40.4 %backward1.1 = (bf16[4,208,768]{2,1,0:T(8,128)(2,1)}, bf16[4,208,3072]{2,1,0:T(8,128)(2,1)}, bf16[4,208,768]{2,1,0:T(8,128)(2,1)}, bf16[4,208,2304]{2,1,0:T(8,12...) custom-call(s32[49]{0:T(128)} %pad_add_fusion.meta, f32[8,197,768]{2,1,0:T(8,128)} %copy.43.dy_ref, ...), custom_call_target="tpu_custom_call" | custom-call | tf_op jit(solution)/shard_map/backward1/pallas_call | solution.py:940
  243.3 0.0 copy-start.5
  243.3 40.8 %backward0.1 = (bf16[4,208,768]{2,1,0:T(8,128)(2,1)}, bf16[4,208,3072]{2,1,0:T(8,128)(2,1)}, bf16[4,208,768]{2,1,0:T(8,128)(2,1)}, bf16[4,208,2304]{2,1,0:T(8,12...) custom-call(s32[49]{0:T(128)} %pad_add_fusion.meta, f32[4,208,768]{2,1,0:T(8,128)} %get-tuple-element.68.dy_ref, ...), custom_call_target="tpu_custom_call" | custom-call | tf_op jit(solution)/shard_map/backward0/pallas_call | solution.py:940
  284.1 0.0 copy-done.5
  284.1 1.4 pad_maximum_fusion.2.vec_ref
  285.6 36.6 %gradients1.1.rest_0_ = bf16[2,48,384,384]{3,2,1,0:T(8,128)(2,1)} custom-call(s32[49]{0:T(128)} %pad_add_fusion.meta, bf16[832,768]{1,0:T(8,128)(2,1)} %bitcast.56, bf16[832,2304]{1,0:T(8,128)(2,1)} %bitcast.48, bf16[832,768]{1,0:T(8,128)(2,1)} %bitcast.57, bf16[832,768]{1,0:T(8,128)(2,1)} %bitcast.60, bf16[832,768]{1,0:T(8,128)(2,1)} %bitcast.58, ...), custom_call_target="tpu_custom_call" | custom-call | tf_op jit(solution)/shard_map/gradients1/pallas_call | solution.py:990
  322.1 36.6 %gradients0.1 = bf16[2,48,384,384]{3,2,1,0:T(8,128)(2,1)} custom-call(s32[49]{0:T(128)} %pad_add_fusion.meta, bf16[832,768]{1,0:T(8,128)(2,1)} %bitcast.51, bf16[832,2304]{1,0:T(8,128)(2,1)} %bitcast.49, bf16[832,768]{1,0:T(8,128)(2,1)} %bitcast.52, bf16[832,768]{1,0:T(8,128)(2,1)} %bitcast.55, ...), custom_call_target="tpu_custom_call", output_to_operand_aliasing={{}: (9, {})} | custom-call | tf_op jit(solution)/shard_map/gradients0/pallas_call | solution.py:990
  358.8 0.2 fusion.8
  359.0 0.2 compare_reduce_fusion
  359.1 0.7 fusion.7.live_ref
  359.8 0.0 copy-start.4
  359.8 0.0 copy-start.8
  359.8 0.0 copy-start.9
  359.8 0.0 copy-start.3
  359.8 0.0 copy-start.6
  359.8 0.0 copy-start.7
  359.9 137.5 %reduce_gradients.1 = (f32[1152,384]{1,0:T(8,128)}, f32[32,768]{1,0:T(8,128)}, f32[8,128]{1,0:T(8,128)}, f32[4,197,768]{2,1,0:T(8,128)}, f32[4,197,768]{2,1,0:T(8,128)}) custom-call(bf16[2,18432,384]{2,1,0:T(8,128)(2,1)} %bitcast.42, f32[32,768]{1,0:T(8,128)} %pad_maximum_fusion.2.vec_ref, f32[3,8,128]{2,1,0:T(8,128)} %fusion.7.live_ref, ...), custom_call_target="tpu_custom_call" | custom-call | tf_op jit(solution)/shard_map/reduce_gradients/pallas_call | solution.py:794
  497.4 0.9 fusion.11
  498.3 1.8 sqrt_bitcast_fusion
  500.8 0.0 copy-done.4
  500.8 0.0 copy-done.8
  500.8 0.0 copy-done.9
  500.9 0.7 multiply_subtract_fusion.1
  501.5 0.0 copy-done.3
  501.5 0.0 copy-done.6
  501.5 0.0 copy-done.7
  501.5 0.8 multiply_subtract_fusion
  502.3 0.6 pad_maximum_fusion.4.factor_ref
  502.9 0.5 convert_element_type.7.live_ref
  503.4 0.0 copy-start.1
  503.4 20.1 %adam.1 = (f32[3,1,384,384]{3,2,1,0:T(8,128)}, f32[3,1,384,384]{3,2,1,0:T(8,128)}, f32[3,1,384,384]{3,2,1,0:T(8,128)}) custom-call(s32[3]{0:T(128)} %convert_element_type.7.live_ref, f32[2]{0:T(128)} %pad_maximum_fusion.4.factor_ref, f32[3,384,384]{2,1,0:T(8,128)} %bitcast.50, f32[3,1,384,384]{3,2,1,0:T(8,128)} %w_ref.1, f32[3,1,384,384]{3,2,1,0:T(8,128)} %l_ref.1, ...), custom_call_target="tpu_custom_call" | custom-call | tf_op jit(solution)/shard_map/adam/pallas_call | solution.py:1005
  523.5 0.0 copy-done.1
  523.5 2.1 broadcast_select_fusion.1
  525.6 0.4 pad_maximum_fusion.1
  526.0 0.0 copy-start
  526.0 0.0 copy-start.2
  526.0 3.7 copy.48
  529.7 0.0 copy-done
  529.7 0.0 copy-done.2
  529.7 0.4 broadcast_select_fusion.3
  530.1 0.4 pad_maximum_fusion
  530.5 3.7 copy.47
  (2 shorter events, 0.0 us)
Async XLA Ops:
  243.3 40.8 %copy-start.5 = (f32[16,768]{1,0:T(8,128)S(1)}, f32[16,768]{1,0:T(8,128)}, u32[]{:S(2)}) copy-start(f32[16,768]{1,0:T(8,128)} %get-tuple-element.91) | copy-start | bytes 147460
  359.8 141.0 %copy-start.4 = (f32[2,6,384]{2,0,1:T(2,128)S(1)}, f32[2,6,384]{2,0,1:T(2,128)}, u32[]{:S(2)}) copy-start(f32[2,6,384]{2,0,1:T(2,128)} %param.27) | copy-start | bytes 55300
  359.8 141.0 %copy-start.8 = (f32[2,6,384]{2,0,1:T(2,128)S(1)}, f32[2,6,384]{2,0,1:T(2,128)}, u32[]{:S(2)}) copy-start(f32[2,6,384]{2,0,1:T(2,128)} %param.28) | copy-start | bytes 55300
  359.8 141.0 %copy-start.9 = (f32[2,6,384]{2,0,1:T(2,128)S(1)}, f32[2,6,384]{2,0,1:T(2,128)}, u32[]{:S(2)}) copy-start(f32[2,6,384]{2,0,1:T(2,128)} %param.29) | copy-start | bytes 55300
  359.8 141.7 %copy-start.3 = (f32[2,6,768]{2,0,1:T(2,128)S(1)}, f32[2,6,768]{2,0,1:T(2,128)}, u32[]{:S(2)}) copy-start(f32[2,6,768]{2,0,1:T(2,128)} %param.24) | copy-start | bytes 110596
  359.8 141.7 %copy-start.6 = (f32[2,6,768]{2,0,1:T(2,128)S(1)}, f32[2,6,768]{2,0,1:T(2,128)}, u32[]{:S(2)}) copy-start(f32[2,6,768]{2,0,1:T(2,128)} %param.25) | copy-start | bytes 110596
  359.8 141.7 %copy-start.7 = (f32[2,6,768]{2,0,1:T(2,128)S(1)}, f32[2,6,768]{2,0,1:T(2,128)}, u32[]{:S(2)}) copy-start(f32[2,6,768]{2,0,1:T(2,128)} %param.26) | copy-start | bytes 110596
  503.4 20.1 %copy-start.1 = (f32[4,197,768]{2,1,0:T(8,128)S(1)}, f32[4,197,768]{2,1,0:T(8,128)}, u32[]{:S(2)}) copy-start(f32[4,197,768]{2,1,0:T(8,128)} %get-tuple-element.92.grad_ref) | copy-start | bytes 7262212
  526.0 3.7 copy-start
  526.0 3.7 copy-start.2

commit v3 on v2

v3 whole, which is shorter than its diff:
```python
import functools
import math

import jax
import jax.numpy as jnp
from jax import lax
from jax.experimental import pallas as pl
from jax.experimental.pallas import tpu as pltpu
from jax.sharding import PartitionSpec as P

DH = 64
GROUP = 4
LANES = GROUP * DH
CLIP_NORM = 1.0
MOMENT_DECAY = 0.5
CORRECTION = 0.9375
ADAM_EPSILON = 1e-08
WEIGHT_DECAY = 0.05
LAYER_EPSILON = 1e-06
VECTOR_RATE = 0.2
VMEM_LIMIT = 60 * 1024 * 1024
F32 = jnp.float32
BF16 = jnp.bfloat16


def nn(a, b):
    return lax.dot_general(a, b, (((1,), (0,)), ((), ())), preferred_element_type=F32)


def nt(a, b):
    return lax.dot_general(a, b, (((1,), (1,)), ((), ())), preferred_element_type=F32)


def tn(a, b):
    return lax.dot_general(a, b, (((0,), (0,)), ((), ())), preferred_element_type=F32)


def round_up(number, step):
    return (number + step - 1) // step * step


def positions(owners, slot_count):
    block_ids = jnp.arange(owners.shape[0], dtype=jnp.int32)
    same_owner = owners[None, :] == owners[:, None]
    earlier = block_ids[None, :] < block_ids[:, None]
    ranking = jnp.sum((same_owner & earlier).astype(jnp.int32), axis=1)
    return owners * slot_count + ranking


def normalized(v):
    center = jnp.mean(v, axis=-1, keepdims=True)
    spread = v - center
    second = jnp.mean(spread * spread, axis=-1, keepdims=True)
    inverse = lax.rsqrt(second + LAYER_EPSILON)
    return spread * inverse, inverse


def norm_back(grad, unit, inverse, gain):
    scaled = grad * gain
    first = jnp.mean(scaled, axis=-1, keepdims=True)
    second = jnp.mean(scaled * unit, axis=-1, keepdims=True)
    return inverse * (scaled - first - unit * second)


def gelu_pair(u):
    bell = jnp.exp(u * u * -0.5)
    mass = 0.5 + 0.5 * lax.erf(u * math.sqrt(0.5))
    return u * mass, mass + u * bell * (1.0 / math.sqrt(2.0 * math.pi))


def weight_copies(meta, layer, blocks, wp, wo, wu, wd, sems):
    side = blocks.shape[-1]
    width = wo.shape[0]
    pieces = width // side
    ratio = wd.shape[0] // width
    per_layer = pieces * (4 + 2 * ratio)
    base = layer * per_layer
    jobs = [[], [], [], []]

    def add(kind, target, b, row, col):
        for t in range(blocks.shape[0]):
            r, c = row(t), col(t)
            jobs[kind].append(
                pltpu.make_async_copy(
                    blocks.at[t, meta[base + b]],
                    target.at[pl.ds(r, side), pl.ds(c, side)],
                    sems.at[kind],
                )
            )

    for r in range(pieces):
        for p in range(3):
            add(0, wp, r * 3 + p, lambda t: r * side, lambda t: p * width + t * side)
    for c in range(pieces):
        add(1, wo, 3 * pieces + c, lambda t: t * side, lambda t: c * side)
    for r in range(pieces):
        for j in range(ratio):
            add(
                2, wu, 4 * pieces + r * ratio + j, lambda t: r * side, lambda t: j * width + t * side
            )
    for j in range(ratio):
        for c in range(pieces):
            add(
                3,
                wd,
                (4 + ratio) * pieces + j * pieces + c,
                lambda t: j * width + t * side,
                lambda t: c * side,
            )
    return jobs


def head_masks():
    lane = lax.broadcasted_iota(jnp.int32, (1, LANES), 1)
    return [(lane // DH) == h for h in range(GROUP)]


def spread_heads(masks, value):
    zero = jnp.zeros((), value.dtype)
    return jnp.concatenate([jnp.where(m, value, zero) for m in masks], axis=0)


def padded_rows(ref, seq, rows, scratch):
    tail = seq // 16 * 16
    scratch[tail:rows, :] = jnp.zeros((rows - tail, ref.shape[2]), F32)
    scratch[0:seq, :] = ref[0].astype(F32)


SAVED = ("a", "mixed", "c", "act", "dyr", "du", "dhr", "dqkv")


def layers_kernel(layer_count, seq, rows, keys, meta, x_ref, dy_ref, hits_ref, shared_ref, split_ref, blocks, *rest):
    outs = rest[: 8 * layer_count]
    y_ref, dx_ref, vec_ref = rest[8 * layer_count : 8 * layer_count + 3]
    rest = rest[8 * layer_count + 3 :]
    saves = rest[: 8 * layer_count]
    rest = rest[8 * layer_count :]
    weights = [rest[4 * n : 4 * n + 4] for n in range(layer_count)]
    rest = rest[4 * layer_count :]
    holds = [rest[7 * n : 7 * n + 7] for n in range(layer_count)]
    seed_ref, save_sems, weight_sems = rest[7 * layer_count :]
    width = x_ref.shape[2]
    ratio = split_ref.shape[1] - 2
    groups = width // LANES
    scale = 1.0 / math.sqrt(DH)
    step = pl.program_id(0)
    zero = jnp.zeros((), BF16)
    masks = head_masks()

    class Kept:
        def __init__(self, layer, name):
            n = layer * 8 + SAVED.index(name)
            self.out, self.ref, self.sem = outs[n], saves[n], save_sems.at[n]

        def copy(self, i):
            return pltpu.make_async_copy(self.ref, self.out.at[i], self.sem)

        def free(self):
            @pl.when(step > 0)
            def _():
                self.copy(step - 1).wait()

        def send(self):
            self.copy(step).start()

    def keep(layer, name, value):
        kept = Kept(layer, name)
        kept.free()
        kept.ref[...] = value
        kept.send()

    jobs = [
        weight_copies(meta, n, blocks, *weights[n], weight_sems.at[n]) for n in range(layer_count)
    ]

    def start(pairs):
        @pl.when(step == 0)
        def _():
            for n, kind in pairs:
                for job in jobs[n][kind]:
                    job.start()

    def ready(layer, kind):
        @pl.when(step == 0)
        def _():
            target = weights[layer][kind]
            pltpu.make_async_copy(target, target, weight_sems.at[layer, kind]).wait()

    start([(0, 0), (0, 1)])

    @pl.when(step == 0)
    def _():
        vec_ref[...] = jnp.zeros_like(vec_ref)
        for hold in holds:
            for ref in (hold[3], hold[4]):
                ref[rows:keys, :] = jnp.zeros((keys - rows, width), BF16)

    padded_rows(x_ref, seq, rows, holds[0][0])
    real = lax.broadcasted_iota(jnp.int32, (1, keys), 1) < seq
    for n in range(layer_count):
        xs, hs, qs, ks, vs, ps, ss = holds[n]
        wp, wo, wu, wd = weights[n]
        unit, _ = normalized(xs[...])
        a = (unit * shared_ref[n, 0:1, :] + shared_ref[n, 1:2, :]).astype(BF16)
        keep(n, "a", a)
        ready(n, 0)
        if n == 0:
            start([(0, 2), (0, 3)])
        qs[...] = ((nn(a, wp[:, 0:width]) + split_ref[n, 0:1, :]) * scale).astype(BF16)
        ks[0:rows, :] = nn(a, wp[:, width : 2 * width]).astype(BF16)
        vs[0:rows, :] = (nn(a, wp[:, 2 * width :]) + split_ref[n, 1:2, :]).astype(BF16)
        mixed = Kept(n, "mixed")
        mixed.free()
        for g in range(groups):
            cols = slice(g * LANES, (g + 1) * LANES)
            scores = nt(spread_heads(masks, qs[:, cols]), ks[:, cols])
            scores = jnp.where(real, scores, -1e30)
            top = jnp.max(scores, axis=-1, keepdims=True)
            power = jnp.exp(scores - top)
            total = jnp.sum(power, axis=-1, keepdims=True)
            probs = (power * (1.0 / total)).astype(BF16)
            ps[g * GROUP * rows : (g + 1) * GROUP * rows, :] = probs
            v4 = vs[:, cols]
            mix = None
            for h in range(GROUP):
                part = nn(probs[h * rows : (h + 1) * rows, :], jnp.where(masks[h], v4, zero))
                mix = part if mix is None else mix + part
            mixed.ref[:, cols] = mix.astype(BF16)
        mixed.send()
        ready(n, 1)
        h = xs[...] + nn(mixed.ref[...], wo[...]) + shared_ref[n, 2:3, :]
        hs[...] = h
        unit, _ = normalized(h)
        c = (unit * shared_ref[n, 3:4, :] + shared_ref[n, 4:5, :]).astype(BF16)
        keep(n, "c", c)
        ready(n, 2)
        ready(n, 3)
        if n == 0:
            start([(m, kind) for m in range(1, layer_count) for kind in range(4)])
        y = h + shared_ref[n, 5:6, :]
        active = Kept(n, "act")
        active.free()
        for j in range(ratio):
            cols = slice(j * width, (j + 1) * width)
            u = nn(c, wu[:, cols]) + split_ref[n, 2 + j : 3 + j, :]
            act, slope = gelu_pair(u)
            act = act.astype(BF16)
            active.ref[:, cols] = act
            ss[:, cols] = slope.astype(BF16)
            y = y + nn(act, wd[cols, :])
        active.send()
        if n + 1 < layer_count:
            holds[n + 1][0][...] = y
        else:
            y_ref[0] = y[0:seq, :]

    wanted = lax.broadcasted_iota(jnp.int32, (rows, 1), 0)
    hit = jnp.max(jnp.where(hits_ref[0] + 1 == wanted, 1.0, 0.0), axis=-1, keepdims=True)
    padded_rows(dy_ref, seq, rows, seed_ref)
    dy = seed_ref[...] * hit
    for n in reversed(range(layer_count)):
        xs, hs, qs, ks, vs, ps, ss = holds[n]
        wp, wo, wu, wd = weights[n]

        def collect(row, value):
            vec_ref[n, row : row + 1, :] += jnp.sum(value, axis=0, keepdims=True)

        collect(5, dy)
        dyr = dy.astype(BF16)
        keep(n, "dyr", dyr)
        hidden = Kept(n, "du")
        hidden.free()
        dc = None
        for j in range(ratio):
            cols = slice(j * width, (j + 1) * width)
            du = (nt(dyr, wd[cols, :]) * ss[:, cols].astype(F32)).astype(BF16)
            hidden.ref[:, cols] = du
            collect(8 + j, du.astype(F32))
            part = nt(du, wu[:, cols])
            dc = part if dc is None else dc + part
        hidden.send()
        unit, inverse = normalized(hs[...])
        collect(3, dc * unit)
        collect(4, dc)
        dh = dy + norm_back(dc, unit, inverse, shared_ref[n, 3:4, :])
        collect(2, dh)
        dhr = dh.astype(BF16)
        keep(n, "dhr", dhr)
        dmixed = nt(dhr, wo[...]).astype(BF16)
        back = Kept(n, "dqkv")
        back.free()
        for g in range(groups):
            cols = slice(g * LANES, (g + 1) * LANES)
            dm = spread_heads(masks, dmixed[:, cols])
            probs = ps[g * GROUP * rows : (g + 1) * GROUP * rows, :]
            k4 = ks[:, cols]
            dprobs = nt(dm, vs[:, cols])
            wide = probs.astype(F32)
            both = wide * dprobs
            ds = (both - wide * jnp.sum(both, axis=-1, keepdims=True)).astype(BF16)
            dv = tn(probs, dm)[0:rows, :].astype(BF16)
            dk = tn(ds, spread_heads(masks, qs[:, cols]))[0:rows, :].astype(BF16)
            dq = None
            for h in range(GROUP):
                part = nn(ds[h * rows : (h + 1) * rows, :], jnp.where(masks[h], k4, zero))
                dq = part if dq is None else dq + part
            back.ref[:, cols] = (dq.astype(BF16).astype(F32) * scale).astype(BF16)
            back.ref[:, width + g * LANES : width + (g + 1) * LANES] = dk
            back.ref[:, 2 * width + g * LANES : 2 * width + (g + 1) * LANES] = dv
        back.send()
        dqkv = back.ref[...]
        collect(6, dqkv[:, 0:width].astype(F32))
        collect(7, dqkv[:, 2 * width :].astype(F32))
        da = nt(dqkv, wp[...])
        unit, inverse = normalized(xs[...])
        collect(0, da * unit)
        collect(1, da)
        dy = dh + norm_back(da, unit, inverse, shared_ref[n, 0:1, :])
    dx_ref[0] = dy[0:seq, :]

    @pl.when(step == pl.num_programs(0) - 1)
    def _():
        for n in range(layer_count):
            for name in SAVED:
                Kept(n, name).copy(step).wait()


def run_layers(count, seq, rows, keys, meta, place, stream, seed, hits, shared, split, blocks):
    layer_count, _, width = shared.shape
    ratio = split.shape[1] - 2
    heads = width // DH
    sd = jax.ShapeDtypeStruct
    widths = [width, width, width, ratio * width, width, ratio * width, width, 3 * width] * layer_count
    anyspace = pl.BlockSpec(memory_space=pl.ANY)
    outs = [sd((count, rows, w), BF16) for w in widths]
    outs += [sd((count, seq, width), F32)] * 2 + [sd((layer_count, 16, width), F32)]
    image = pl.BlockSpec((1, seq, width), lambda i, meta: (i, 0, 0))

    def shifted(shape):
        return pl.BlockSpec((1,) + tuple(shape[1:]), lambda i, meta: (meta[place] * count + i, 0, 0))

    def whole(shape):
        return pl.BlockSpec(tuple(shape), lambda i, meta: (0,) * len(shape))

    vmem = pltpu.VMEM
    scratch = [vmem((rows, w), BF16) for w in widths]
    scratch += [
        vmem((width, 3 * width), BF16),
        vmem((width, width), BF16),
        vmem((width, ratio * width), BF16),
        vmem((ratio * width, width), BF16),
    ] * layer_count
    scratch += [
        vmem((rows, width), F32),
        vmem((rows, width), F32),
        vmem((rows, width), BF16),
        vmem((keys, width), BF16),
        vmem((keys, width), BF16),
        vmem((heads * rows, keys), BF16),
        vmem((rows, ratio * width), BF16),
    ] * layer_count
    scratch += [
        vmem((rows, width), F32),
        pltpu.SemaphoreType.DMA((8 * layer_count,)),
        pltpu.SemaphoreType.DMA((layer_count, 4)),
    ]
    grid = pltpu.PrefetchScalarGridSpec(
        num_scalar_prefetch=1,
        grid=(count,),
        in_specs=[
            shifted(stream.shape),
            shifted(seed.shape),
            shifted(hits.shape),
            whole(shared.shape),
            whole(split.shape),
            anyspace,
        ],
        out_specs=[anyspace] * len(widths) + [image, image, whole((layer_count, 16, width))],
        scratch_shapes=scratch,
    )
    res = pl.pallas_call(
        functools.partial(layers_kernel, layer_count, seq, rows, keys),
        grid_spec=grid,
        out_shape=outs,
        compiler_params=params(),
        name="layers",
    )(meta, stream, seed, hits, shared, split, blocks)
    kept = [dict(zip(SAVED, res[8 * n : 8 * n + 8])) for n in range(layer_count)]
    return kept, res[8 * layer_count], res[8 * layer_count + 1], res[8 * layer_count + 2]


def gradient_kernel(
    layer, pieces, ratio, meta, a_ref, dqkv_ref, mixed_ref, dhr_ref, c_ref, du_ref, act_ref,
    dyr_ref, *rest,
):
    out_ref, turned, stage, sems = rest[-4:]
    side = out_ref.shape[-1]
    shares = out_ref.shape[0]
    step = pl.program_id(0)
    last = pl.num_programs(0) - 1
    start_up = 4
    start_down = 4 + ratio
    base = layer * pieces * (4 + 2 * ratio)
    slot = step % 2

    def saves(buffer, place):
        out = []
        for i in range(pieces):
            for j in range(pieces):
                block, share = place(i, j)
                out.append(
                    pltpu.make_async_copy(
                        stage.at[buffer, pl.ds(i * side, side), pl.ds(j * side, side)],
                        out_ref.at[share, meta[base + block]],
                        sems.at[buffer],
                    )
                )
        return out

    def drain(buffer):
        pltpu.make_async_copy(stage.at[buffer], stage.at[buffer], sems.at[buffer]).wait()

    @pl.when(step >= 2)
    def _():
        drain(slot)

    def work(lhs_ref, rhs_ref, first, place):
        if first is None:
            lhs = lhs_ref[...].T
        else:

            @pl.when(first)
            def _():
                turned[...] = lhs_ref[...].T

            lhs = turned[...]
        stage[slot] = nn(lhs, rhs_ref[...]).astype(BF16)
        for save in saves(slot, place):
            save.start()

    @pl.when(step < 3)
    def _():
        work(a_ref, dqkv_ref, step == 0, lambda i, j: (i * 3 + step, j))

    @pl.when(step == 3)
    def _():
        work(mixed_ref, dhr_ref, None, lambda i, j: (3 * pieces + j, i))

    @pl.when((step >= start_up) & (step < start_down))
    def _():
        work(
            c_ref, du_ref, step == start_up,
            lambda i, j: (4 * pieces + i * ratio + step - start_up, j),
        )

    @pl.when(step >= start_down)
    def _():
        work(
            act_ref, dyr_ref, None,
            lambda i, j: ((4 + ratio) * pieces + (step - start_down) * pieces + j, i),
        )

    @pl.when(step == last)
    def _():
        drain(1 - slot)
        drain(slot)


def adam_kernel(live_ref, factor_ref, g_ref, w_ref, l_ref, r_ref, m_ref, s_ref, w_out, m_out, s_out):
    step_rate = factor_ref[1]
    slot = pl.program_id(0)
    alive = live_ref[slot] > 0
    weight = w_ref[0, 0]
    left = l_ref[0, 0].astype(BF16)
    right = r_ref[0, 0].astype(BF16)
    turned = nn(tn(left, g_ref[0].astype(BF16)).astype(BF16), right) * factor_ref[0]
    first = MOMENT_DECAY * m_ref[0, 0] + (1.0 - MOMENT_DECAY) * turned
    second = MOMENT_DECAY * s_ref[0, 0] + (1.0 - MOMENT_DECAY) * turned * turned
    stepped = first / CORRECTION / (jnp.sqrt(second / CORRECTION) + ADAM_EPSILON)
    back = nt(nn(left, stepped.astype(BF16)).astype(BF16), right)
    w_out[0, 0] = jnp.where(alive, weight - step_rate * (back + WEIGHT_DECAY * weight), weight)
    m_out[0, 0] = jnp.where(alive, first, m_ref[0, 0])
    s_out[0, 0] = jnp.where(alive, second, s_ref[0, 0])


def line_sizes(dp_count):
    if dp_count == 16:
        return (4, 2, 2)
    if dp_count == 64:
        return (4, 4, 4)
    return (dp_count, 1, 1)


def part_table(sizes, total_rows):
    step = 16
    if sizes[0] > sizes[1]:
        large = int(total_rows * 0.39) // step * step
        lengths = (total_rows - 2 * large, large, large)
        orders = ((2, 1, 0), (0, 1, 2), (0, 2, 1))
    else:
        small = total_rows // 3 // step * step
        lengths = (total_rows - 2 * small, small, small)
        orders = ((2, 1, 0), (0, 2, 1), (1, 0, 2))
    offsets = (0, lengths[0], lengths[0] + lengths[1])
    return [(orders[i], offsets[i], lengths[i]) for i in range(3)]


def gather_plan(sizes, parts):
    ready, moves, plan = {}, [], []
    free = [0.0] * 3
    for p, (order, _, _) in enumerate(parts):
        n = [sizes[d] for d in order]
        ready[(p, (0, 0, 0))] = 0.0
        for a in range(n[0]):
            if a + 1 < n[0]:
                moves.append((p, 0, (a, 0, 0)))
            for b in range(n[1]):
                if b + 1 < n[1]:
                    moves.append((p, 1, (a, b, 0)))
                for c in range(n[2] - 1):
                    moves.append((p, 2, (a, b, c)))
    while moves:
        choices = []
        for move in moves:
            p, stage, unit = move
            if (p, unit) in ready:
                start = max(ready[(p, unit)], free[parts[p][0][stage]])
                choices.append((start, stage, p, unit))
        start, stage, p, unit = min(choices)
        end = start + parts[p][2]
        free[parts[p][0][stage]] = end
        ready[(p, one_on(unit, stage))] = end + 60.0
        plan.append((p, stage, unit))
        moves.remove((p, stage, unit))
    return plan


def one_on(unit, stage):
    return tuple(v + (1 if i == stage else 0) for i, v in enumerate(unit))


class Place:
    def __init__(self, sizes):
        self.sizes = sizes
        self.dp = lax.axis_index("dp")
        self.tp = lax.axis_index("tp")
        nz, ny, nx = sizes
        self.at = (self.dp // (ny * nx), self.dp // nx % ny, self.dp % nx)

    def shifted(self, offsets):
        nz, ny, nx = self.sizes
        z, y, x = [
            lax.rem(self.at[d] + (offsets[d] + self.sizes[d]) % self.sizes[d], self.sizes[d])
            for d in range(3)
        ]
        return (z * ny + y) * nx + x

    def along(self, dim, step):
        return self.shifted(tuple(step if d == dim else 0 for d in range(3)))

    def behind(self, order, unit, sign):
        offsets = [0, 0, 0]
        for d, v in zip(order, unit):
            offsets[d] = sign * v
        return self.shifted(tuple(offsets))


def greet(place):
    barrier = pltpu.get_barrier_semaphore()
    number = 1
    pl.semaphore_signal(
        barrier, inc=1, device_id=(place.dp, 1 - place.tp), device_id_type=pl.DeviceIdType.MESH
    )
    for d in range(3):
        for step in range(1, place.sizes[d]):
            number += 1
            pl.semaphore_signal(
                barrier,
                inc=1,
                device_id=(place.along(d, step), place.tp),
                device_id_type=pl.DeviceIdType.MESH,
            )
    pl.semaphore_wait(barrier, number)


def remote(src, dst, send, recv, dp, tp):
    return pltpu.make_async_remote_copy(
        src_ref=src,
        dst_ref=dst,
        send_sem=send,
        recv_sem=recv,
        device_id=(dp, tp),
        device_id_type=pl.DeviceIdType.MESH,
    )


def gather_kernel(
    sizes, parts, plan, master_ref, split_ref, out_ref, split_out,
    own_ref, send, recv, over_send, over_recv, here,
):
    place = Place(sizes)
    dp, tp = place.dp, place.tp
    rows = own_ref.shape[0]
    dims = [n for n in sizes]
    numbers = {}
    for p, (order, _, _) in enumerate(parts):
        for a in range(dims[order[0]]):
            for b in range(dims[order[1]]):
                for c in range(dims[order[2]]):
                    numbers[(p, (a, b, c))] = len(numbers)

    def region(p, unit, share):
        order, start, length = parts[p]
        owner = place.behind(order, unit, -1)
        return out_ref.at[share, pl.ds(pl.multiple_of(owner * rows + start, 16), length)]

    def source(p, unit):
        if unit == (0, 0, 0):
            return own_ref.at[pl.ds(parts[p][1], parts[p][2])]
        return region(p, unit, tp)

    def pass_over(p, unit):
        n = numbers[(p, unit)]
        return remote(
            source(p, unit), region(p, unit, tp), over_send.at[n], over_recv.at[n], dp, 1 - tp
        )

    def taken_over(p, unit):
        n = numbers[(p, unit)]
        piece = region(p, unit, 1 - tp)
        return remote(piece, piece, over_send.at[n], over_recv.at[n], dp, 1 - tp)

    def arriving(p, unit):
        n = numbers[(p, unit)]
        piece = region(p, unit, tp)
        return remote(piece, piece, send.at[n], recv.at[n], dp, 1 - tp)

    def sending(p, stage, unit):
        n = numbers[(p, one_on(unit, stage))]
        target = place.along(parts[p][0][stage], 1)
        return remote(source(p, unit), region(p, unit, tp), send.at[n], recv.at[n], target, tp)

    own_ref[...] = master_ref[...].astype(BF16)
    greet(place)
    started = []
    arrived = set()

    def need(p, unit):
        if (p, unit) in arrived:
            return
        arrived.add((p, unit))
        if unit != (0, 0, 0):
            arriving(p, unit).wait_recv()
        late.append((p, unit))

    late = []
    for p, stage, unit in plan:
        need(p, unit)
        move = sending(p, stage, unit)
        move.start()
        started.append(move)
        while late:
            item = late.pop()
            move = pass_over(*item)
            move.start()
            started.append(move)
    vector = remote(split_ref, split_out.at[tp], here.at[1], here.at[2], dp, 1 - tp)
    vector.start()
    mine = pltpu.make_async_copy(
        own_ref, out_ref.at[tp, pl.ds(pl.multiple_of(dp * rows, 16), rows)], here.at[0]
    )
    mine.start()
    split_out[tp] = split_ref[...]
    for p, unit in numbers:
        need(p, unit)
        while late:
            item = late.pop()
            move = pass_over(*item)
            move.start()
            started.append(move)
    for p, unit in numbers:
        taken_over(p, unit).wait_recv()
    for move in started:
        move.wait_send()
    remote(split_ref, split_out.at[1 - tp], here.at[1], here.at[2], dp, 1 - tp).wait()
    mine.wait()


def gather_weights(sizes, own, split):
    dp_count = sizes[0] * sizes[1] * sizes[2]
    rows, side = own.shape
    parts = part_table(sizes, rows)
    plan = gather_plan(sizes, parts)
    count = 3 * dp_count
    anyspace = pl.BlockSpec(memory_space=pl.ANY)
    vmem = pl.BlockSpec(memory_space=pltpu.VMEM)
    return pl.pallas_call(
        functools.partial(gather_kernel, sizes, parts, plan),
        in_specs=[vmem] * 2,
        out_specs=[anyspace, vmem],
        out_shape=[
            jax.ShapeDtypeStruct((2, dp_count * rows, side), BF16),
            jax.ShapeDtypeStruct((2,) + split.shape, split.dtype),
        ],
        scratch_shapes=[pltpu.VMEM((rows, side), BF16)]
        + [pltpu.SemaphoreType.DMA((count,))] * 4
        + [pltpu.SemaphoreType.DMA((3,))],
        compiler_params=pltpu.CompilerParams(
            collective_id=0, has_side_effects=True, vmem_limit_bytes=VMEM_LIMIT
        ),
        name="gather_weights",
    )(own, split)


def reduce_kernel(
    sizes, parts, plan, layer_count, target_ref, vec_ref, live_ref, block_ref, grad_ref,
    sum_ref, vec_out, square_out, block_out, grad_out,
    own, other, pieces, tiles, far_tiles, tile_pieces, full,
    load, over_send, over_recv, send, recv, tile_send, tile_recv, hop_send, hop_recv, image_sems,
):
    place = Place(sizes)
    dp, tp = place.dp, place.tp
    rows, side = sum_ref.shape
    moves = [(p, stage, one_on(unit, stage), unit) for p, stage, unit in reversed(plan)]
    order_used = []
    for p, stage, unit, _ in moves:
        if (p, unit) not in order_used:
            order_used.append((p, unit))
    for p in range(len(parts)):
        order_used.append((p, (0, 0, 0)))
    numbers = {item: i for i, item in enumerate(order_used)}
    landing = {}
    offset = 0
    inbound = {item: [] for item in order_used}
    for i, (p, stage, unit, to) in enumerate(moves):
        landing[i] = (offset, parts[p][2])
        offset += parts[p][2]
        inbound[(p, to)].append(i)

    def row_range(p, unit):
        order, start, length = parts[p]
        owner = place.behind(order, unit, 1)
        return pl.ds(pl.multiple_of(owner * rows + start, 16), length)

    def loading(item):
        span = row_range(*item)
        n = numbers[item]
        return pltpu.make_async_copy(target_ref.at[tp, span], own.at[span], load.at[n])

    def passing(item):
        span = row_range(*item)
        n = numbers[item]
        return remote(
            target_ref.at[1 - tp, span], other.at[span], over_send.at[n], over_recv.at[n], dp, 1 - tp
        )

    def sending(i):
        p, stage, unit, _ = moves[i]
        start, length = landing[i]
        return remote(
            own.at[row_range(p, unit)],
            pieces.at[pl.ds(start, length)],
            send.at[i],
            recv.at[i],
            place.along(parts[p][0][stage], 1),
            tp,
        )

    def combine(item, final):
        p, unit = item
        order, start, length = parts[p]
        owner = place.behind(order, unit, 1)
        base = owner * rows + start
        froms = [landing[i][0] for i in inbound[item]]
        step = math.gcd(length, 64)

        def body(k, carry):
            at = pl.ds(pl.multiple_of(base + k * step, 16), step)
            total = own[at, :].astype(F32) + other[at, :].astype(F32)
            for place_from in froms:
                got = pieces[pl.ds(pl.multiple_of(place_from + k * step, 16), step), :]
                total = total + got.astype(F32)
            if final:
                sum_ref[pl.ds(pl.multiple_of(start + k * step, 16), step), :] = total
            else:
                own[at, :] = total.astype(BF16)
            return carry

        lax.fori_loop(0, length // step, body, 0)

    dp_count = sizes[0] * sizes[1] * sizes[2]
    lanes = tiles.shape[2]
    chunks = vec_ref.shape[1] // lanes
    square_row = chunks
    riding = [i for i in range(len(moves)) if moves[i][0] == 1]

    def tile_of(p, unit):
        return tp * dp_count + place.behind(parts[p][0], unit, 1)

    def tile_over():
        return remote(
            tiles.at[pl.ds((1 - tp) * dp_count, dp_count)],
            far_tiles,
            tile_send.at[len(riding)],
            tile_recv.at[len(riding)],
            dp,
            1 - tp,
        )

    def tile_sending(i):
        p, stage, unit, _ = moves[i]
        n = riding.index(i)
        return remote(
            tiles.at[tile_of(p, unit)],
            tile_pieces.at[n],
            tile_send.at[n],
            tile_recv.at[n],
            place.along(parts[p][0][stage], 1),
            tp,
        )

    def tile_combine(item):
        at = tile_of(*item)
        total = tiles[at] + far_tiles[place.behind(parts[1][0], item[1], 1)]
        for j in inbound[item]:
            tile_sending(j).wait_recv()
            total = total + tile_pieces[riding.index(j)]
        tiles[at] = total

    hops = []
    for d in (2, 1, 0):
        reach = 1
        while reach < sizes[d]:
            bit = place.at[d] // reach % 2
            there = place.at[d] + reach * (1 - 2 * bit)
            coords = [there if e == d else place.at[e] for e in range(3)]
            stride = (sizes[1] * sizes[2], sizes[2], 1)[d]
            low = dp // (stride * reach) * (stride * reach)
            hops.append(((coords[0] * sizes[1] + coords[1]) * sizes[2] + coords[2], tp, stride * reach, low))
            reach *= 2

    def hop_copy(k):
        far_dp, far_tp, span, low = hops[k]
        region = full.at[:, pl.ds(low, span)]
        return remote(region, region, hop_send.at[k], hop_recv.at[k], far_dp, far_tp)

    def hop_arrival(k):
        far_dp, far_tp, span, low = hops[k]
        region = full.at[:, pl.ds(far_dp // span * span, span)]
        return remote(region, region, hop_send.at[k], hop_recv.at[k], far_dp, far_tp)

    def swap_copy(share):
        region = full.at[share, dp]
        return remote(region, region, hop_send.at[len(hops)], hop_recv.at[len(hops)], dp, 1 - tp)

    tiles[...] = jnp.zeros_like(tiles)
    for r in range(vec_ref.shape[0]):
        for i in range(chunks):
            tiles[r, i : i + 1, :] = vec_ref[r : r + 1, i * lanes : (i + 1) * lanes]
    greet(place)
    tile_over().start()
    for item in order_used:
        loading(item).start()
        passing(item).start()
    combined = set()
    tile_over().wait_recv()
    for i, (p, stage, unit, to) in enumerate(moves):
        item = (p, unit)
        if item not in combined:
            combined.add(item)
            loading(item).wait()
            passing(item).wait_recv()
            for j in inbound[item]:
                sending(j).wait_recv()
            combine(item, False)
            if p == 1:
                tile_combine(item)
        sending(i).start()
        if p == 1:
            tile_sending(i).start()
    images = [
        remote(src, dst, image_sems.at[2 * n], image_sems.at[2 * n + 1], dp, 1 - tp)
        for n, (src, dst) in enumerate(((block_ref, block_out), (grad_ref, grad_out)))
    ]
    for image in images:
        image.start()
    for p in range(len(parts)):
        item = (p, (0, 0, 0))
        loading(item).wait()
        passing(item).wait_recv()
        for j in inbound[item]:
            sending(j).wait_recv()
        combine(item, True)
    slot_count = live_ref.shape[0]
    squares = jnp.zeros((1, lanes), F32)
    for n in range(slot_count):
        block = sum_ref[n * side : (n + 1) * side, :]
        square = jnp.sum(jnp.sum(block * block, axis=0, keepdims=True), axis=1, keepdims=True)
        squares = squares + jnp.where(live_ref[n, 0:1, :] > 0, square, 0.0)
    tile_combine((1, (0, 0, 0)))
    full[tp, dp] = tiles[tp * dp_count + dp]
    full[tp, dp, square_row : square_row + 1, :] = squares
    swap_copy(tp).start()
    swap_copy(1 - tp).wait_recv()
    for k in range(len(hops)):
        hop_copy(k).start()
        hop_arrival(k).wait_recv()
    total = full[0, 0]
    for n in range(1, 2 * dp_count):
        total = total + full[n // dp_count, n % dp_count]
    squares = total[square_row : square_row + 1, :]
    for r in range(vec_ref.shape[0]):
        for i in range(chunks):
            vec_out[r : r + 1, i * lanes : (i + 1) * lanes] = full[r // dp_count, r % dp_count, i : i + 1, :]
    lane = lax.broadcasted_iota(jnp.int32, (1, lanes), 1)
    per_layer = vec_ref.shape[0] // layer_count
    for layer in range(layer_count):
        block = vec_out[layer * per_layer : (layer + 1) * per_layer, :]
        square = jnp.sum(jnp.sum(block * block, axis=0, keepdims=True), axis=1, keepdims=True)
        squares = squares + jnp.where(lane == layer, square, 0.0)
    square_out[...] = jnp.broadcast_to(squares, square_out.shape)
    for item in order_used:
        passing(item).wait_send()
    for i in range(len(moves)):
        sending(i).wait_send()
    tile_over().wait_send()
    for i in riding:
        tile_sending(i).wait_send()
    swap_copy(tp).wait_send()
    for k in range(len(hops)):
        hop_copy(k).wait_send()
    for image in images:
        image.wait()


def reduce_gradients(sizes, layer_count, slot_count, target, vectors, live_tile, block_own, grad_own):
    dp_count = sizes[0] * sizes[1] * sizes[2]
    side = target.shape[-1]
    rows = slot_count * side
    target = target.reshape(2, dp_count * rows, side)
    parts = part_table(sizes, rows)
    plan = gather_plan(sizes, parts)
    hops = 1 + sum(n.bit_length() - 1 for n in sizes)
    riding = sum(1 for p, _, _ in plan if p == 1)
    units = 3 * dp_count
    landing = sum(parts[p][2] for p, _, _ in plan)
    anyspace = pl.BlockSpec(memory_space=pl.ANY)
    vmem = pl.BlockSpec(memory_space=pltpu.VMEM)
    sd = jax.ShapeDtypeStruct
    dma = pltpu.SemaphoreType.DMA
    return pl.pallas_call(
        functools.partial(reduce_kernel, sizes, parts, plan, layer_count),
        in_specs=[anyspace, vmem, vmem, anyspace, anyspace],
        out_specs=[vmem, vmem, vmem, anyspace, anyspace],
        out_shape=[
            sd((rows, side), F32),
            sd(vectors.shape, F32),
            sd(live_tile.shape[1:], F32),
            sd(block_own.shape, F32),
            sd(block_own.shape, F32),
        ],
        scratch_shapes=[
            pltpu.VMEM((dp_count * rows, side), BF16),
            pltpu.VMEM((dp_count * rows, side), BF16),
            pltpu.VMEM((landing, side), BF16),
            pltpu.VMEM((2 * dp_count,) + live_tile.shape[1:], F32),
            pltpu.VMEM((dp_count,) + live_tile.shape[1:], F32),
            pltpu.VMEM((riding,) + live_tile.shape[1:], F32),
            pltpu.VMEM((2, dp_count) + live_tile.shape[1:], F32),
            dma((units,)),
            dma((units,)),
            dma((units,)),
            dma((len(plan),)),
            dma((len(plan),)),
            dma((riding + 1,)),
            dma((riding + 1,)),
            dma((hops,)),
            dma((hops,)),
            dma((4,)),
        ],
        compiler_params=pltpu.CompilerParams(
            collective_id=1, has_side_effects=True, vmem_limit_bytes=VMEM_LIMIT
        ),
        name="reduce_gradients",
    )(target, vectors, live_tile, block_own, grad_own)


def plain_update(gradient, weight, first_state, second_state, step_rate):
    first_new = MOMENT_DECAY * first_state + (1.0 - MOMENT_DECAY) * gradient
    second_new = MOMENT_DECAY * second_state + (1.0 - MOMENT_DECAY) * gradient * gradient
    stepped = first_new / CORRECTION / (jnp.sqrt(second_new / CORRECTION) + ADAM_EPSILON)
    return (weight - step_rate * stepped, first_new, second_new)


def params():
    return pltpu.CompilerParams(vmem_limit_bytes=VMEM_LIMIT, dimension_semantics=("arbitrary",))


def layer_gradients(layer, meta, kept, target, slot_total, side, share_count):
    names = ("a", "dqkv", "mixed", "dhr", "c", "du", "act", "dyr")
    ops = [kept[name].reshape(-1, kept[name].shape[-1]) for name in names]
    tokens, width = ops[0].shape
    ratio = ops[5].shape[1] // width
    pieces = width // side

    def clip(s, low, count):
        return jnp.minimum(jnp.maximum(s - low, 0), count - 1)

    block = (tokens, width)
    maps = [
        lambda s, meta: (0, 0),
        lambda s, meta: (0, clip(s, 0, 3)),
        lambda s, meta: (0, 0),
        lambda s, meta: (0, 0),
        lambda s, meta: (0, 0),
        lambda s, meta: (0, clip(s, 4, ratio)),
        lambda s, meta: (0, clip(s, 4 + ratio, ratio)),
        lambda s, meta: (0, 0),
    ]
    in_specs = [pl.BlockSpec(block, index) for index in maps]
    alias = {}
    if target is not None:
        in_specs.append(pl.BlockSpec(memory_space=pl.ANY))
        ops.append(target)
        alias = {len(ops): 0}
    grid = pltpu.PrefetchScalarGridSpec(
        num_scalar_prefetch=1,
        grid=(4 + 2 * ratio,),
        in_specs=in_specs,
        out_specs=pl.BlockSpec(memory_space=pl.ANY),
        scratch_shapes=[
            pltpu.VMEM((width, tokens), BF16),
            pltpu.VMEM((2, width, width), BF16),
            pltpu.SemaphoreType.DMA((2,)),
        ],
    )
    return pl.pallas_call(
        functools.partial(gradient_kernel, layer, pieces, ratio),
        grid_spec=grid,
        out_shape=jax.ShapeDtypeStruct((share_count, slot_total, side, side), BF16),
        input_output_aliases=alias,
        compiler_params=params(),
        name=f"gradients{layer}",
    )(meta, *ops)


def adam(live, scalars, gradient, weight, left, right, first, second):
    count, _, side, _ = weight.shape
    spec = pl.BlockSpec((1, 1, side, side), lambda i: (i, 0, 0, 0))
    smem = pl.BlockSpec(memory_space=pltpu.SMEM)
    out = jax.ShapeDtypeStruct(weight.shape, F32)
    return pl.pallas_call(
        adam_kernel,
        grid=(count,),
        in_specs=[smem, smem, pl.BlockSpec((1, side, side), lambda i: (i, 0, 0))] + [spec] * 5,
        out_specs=[spec] * 3,
        out_shape=[out] * 3,
        compiler_params=params(),
        name="adam",
    )(live, scalars, gradient, weight, left, right, first, second)


def shards(
    block_input,
    cotangent,
    mask_patches,
    owners,
    master_slots,
    left_bases,
    right_bases,
    first_moment,
    second_moment,
    shared_vectors,
    shared_first,
    shared_second,
    split_vectors,
    split_first,
    split_second,
):
    slot_count = master_slots.shape[0]
    side = master_slots.shape[-1]
    layer_count = shared_vectors.shape[0]
    width = shared_vectors.shape[2]
    half = split_vectors.shape[2]
    ratio = split_vectors.shape[1] - 2
    block_total = owners.shape[0]
    per_layer = block_total // layer_count
    image_total, seq = block_input.shape[:2]
    dp_count = lax.axis_size("dp")
    tp_count = lax.axis_size("tp")
    count = image_total // tp_count
    rows = round_up(seq, 16)
    keys = round_up(seq, 128)
    slot_total = dp_count * slot_count
    dp_rank = lax.axis_index("dp")
    tp_rank = lax.axis_index("tp")
    slot_index = positions(owners, slot_count)
    meta = jnp.concatenate([slot_index, tp_rank[None].astype(jnp.int32)])
    place = block_total

    sizes = line_sizes(dp_count)
    own = master_slots.reshape(slot_count * side, side)
    blocks, split_pair = gather_weights(sizes, own, split_vectors)
    blocks = blocks.reshape(tp_count, slot_total, side, side)
    split_all = jnp.concatenate([split_pair[t] for t in range(tp_count)], axis=2)
    hits = mask_patches[:, None, :]

    kept, output_own, grad_own, vectors = run_layers(
        count, seq, rows, keys, meta, place, block_input, cotangent, hits, shared_vectors, split_all, blocks
    )
    target = None
    for layer in reversed(range(layer_count)):
        target = layer_gradients(layer, meta, kept[layer], target, slot_total, side, tp_count)
    mine_ids = dp_rank * slot_count + jnp.arange(slot_count, dtype=jnp.int32)
    matches = slot_index[None, :] == mine_ids[:, None]
    live = jnp.any(matches, axis=1)
    block_layer = jnp.arange(block_total, dtype=jnp.int32) // per_layer
    owned_layer = jnp.sum(jnp.where(matches, block_layer[None, :], 0), axis=1)
    lanes = lax.broadcasted_iota(jnp.int32, (slot_count, 8, 128), 2)
    live_tile = jnp.where((lanes == owned_layer[:, None, None]) & live[:, None, None], 1.0, 0.0)
    reduced, vector_sum, square_tile, block_far, grad_far = reduce_gradients(
        sizes, layer_count, slot_count, target, vectors.reshape(-1, width), live_tile, output_own, grad_own
    )

    def both(near, far):
        low = jnp.where(tp_rank == 0, near, far)
        high = jnp.where(tp_rank == 0, far, near)
        return jnp.concatenate([low, high], axis=0)

    block_output = both(output_own, block_far)
    input_grad = both(grad_own, grad_far)
    reduced = reduced.reshape(slot_count, side, side)
    vector_sum = vector_sum.reshape(layer_count, -1, width)
    shared_sum = vector_sum[:, :6]
    split_full = vector_sum[:, 6 : 8 + ratio]
    split_sum = lax.dynamic_slice_in_dim(split_full, tp_rank * half, half, axis=2)
    squares = square_tile[0, :layer_count]
    layer_norms = jnp.sqrt(squares)
    global_norm = jnp.sqrt(jnp.sum(squares))
    factor = CLIP_NORM / jnp.maximum(global_norm, CLIP_NORM)
    step_rate = 0.5 / math.sqrt(width)
    scalars = jnp.stack([factor, jnp.asarray(step_rate, F32)])
    new_master, new_first, new_second = adam(
        live.astype(jnp.int32), scalars, reduced, master_slots, left_bases, right_bases,
        first_moment, second_moment,
    )
    new_shared, new_shared_first, new_shared_second = plain_update(
        shared_sum * factor, shared_vectors, shared_first, shared_second, VECTOR_RATE
    )
    new_split, new_split_first, new_split_second = plain_update(
        split_sum * factor, split_vectors, split_first, split_second, VECTOR_RATE
    )
    return (
        block_output,
        input_grad,
        new_master,
        new_first,
        new_second,
        new_shared,
        new_shared_first,
        new_shared_second,
        new_split,
        new_split_first,
        new_split_second,
        layer_norms,
        global_norm,
    )


def solution(mesh):
    sharded = P("dp", None, None)
    slots = P("dp", "tp", None, None)
    split = P(None, None, "tp")
    return jax.shard_map(
        shards,
        mesh=mesh,
        in_specs=(sharded, sharded, P("dp", None), P())
        + (slots,) * 5
        + (P(),) * 3
        + (split,) * 3,
        out_specs=(sharded, sharded) + (slots,) * 3 + (P(),) * 3 + (split,) * 3 + (P(), P()),
        check_vma=False,
    )
```

time: 544 us -> 474 us (0.87)
  Pallas kernels: 498 us -> 435 us
    pallas_call x6 -> x3, Pallas kernels: 225 us -> 188 us  [the longest x1 137 us: run_layers(): pl.pallas_call(functools.partial(layers_kernel, layer_count, seq, rows, k...]
    pallas_call x1, Pallas kernels: 138 us -> 123 us  [reduce_gradients(): pl.pallas_call(functools.partial(reduce_kernel, sizes, parts, plan, layer...]
    pallas_call x1, Pallas kernels: 20.1 us -> 8.78 us  [adam(): pl.pallas_call(adam_kernel, grid=(count,), in_specs=[smem, smem, pl.Block...]
    unnamed x25 -> x22, local copies, waits for them, and re-layouts: 18.5 us -> 17.6 us
where the time goes in v3:
time: 474 us; the launch traced here: 470 us
  Pallas kernels  435 us (92%)
  local copies, waits for them, and re-layouts  19.3 us (4%)
  other arithmetic  12.8 us (3%)
    pallas_call x1, Pallas kernels, run_layers(): pl.pallas_call(functools.partial(layers_kernel, layer_count, seq, rows, k...  137 us
    pallas_call x1, Pallas kernels, reduce_gradients(): pl.pallas_call(functools.partial(reduce_kernel, sizes, parts, plan, layer...  123 us
    pallas_call x1, Pallas kernels, gather_weights(): pl.pallas_call(functools.partial(gather_kernel, sizes, parts, plan), in_s...  115 us
    pallas_call x2, Pallas kernels, layer_gradients(): pl.pallas_call(functools.partial(gradient_kernel, layer, pieces, ratio),...  50.2 us
    unnamed x22, local copies, waits for them, and re-layouts  17.6 us

profile of v3, /device:TPU:0, one launch (start us, length us, event | category | flops | bytes accessed | tf_op | source)
XLA Modules:
  0.0 469.8 jit_solution(5825980166424330629)
XLA Ops:
  0.7 0.9 convert_reduce_fusion
  1.6 0.7 multiply_add_fusion.2
  2.2 0.6 pad_add_fusion.meta
  2.8 1.3 copy.37.split_ref
  4.1 115.1 %gather_weights.1 = (bf16[2,18432,384]{2,1,0:T(8,128)(2,1)}, f32[2,2,6,384]{3,2,1,0:T(8,128)}) custom-call(f32[1152,384]{1,0:T(8,128)} %bitcast.33, f32[2,6,384]{2,1,0:T(8,128)} %copy.37.split_ref), custom_call_target="tpu_custom_call" | custom-call | tf_op jit(solution)/shard_map/gather_weights/pallas_call | solution.py:697
  119.3 0.8 slice_bitcast_fusion.1
  120.0 0.6 pad_maximum_fusion.2.split_ref
  120.7 0.0 copy-start.1
  120.7 6.2 %copy.39.dy_ref = f32[8,197,768]{2,1,0:T(8,128)} copy(f32[8,197,768]{2,0,1:T(8,128)} %param.16) | data formatting | bytes 9682944 | tf_op args[1]
  126.9 0.0 copy-done.1
  126.9 0.0 copy-start.2
  126.9 2.0 copy.38.x_ref
  128.9 0.0 copy-done.2
  128.9 0.6 copy.40.shared_ref
  129.5 137.5 %layers.1 = (bf16[4,208,768]{2,1,0:T(8,128)(2,1)}, bf16[4,208,768]{2,1,0:T(8,128)(2,1)}, bf16[4,208,768]{2,1,0:T(8,128)(2,1)}, bf16[4,208,3072]{2,1,0:T(8,128)(2...) custom-call(s32[49]{0:T(128)} %pad_add_fusion.meta, ...), custom_call_target="tpu_custom_call" | custom-call | tf_op jit(solution)/shard_map/layers/pallas_call | solution.py:381
  267.0 25.1 %gradients1.1.rest_0_ = bf16[2,48,384,384]{3,2,1,0:T(8,128)(2,1)} custom-call(s32[49]{0:T(128)} %pad_add_fusion.meta, bf16[832,768]{1,0:T(8,128)(2,1)} %bitcast.46, bf16[832,2304]{1,0:T(8,128)(2,1)} %bitcast.39, bf16[832,768]{1,0:T(8,128)(2,1)} %bitcast.47, bf16[832,768]{1,0:T(8,128)(2,1)} %bitcast.50, bf16[832,768]{1,0:T(8,128)(2,1)} %bitcast.48, ...), custom_call_target="tpu_custom_call" | custom-call | tf_op jit(solution)/shard_map/gradients1/pallas_call | solution.py:1037
  292.1 25.1 %gradients0.1 = bf16[2,48,384,384]{3,2,1,0:T(8,128)(2,1)} custom-call(s32[49]{0:T(128)} %pad_add_fusion.meta, bf16[832,768]{1,0:T(8,128)(2,1)} %bitcast.41, bf16[832,2304]{1,0:T(8,128)(2,1)} %bitcast.38, bf16[832,768]{1,0:T(8,128)(2,1)} %bitcast.42, bf16[832,768]{1,0:T(8,128)(2,1)} %bitcast.45, ...), custom_call_target="tpu_custom_call", output_to_operand_aliasing={{}: (9, {})} | custom-call | tf_op jit(solution)/shard_map/gradients0/pallas_call | solution.py:1037
  317.2 0.2 compare_reduce_fusion
  317.4 0.2 fusion.5
  317.6 0.7 fusion.4.live_ref
  318.3 0.0 copy-start.3
  318.3 0.0 copy-start.6
  318.3 0.0 copy-start.7
  318.3 0.0 copy-start.4
  318.3 0.0 copy-start.5
  318.3 123.2 %reduce_gradients.1 = (f32[1152,384]{1,0:T(8,128)}, f32[32,768]{1,0:T(8,128)}, f32[8,128]{1,0:T(8,128)}, f32[4,197,768]{2,1,0:T(8,128)}, f32[4,197,768]{2,1,0:T(8,128)}) custom-call(bf16[2,18432,384]{2,1,0:T(8,128)(2,1)} %bitcast.31, f32[32,768]{1,0:T(8,128)} %bitcast.52, f32[3,8,128]{2,1,0:T(8,128)} %fusion.4.live_ref, ...), custom_call_target="tpu_custom_call" | custom-call | tf_op jit(solution)/shard_map/reduce_gradients/pallas_call | solution.py:951
  441.6 0.9 fusion.8
  442.5 1.8 sqrt_bitcast_fusion
  445.0 0.0 copy-done.3
  445.0 0.0 copy-done.6
  445.0 0.0 copy-done.7
  445.0 0.7 multiply_subtract_fusion.1
  445.7 0.0 copy-done.4
  445.7 0.0 copy-done.5
  445.7 0.7 multiply_subtract_fusion
  446.5 0.6 pad_maximum_fusion.3.factor_ref
  447.1 0.5 convert_element_type.7.live_ref
  447.6 0.0 copy-start
  447.6 8.8 %adam.1 = (f32[3,1,384,384]{3,2,1,0:T(8,128)}, f32[3,1,384,384]{3,2,1,0:T(8,128)}, f32[3,1,384,384]{3,2,1,0:T(8,128)}) custom-call(s32[3]{0:T(128)} %convert_element_type.7.live_ref, f32[2]{0:T(128)} %pad_maximum_fusion.3.factor_ref, f32[3,384,384]{2,1,0:T(8,128)} %bitcast.40, f32[3,1,384,384]{3,2,1,0:T(8,128)} %w_ref.1, f32[3,1,384,384]{3,2,1,0:T(8,128)} %l_ref.1, ...), custom_call_target="tpu_custom_call" | custom-call | tf_op jit(solution)/shard_map/adam/pallas_call | solution.py:1052
  456.4 0.0 copy-done
  456.4 4.0 broadcast_select_fusion.1
  460.4 0.3 pad_maximum_fusion.1
  460.7 3.7 copy.44
  464.4 0.3 pad_maximum_fusion
  464.8 3.7 copy.43
  (3 shorter events, 0.0 us)
Async XLA Ops:
  120.7 6.2 %copy-start.1 = (bf16[8,197,768]{2,0,1:T(8,128)(2,1)S(1)}, bf16[8,197,768]{2,0,1:T(8,128)(2,1)}, u32[]{:S(2)}) copy-start(bf16[8,197,768]{2,0,1:T(8,128)(2,1)} %param.15) | copy-start | bytes 7262212
  126.9 2.0 copy-start.2
  318.3 126.7 %copy-start.3 = (f32[2,6,384]{2,0,1:T(2,128)S(1)}, f32[2,6,384]{2,0,1:T(2,128)}, u32[]{:S(2)}) copy-start(f32[2,6,384]{2,0,1:T(2,128)} %param.27) | copy-start | bytes 55300
  318.3 126.7 %copy-start.6 = (f32[2,6,384]{2,0,1:T(2,128)S(1)}, f32[2,6,384]{2,0,1:T(2,128)}, u32[]{:S(2)}) copy-start(f32[2,6,384]{2,0,1:T(2,128)} %param.28) | copy-start | bytes 55300
  318.3 126.7 %copy-start.7 = (f32[2,6,384]{2,0,1:T(2,128)S(1)}, f32[2,6,384]{2,0,1:T(2,128)}, u32[]{:S(2)}) copy-start(f32[2,6,384]{2,0,1:T(2,128)} %param.29) | copy-start | bytes 55300
  318.3 127.4 %copy-start.4 = (f32[2,6,768]{2,0,1:T(2,128)S(1)}, f32[2,6,768]{2,0,1:T(2,128)}, u32[]{:S(2)}) copy-start(f32[2,6,768]{2,0,1:T(2,128)} %param.25) | copy-start | bytes 110596
  318.3 127.4 %copy-start.5 = (f32[2,6,768]{2,0,1:T(2,128)S(1)}, f32[2,6,768]{2,0,1:T(2,128)}, u32[]{:S(2)}) copy-start(f32[2,6,768]{2,0,1:T(2,128)} %param.26) | copy-start | bytes 110596
  447.6 8.8 %copy-start = (f32[4,197,768]{2,1,0:T(8,128)S(1)}, f32[4,197,768]{2,1,0:T(8,128)}, u32[]{:S(2)}) copy-start(f32[4,197,768]{2,1,0:T(8,128)} %get-tuple-element.44.block_ref) | copy-start | bytes 7262212

commit v4 on v3

--- a/solution.py
+++ b/solution.py
@@ -120,12 +120,6 @@
     return jnp.concatenate([jnp.where(m, value, zero) for m in masks], axis=0)
 
 
-def padded_rows(ref, seq, rows, scratch):
-    tail = seq // 16 * 16
-    scratch[tail:rows, :] = jnp.zeros((rows - tail, ref.shape[2]), F32)
-    scratch[0:seq, :] = ref[0].astype(F32)
-
-
 SAVED = ("a", "mixed", "c", "act", "dyr", "du", "dhr", "dqkv")
 
 
@@ -138,7 +132,7 @@
     weights = [rest[4 * n : 4 * n + 4] for n in range(layer_count)]
     rest = rest[4 * layer_count :]
     holds = [rest[7 * n : 7 * n + 7] for n in range(layer_count)]
-    seed_ref, save_sems, weight_sems = rest[7 * layer_count :]
+    save_sems, weight_sems = rest[7 * layer_count :]
     width = x_ref.shape[2]
     ratio = split_ref.shape[1] - 2
     groups = width // LANES
@@ -147,27 +141,24 @@
     zero = jnp.zeros((), BF16)
     masks = head_masks()
 
-    class Kept:
-        def __init__(self, layer, name):
-            n = layer * 8 + SAVED.index(name)
-            self.out, self.ref, self.sem = outs[n], saves[n], save_sems.at[n]
-
-        def copy(self, i):
-            return pltpu.make_async_copy(self.ref, self.out.at[i], self.sem)
-
-        def free(self):
-            @pl.when(step > 0)
-            def _():
-                self.copy(step - 1).wait()
-
-        def send(self):
-            self.copy(step).start()
-
-    def keep(layer, name, value):
-        kept = Kept(layer, name)
-        kept.free()
-        kept.ref[...] = value
-        kept.send()
+    def saving(layer, name, i):
+        n = layer * 8 + SAVED.index(name)
+        return pltpu.make_async_copy(saves[n], outs[n].at[i], save_sems.at[n])
+
+    def free(names):
+        @pl.when(step > 0)
+        def _():
+            for n in range(layer_count):
+                for name in names:
+                    saving(n, name, step - 1).wait()
+
+    def send(names):
+        for n in range(layer_count):
+            for name in names:
+                saving(n, name, step).start()
+
+    def buffer(layer, name):
+        return saves[layer * 8 + SAVED.index(name)]
 
     jobs = [
         weight_copies(meta, n, blocks, *weights[n], weight_sems.at[n]) for n in range(layer_count)
@@ -180,13 +171,14 @@
                 for job in jobs[n][kind]:
                     job.start()
 
-    def ready(layer, kind):
+    def ready(pairs):
         @pl.when(step == 0)
         def _():
-            target = weights[layer][kind]
-            pltpu.make_async_copy(target, target, weight_sems.at[layer, kind]).wait()
-
-    start([(0, 0), (0, 1)])
+            for n, kind in pairs:
+                target = weights[n][kind]
+                pltpu.make_async_copy(target, target, weight_sems.at[n, kind]).wait()
+
+    start([(0, 0)])
 
     @pl.when(step == 0)
     def _():
@@ -195,22 +187,22 @@
             for ref in (hold[3], hold[4]):
                 ref[rows:keys, :] = jnp.zeros((keys - rows, width), BF16)
 
-    padded_rows(x_ref, seq, rows, holds[0][0])
+    free(SAVED[:4])
+    holds[0][0][...] = x_ref[0].astype(F32)
     real = lax.broadcasted_iota(jnp.int32, (1, keys), 1) < seq
     for n in range(layer_count):
         xs, hs, qs, ks, vs, ps, ss = holds[n]
         wp, wo, wu, wd = weights[n]
         unit, _ = normalized(xs[...])
         a = (unit * shared_ref[n, 0:1, :] + shared_ref[n, 1:2, :]).astype(BF16)
-        keep(n, "a", a)
-        ready(n, 0)
+        buffer(n, "a")[...] = a
         if n == 0:
-            start([(0, 2), (0, 3)])
+            ready([(0, 0)])
+            start([(0, 1), (0, 2), (0, 3)])
         qs[...] = ((nn(a, wp[:, 0:width]) + split_ref[n, 0:1, :]) * scale).astype(BF16)
         ks[0:rows, :] = nn(a, wp[:, width : 2 * width]).astype(BF16)
         vs[0:rows, :] = (nn(a, wp[:, 2 * width :]) + split_ref[n, 1:2, :]).astype(BF16)
-        mixed = Kept(n, "mixed")
-        mixed.free()
+        mixed = buffer(n, "mixed")
         for g in range(groups):
             cols = slice(g * LANES, (g + 1) * LANES)
             scores = nt(spread_heads(masks, qs[:, cols]), ks[:, cols])
@@ -225,39 +217,36 @@
             for h in range(GROUP):
                 part = nn(probs[h * rows : (h + 1) * rows, :], jnp.where(masks[h], v4, zero))
                 mix = part if mix is None else mix + part
-            mixed.ref[:, cols] = mix.astype(BF16)
-        mixed.send()
-        ready(n, 1)
-        h = xs[...] + nn(mixed.ref[...], wo[...]) + shared_ref[n, 2:3, :]
+            mixed[:, cols] = mix.astype(BF16)
+        if n == 0:
+            ready([(0, 1), (0, 2), (0, 3)])
+            start([(m, kind) for m in range(1, layer_count) for kind in range(4)])
+        h = xs[...] + nn(mixed[...], wo[...]) + shared_ref[n, 2:3, :]
         hs[...] = h
         unit, _ = normalized(h)
         c = (unit * shared_ref[n, 3:4, :] + shared_ref[n, 4:5, :]).astype(BF16)
-        keep(n, "c", c)
-        ready(n, 2)
-        ready(n, 3)
-        if n == 0:
-            start([(m, kind) for m in range(1, layer_count) for kind in range(4)])
+        buffer(n, "c")[...] = c
         y = h + shared_ref[n, 5:6, :]
-        active = Kept(n, "act")
-        active.free()
+        active = buffer(n, "act")
         for j in range(ratio):
             cols = slice(j * width, (j + 1) * width)
             u = nn(c, wu[:, cols]) + split_ref[n, 2 + j : 3 + j, :]
             act, slope = gelu_pair(u)
             act = act.astype(BF16)
-            active.ref[:, cols] = act
+            active[:, cols] = act
             ss[:, cols] = slope.astype(BF16)
             y = y + nn(act, wd[cols, :])
-        active.send()
         if n + 1 < layer_count:
             holds[n + 1][0][...] = y
+            ready([(n + 1, kind) for kind in range(4)])
         else:
             y_ref[0] = y[0:seq, :]
 
+    send(SAVED[:4])
+    free(SAVED[4:])
     wanted = lax.broadcasted_iota(jnp.int32, (rows, 1), 0)
     hit = jnp.max(jnp.where(hits_ref[0] + 1 == wanted, 1.0, 0.0), axis=-1, keepdims=True)
-    padded_rows(dy_ref, seq, rows, seed_ref)
-    dy = seed_ref[...] * hit
+    dy = dy_ref[0] * hit
     for n in reversed(range(layer_count)):
         xs, hs, qs, ks, vs, ps, ss = holds[n]
         wp, wo, wu, wd = weights[n]
@@ -267,28 +256,25 @@
 
         collect(5, dy)
         dyr = dy.astype(BF16)
-        keep(n, "dyr", dyr)
-        hidden = Kept(n, "du")
-        hidden.free()
+        buffer(n, "dyr")[...] = dyr
+        hidden = buffer(n, "du")
         dc = None
         for j in range(ratio):
             cols = slice(j * width, (j + 1) * width)
             du = (nt(dyr, wd[cols, :]) * ss[:, cols].astype(F32)).astype(BF16)
-            hidden.ref[:, cols] = du
+            hidden[:, cols] = du
             collect(8 + j, du.astype(F32))
             part = nt(du, wu[:, cols])
             dc = part if dc is None else dc + part
-        hidden.send()
         unit, inverse = normalized(hs[...])
         collect(3, dc * unit)
         collect(4, dc)
         dh = dy + norm_back(dc, unit, inverse, shared_ref[n, 3:4, :])
         collect(2, dh)
         dhr = dh.astype(BF16)
-        keep(n, "dhr", dhr)
+        buffer(n, "dhr")[...] = dhr
         dmixed = nt(dhr, wo[...]).astype(BF16)
-        back = Kept(n, "dqkv")
-        back.free()
+        back = buffer(n, "dqkv")
         for g in range(groups):
             cols = slice(g * LANES, (g + 1) * LANES)
             dm = spread_heads(masks, dmixed[:, cols])
@@ -304,11 +290,10 @@
             for h in range(GROUP):
                 part = nn(ds[h * rows : (h + 1) * rows, :], jnp.where(masks[h], k4, zero))
                 dq = part if dq is None else dq + part
-            back.ref[:, cols] = (dq.astype(BF16).astype(F32) * scale).astype(BF16)
-            back.ref[:, width + g * LANES : width + (g + 1) * LANES] = dk
-            back.ref[:, 2 * width + g * LANES : 2 * width + (g + 1) * LANES] = dv
-        back.send()
-        dqkv = back.ref[...]
+            back[:, cols] = (dq.astype(BF16).astype(F32) * scale).astype(BF16)
+            back[:, width + g * LANES : width + (g + 1) * LANES] = dk
+            back[:, 2 * width + g * LANES : 2 * width + (g + 1) * LANES] = dv
+        dqkv = back[...]
         collect(6, dqkv[:, 0:width].astype(F32))
         collect(7, dqkv[:, 2 * width :].astype(F32))
         da = nt(dqkv, wp[...])
@@ -317,12 +302,13 @@
         collect(1, da)
         dy = dh + norm_back(da, unit, inverse, shared_ref[n, 0:1, :])
     dx_ref[0] = dy[0:seq, :]
+    send(SAVED[4:])
 
     @pl.when(step == pl.num_programs(0) - 1)
     def _():
         for n in range(layer_count):
             for name in SAVED:
-                Kept(n, name).copy(step).wait()
+                saving(n, name, step).wait()
 
 
 def run_layers(count, seq, rows, keys, meta, place, stream, seed, hits, shared, split, blocks):
@@ -333,8 +319,8 @@
     widths = [width, width, width, ratio * width, width, ratio * width, width, 3 * width] * layer_count
     anyspace = pl.BlockSpec(memory_space=pl.ANY)
     outs = [sd((count, rows, w), BF16) for w in widths]
-    outs += [sd((count, seq, width), F32)] * 2 + [sd((layer_count, 16, width), F32)]
-    image = pl.BlockSpec((1, seq, width), lambda i, meta: (i, 0, 0))
+    outs += [sd((2 * count, seq, width), F32)] * 2 + [sd((layer_count, 16, width), F32)]
+    image = pl.BlockSpec((1, seq, width), lambda i, meta: (meta[place] * count + i, 0, 0))
 
     def shifted(shape):
         return pl.BlockSpec((1,) + tuple(shape[1:]), lambda i, meta: (meta[place] * count + i, 0, 0))
@@ -360,7 +346,6 @@
         vmem((rows, ratio * width), BF16),
     ] * layer_count
     scratch += [
-        vmem((rows, width), F32),
         pltpu.SemaphoreType.DMA((8 * layer_count,)),
         pltpu.SemaphoreType.DMA((layer_count, 4)),
     ]
@@ -368,8 +353,8 @@
         num_scalar_prefetch=1,
         grid=(count,),
         in_specs=[
-            shifted(stream.shape),
-            shifted(seed.shape),
+            pl.BlockSpec((1, rows, width), lambda i, meta: (i, 0, 0)),
+            pl.BlockSpec((1, rows, width), lambda i, meta: (i, 0, 0)),
             shifted(hits.shape),
             whole(shared.shape),
             whole(split.shape),
@@ -466,14 +451,16 @@
         drain(slot)
 
 
-def adam_kernel(live_ref, factor_ref, g_ref, w_ref, l_ref, r_ref, m_ref, s_ref, w_out, m_out, s_out):
-    step_rate = factor_ref[1]
+def adam_kernel(layer_count, step_rate, live_ref, square_ref, g_ref, w_ref, l_ref, r_ref, m_ref, s_ref, w_out, m_out, s_out):
+    lane = lax.broadcasted_iota(jnp.int32, (1, square_ref.shape[1]), 1)
+    total = jnp.sum(jnp.where(lane < layer_count, square_ref[0:1, :], 0.0), axis=1, keepdims=True)
+    factor = CLIP_NORM / jnp.maximum(jnp.sqrt(total), CLIP_NORM)
     slot = pl.program_id(0)
     alive = live_ref[slot] > 0
     weight = w_ref[0, 0]
     left = l_ref[0, 0].astype(BF16)
     right = r_ref[0, 0].astype(BF16)
-    turned = nn(tn(left, g_ref[0].astype(BF16)).astype(BF16), right) * factor_ref[0]
+    turned = nn(tn(left, g_ref[0].astype(BF16)).astype(BF16), right) * factor
     first = MOMENT_DECAY * m_ref[0, 0] + (1.0 - MOMENT_DECAY) * turned
     second = MOMENT_DECAY * s_ref[0, 0] + (1.0 - MOMENT_DECAY) * turned * turned
     stepped = first / CORRECTION / (jnp.sqrt(second / CORRECTION) + ADAM_EPSILON)
@@ -595,8 +582,8 @@
 
 
 def gather_kernel(
-    sizes, parts, plan, master_ref, split_ref, out_ref, split_out,
-    own_ref, send, recv, over_send, over_recv, here,
+    sizes, parts, plan, master_ref, split_ref, x_ref, seed_ref, out_ref, split_out, x_out, seed_out,
+    own_ref, x_in, x_wide, seed_in, x_own, seed_own, send, recv, over_send, over_recv, here, stream_sems,
 ):
     place = Place(sizes)
     dp, tp = place.dp, place.tp
@@ -644,6 +631,43 @@
     greet(place)
     started = []
     arrived = set()
+    count, padded = x_own.shape[:2]
+    images = 2 * count
+    seq = x_in.shape[0] // images
+    strips, _, lanes = x_wide.shape
+    fetch = [pltpu.make_async_copy(x_ref, x_in, stream_sems.at[0])] + [
+        pltpu.make_async_copy(
+            seed_ref.at[:, pl.ds(n * lanes, lanes)], seed_in.at[n], stream_sems.at[4 + n]
+        )
+        for n in range(strips)
+    ]
+    leave = [
+        pltpu.make_async_copy(x_own, x_out, stream_sems.at[2]),
+        pltpu.make_async_copy(seed_own, seed_out, stream_sems.at[3]),
+    ]
+    tail = seq // 16 * 16
+
+    def widen():
+        fetch[0].wait()
+        for n in range(strips):
+            x_wide[n] = x_in[:, n * lanes : (n + 1) * lanes].astype(F32)
+
+    def pick(source, target, i):
+        def go():
+            target[i, tail:padded, :] = jnp.zeros((padded - tail, target.shape[2]), target.dtype)
+            for n in range(strips):
+                rows_of = source[n, pl.ds(tp * count + i, seq, stride=images), :]
+                target[i, 0:seq, n * lanes : (n + 1) * lanes] = rows_of.astype(target.dtype)
+
+        return go
+
+    def leaving(n):
+        return lambda: leave[n].start()
+
+    tasks = [lambda: [copy.start() for copy in fetch], widen]
+    tasks += [pick(x_wide, x_own, i) for i in range(count)] + [leaving(0), lambda: [copy.wait() for copy in fetch[1:]]]
+    tasks += [pick(seed_in, seed_own, i) for i in range(count)] + [leaving(1)]
+    spacing = max(1, len(plan) // (len(tasks) + 1))
 
     def need(p, unit):
         if (p, unit) in arrived:
@@ -654,7 +678,9 @@
         late.append((p, unit))
 
     late = []
-    for p, stage, unit in plan:
+    for i, (p, stage, unit) in enumerate(plan):
+        if (i + 1) % spacing == 0 and tasks:
+            tasks.pop(0)()
         need(p, unit)
         move = sending(p, stage, unit)
         move.start()
@@ -664,6 +690,8 @@
             move = pass_over(*item)
             move.start()
             started.append(move)
+    for task in tasks:
+        task()
     vector = remote(split_ref, split_out.at[tp], here.at[1], here.at[2], dp, 1 - tp)
     vector.start()
     mine = pltpu.make_async_copy(
@@ -682,34 +710,54 @@
         taken_over(p, unit).wait_recv()
     for move in started:
         move.wait_send()
+    for copy in leave:
+        copy.wait()
     remote(split_ref, split_out.at[1 - tp], here.at[1], here.at[2], dp, 1 - tp).wait()
     mine.wait()
 
 
-def gather_weights(sizes, own, split):
+def gather_weights(sizes, own, split, stream, seed, rows_padded):
     dp_count = sizes[0] * sizes[1] * sizes[2]
     rows, side = own.shape
     parts = part_table(sizes, rows)
     plan = gather_plan(sizes, parts)
-    count = 3 * dp_count
+    units = 3 * dp_count
     anyspace = pl.BlockSpec(memory_space=pl.ANY)
     vmem = pl.BlockSpec(memory_space=pltpu.VMEM)
+    sd = jax.ShapeDtypeStruct
+    tokens, images, width = stream.shape
+    flat = (tokens * images, width)
+    mine = (images // 2, rows_padded, width)
+    dma = pltpu.SemaphoreType.DMA
     return pl.pallas_call(
         functools.partial(gather_kernel, sizes, parts, plan),
-        in_specs=[vmem] * 2,
-        out_specs=[anyspace, vmem],
+        in_specs=[vmem, vmem, anyspace, anyspace],
+        out_specs=[anyspace, vmem, anyspace, anyspace],
         out_shape=[
-            jax.ShapeDtypeStruct((2, dp_count * rows, side), BF16),
-            jax.ShapeDtypeStruct((2,) + split.shape, split.dtype),
+            sd((2, dp_count * rows, side), BF16),
+            sd((2,) + split.shape, split.dtype),
+            sd(mine, BF16),
+            sd(mine, F32),
         ],
-        scratch_shapes=[pltpu.VMEM((rows, side), BF16)]
-        + [pltpu.SemaphoreType.DMA((count,))] * 4
-        + [pltpu.SemaphoreType.DMA((3,))],
+        scratch_shapes=[
+            pltpu.VMEM((rows, side), BF16),
+            pltpu.VMEM(flat, BF16),
+            pltpu.VMEM((width // 128, tokens * images, 128), F32),
+            pltpu.VMEM((width // 128, tokens * images, 128), F32),
+            pltpu.VMEM(mine, BF16),
+            pltpu.VMEM(mine, F32),
+            dma((units,)),
+            dma((units,)),
+            dma((units,)),
+            dma((units,)),
+            dma((3,)),
+            dma((4 + width // 128,)),
+        ],
         compiler_params=pltpu.CompilerParams(
             collective_id=0, has_side_effects=True, vmem_limit_bytes=VMEM_LIMIT
         ),
         name="gather_weights",
-    )(own, split)
+    )(own, split, stream.reshape(flat), seed.reshape(flat))
 
 
 def reduce_kernel(
@@ -878,12 +926,14 @@
         sending(i).start()
         if p == 1:
             tile_sending(i).start()
-    images = [
-        remote(src, dst, image_sems.at[2 * n], image_sems.at[2 * n + 1], dp, 1 - tp)
-        for n, (src, dst) in enumerate(((block_ref, block_out), (grad_ref, grad_out)))
-    ]
-    for image in images:
-        image.start()
+    half = block_out.shape[0] // 2
+
+    def image_copy(n, ref, share):
+        region = ref.at[pl.ds(share * half, half)]
+        return remote(region, region, image_sems.at[2 * n], image_sems.at[2 * n + 1], dp, 1 - tp)
+
+    for n, ref in enumerate((block_out, grad_out)):
+        image_copy(n, ref, tp).start()
     for p in range(len(parts)):
         item = (p, (0, 0, 0))
         loading(item).wait()
@@ -929,8 +979,9 @@
     swap_copy(tp).wait_send()
     for k in range(len(hops)):
         hop_copy(k).wait_send()
-    for image in images:
-        image.wait()
+    for n, ref in enumerate((block_out, grad_out)):
+        image_copy(n, ref, tp).wait_send()
+        image_copy(n, ref, 1 - tp).wait_recv()
 
 
 def reduce_gradients(sizes, layer_count, slot_count, target, vectors, live_tile, block_own, grad_own):
@@ -978,6 +1029,7 @@
             dma((hops,)),
             dma((4,)),
         ],
+        input_output_aliases={3: 3, 4: 4},
         compiler_params=pltpu.CompilerParams(
             collective_id=1, has_side_effects=True, vmem_limit_bytes=VMEM_LIMIT
         ),
@@ -1044,20 +1096,20 @@
     )(meta, *ops)
 
 
-def adam(live, scalars, gradient, weight, left, right, first, second):
+def adam(layer_count, step_rate, live, squares, gradient, weight, left, right, first, second):
     count, _, side, _ = weight.shape
     spec = pl.BlockSpec((1, 1, side, side), lambda i: (i, 0, 0, 0))
     smem = pl.BlockSpec(memory_space=pltpu.SMEM)
     out = jax.ShapeDtypeStruct(weight.shape, F32)
     return pl.pallas_call(
-        adam_kernel,
+        functools.partial(adam_kernel, layer_count, step_rate),
         grid=(count,),
-        in_specs=[smem, smem, pl.BlockSpec((1, side, side), lambda i: (i, 0, 0))] + [spec] * 5,
+        in_specs=[smem, pl.BlockSpec(squares.shape, lambda i: (0, 0)), pl.BlockSpec((1, side, side), lambda i: (i, 0, 0))] + [spec] * 5,
         out_specs=[spec] * 3,
         out_shape=[out] * 3,
         compiler_params=params(),
         name="adam",
-    )(live, scalars, gradient, weight, left, right, first, second)
+    )(live, squares, gradient, weight, left, right, first, second)
 
 
 def shards(
@@ -1100,13 +1152,20 @@
 
     sizes = line_sizes(dp_count)
     own = master_slots.reshape(slot_count * side, side)
-    blocks, split_pair = gather_weights(sizes, own, split_vectors)
+    blocks, split_pair, stream, seed = gather_weights(
+        sizes,
+        own,
+        split_vectors,
+        block_input.transpose(1, 0, 2),
+        cotangent.transpose(1, 0, 2),
+        rows,
+    )
     blocks = blocks.reshape(tp_count, slot_total, side, side)
     split_all = jnp.concatenate([split_pair[t] for t in range(tp_count)], axis=2)
     hits = mask_patches[:, None, :]
 
     kept, output_own, grad_own, vectors = run_layers(
-        count, seq, rows, keys, meta, place, block_input, cotangent, hits, shared_vectors, split_all, blocks
+        count, seq, rows, keys, meta, place, stream, seed, hits, shared_vectors, split_all, blocks
     )
     target = None
     for layer in reversed(range(layer_count)):
@@ -1118,17 +1177,10 @@
     owned_layer = jnp.sum(jnp.where(matches, block_layer[None, :], 0), axis=1)
     lanes = lax.broadcasted_iota(jnp.int32, (slot_count, 8, 128), 2)
     live_tile = jnp.where((lanes == owned_layer[:, None, None]) & live[:, None, None], 1.0, 0.0)
-    reduced, vector_sum, square_tile, block_far, grad_far = reduce_gradients(
+    reduced, vector_sum, square_tile, block_output, input_grad = reduce_gradients(
         sizes, layer_count, slot_count, target, vectors.reshape(-1, width), live_tile, output_own, grad_own
     )
 
-    def both(near, far):
-        low = jnp.where(tp_rank == 0, near, far)
-        high = jnp.where(tp_rank == 0, far, near)
-        return jnp.concatenate([low, high], axis=0)
-
-    block_output = both(output_own, block_far)
-    input_grad = both(grad_own, grad_far)
     reduced = reduced.reshape(slot_count, side, side)
     vector_sum = vector_sum.reshape(layer_count, -1, width)
     shared_sum = vector_sum[:, :6]
@@ -1139,9 +1191,8 @@
     global_norm = jnp.sqrt(jnp.sum(squares))
     factor = CLIP_NORM / jnp.maximum(global_norm, CLIP_NORM)
     step_rate = 0.5 / math.sqrt(width)
-    scalars = jnp.stack([factor, jnp.asarray(step_rate, F32)])
     new_master, new_first, new_second = adam(
-        live.astype(jnp.int32), scalars, reduced, master_slots, left_bases, right_bases,
+        layer_count, step_rate, live.astype(jnp.int32), square_tile, reduced, master_slots, left_bases, right_bases,
         first_moment, second_moment,
     )
     new_shared, new_shared_first, new_shared_second = plain_update(

time: 474 us -> 459 us (0.968)
  other arithmetic: 12.8 us -> 6.2 us
  Pallas kernels: 435 us -> 430 us
    pallas_call x1, Pallas kernels: 137 us -> 133 us  [run_layers(): pl.pallas_call(functools.partial(layers_kernel, layer_count, seq, rows, k...]
    unnamed x22 -> x18, local copies, waits for them, and re-layouts: 17.6 us -> 14.3 us
where the time goes in v4:
time: 459 us; the launch traced here: 455 us
  Pallas kernels  430 us (94%)
  local copies, waits for them, and re-layouts  16 us (3%)
  other arithmetic  6.2 us (1%)
    pallas_call x1, Pallas kernels, run_layers(): pl.pallas_call(functools.partial(layers_kernel, layer_count, seq, rows, k...  133 us
    pallas_call x1, Pallas kernels, reduce_gradients(): pl.pallas_call(functools.partial(reduce_kernel, sizes, parts, plan, layer...  123 us
    pallas_call x1, Pallas kernels, gather_weights(): pl.pallas_call(functools.partial(gather_kernel, sizes, parts, plan), in_s...  115 us
    pallas_call x2, Pallas kernels, layer_gradients(): pl.pallas_call(functools.partial(gradient_kernel, layer, pieces, ratio),...  50.2 us
    unnamed x18, local copies, waits for them, and re-layouts  14.3 us

profile of v4, /device:TPU:0, one launch (start us, length us, event | category | flops | bytes accessed | tf_op | source)
XLA Modules:
  0.0 455.3 jit_solution(393569511692802782)
XLA Ops:
  0.6 1.3 copy.37.split_ref
  2.0 0.0 copy-start.6
  2.0 0.0 copy-start
  2.0 115.2 %gather_weights.1 = (bf16[2,18432,384]{2,1,0:T(8,128)(2,1)}, f32[2,2,6,384]{3,2,1,0:T(8,128)}, bf16[4,208,768]{2,1,0:T(8,128)(2,1)}, f32[4,208,768]{2,1,0:T(8,128)}) custom-call(f32[1152,384]{1,0:T(8,128)} %bitcast.38, f32[2,6,384]{2,1,0:T(8,128)} %copy.37.split_ref, bf16[1576,768]{1,0:T(8,128)(2,1)} %bitcast.46, f32[1576,768]{1,0:T(8,128)} %bitcast.43), custom_call_target="tpu_custom_call" | custom-call | tf_op jit(solution)/shard_map/gather_weights/pallas_call | solution.py:732
  117.2 0.8 slice_bitcast_fusion.1
  118.0 0.6 pad_maximum_fusion.split_ref
  118.6 0.0 copy-done.6
  118.6 0.2 convert_reduce_fusion
  118.8 0.6 pad_add_fusion.meta
  119.4 0.0 copy-done
  119.4 0.6 copy.38.shared_ref
  120.0 132.5 %layers.1 = (bf16[4,208,768]{2,1,0:T(8,128)(2,1)}, bf16[4,208,768]{2,1,0:T(8,128)(2,1)}, bf16[4,208,768]{2,1,0:T(8,128)(2,1)}, bf16[4,208,3072]{2,1,0:T(8,128)(2...) custom-call(s32[49]{0:T(128)} %pad_add_fusion.meta, ...), custom_call_target="tpu_custom_call" | custom-call | tf_op jit(solution)/shard_map/layers/pallas_call | solution.py:366
  252.6 25.1 %gradients1.1.rest_0_ = bf16[2,48,384,384]{3,2,1,0:T(8,128)(2,1)} custom-call(s32[49]{0:T(128)} %pad_add_fusion.meta, bf16[832,768]{1,0:T(8,128)(2,1)} %bitcast.53, bf16[832,2304]{1,0:T(8,128)(2,1)} %bitcast.45, bf16[832,768]{1,0:T(8,128)(2,1)} %bitcast.54, bf16[832,768]{1,0:T(8,128)(2,1)} %bitcast.57, bf16[832,768]{1,0:T(8,128)(2,1)} %bitcast.55, ...), custom_call_target="tpu_custom_call" | custom-call | tf_op jit(solution)/shard_map/gradients1/pallas_call | solution.py:1089
  277.6 25.2 %gradients0.1 = bf16[2,48,384,384]{3,2,1,0:T(8,128)(2,1)} custom-call(s32[49]{0:T(128)} %pad_add_fusion.meta, bf16[832,768]{1,0:T(8,128)(2,1)} %bitcast.48, bf16[832,2304]{1,0:T(8,128)(2,1)} %bitcast.44, bf16[832,768]{1,0:T(8,128)(2,1)} %bitcast.49, bf16[832,768]{1,0:T(8,128)(2,1)} %bitcast.52, ...), custom_call_target="tpu_custom_call", output_to_operand_aliasing={{}: (9, {})} | custom-call | tf_op jit(solution)/shard_map/gradients0/pallas_call | solution.py:1089
  302.8 0.2 fusion.5
  303.0 0.2 compare_reduce_fusion
  303.2 0.7 fusion.4.live_ref
  303.9 0.0 copy-start.1
  303.9 0.0 copy-start.4
  303.9 0.0 copy-start.5
  303.9 0.0 copy-start.2
  303.9 0.0 copy-start.3
  303.9 123.3 %reduce_gradients.1 = (f32[1152,384]{1,0:T(8,128)}, f32[32,768]{1,0:T(8,128)}, f32[8,128]{1,0:T(8,128)}, f32[8,197,768]{2,1,0:T(8,128)}, f32[8,197,768]{2,1,0:T(8,128)}) custom-call(bf16[2,18432,384]{2,1,0:T(8,128)(2,1)} %bitcast.36, f32[32,768]{1,0:T(8,128)} %bitcast.58, ...), custom_call_target="tpu_custom_call", output_to_operand_aliasing={{3}: (3, {}), {4}: (4, {})} | custom-call | tf_op jit(solution)/shard_map/reduce_gradients/pallas_call | solution.py:1002
  427.2 0.9 fusion.8
  428.1 1.8 sqrt_bitcast_fusion
  430.7 0.0 copy-done.1
  430.7 0.0 copy-done.4
  430.7 0.0 copy-done.5
  430.7 0.7 multiply_subtract_fusion.1
  431.4 0.0 copy-done.2
  431.4 0.0 copy-done.3
  431.4 0.7 multiply_subtract_fusion
  432.1 0.5 convert_element_type.7.live_ref
  432.6 9.0 %adam.1 = (f32[3,1,384,384]{3,2,1,0:T(8,128)}, f32[3,1,384,384]{3,2,1,0:T(8,128)}, f32[3,1,384,384]{3,2,1,0:T(8,128)}) custom-call(s32[3]{0:T(128)} %convert_element_type.7.live_ref, f32[8,128]{1,0:T(8,128)} %get-tuple-element.69.square_ref, f32[3,384,384]{2,1,0:T(8,128)} %bitcast.47, f32[3,1,384,384]{3,2,1,0:T(8,128)} %w_ref.1, f32[3,1,384,384]{3,2,1,0:T(8,128)} %l_ref.1, ...), custom_call_target="tpu_custom_call" | custom-call | tf_op jit(solution)/shard_map/adam/pallas_call | solution.py:1104
  441.6 6.2 %copy.41 = f32[8,197,768]{2,0,1:T(8,128)} copy(f32[8,197,768]{2,1,0:T(8,128)} %get-tuple-element.88) | data formatting | bytes 9682944
  447.8 6.2 %copy.42 = f32[8,197,768]{2,0,1:T(8,128)} copy(f32[8,197,768]{2,1,0:T(8,128)} %get-tuple-element.89) | data formatting | bytes 9682944
  (3 shorter events, 0.0 us)
Async XLA Ops:
  2.0 116.7 %copy-start.6 = (s32[48]{0:T(128)S(1)}, s32[48]{0:T(128)}, u32[]{:S(2)}) copy-start(s32[48]{0:T(128)} %param.18) | copy-start | bytes 580
  2.0 117.4 %copy-start = (f32[2,6,768]{2,0,1:T(2,128)S(1)}, f32[2,6,768]{2,0,1:T(2,128)}, u32[]{:S(2)}) copy-start(f32[2,6,768]{2,0,1:T(2,128)} %param.24) | copy-start | bytes 110596
  303.9 126.8 %copy-start.1 = (f32[2,6,384]{2,0,1:T(2,128)S(1)}, f32[2,6,384]{2,0,1:T(2,128)}, u32[]{:S(2)}) copy-start(f32[2,6,384]{2,0,1:T(2,128)} %param.27) | copy-start | bytes 55300
  303.9 126.8 %copy-start.4 = (f32[2,6,384]{2,0,1:T(2,128)S(1)}, f32[2,6,384]{2,0,1:T(2,128)}, u32[]{:S(2)}) copy-start(f32[2,6,384]{2,0,1:T(2,128)} %param.28) | copy-start | bytes 55300
  303.9 126.8 %copy-start.5 = (f32[2,6,384]{2,0,1:T(2,128)S(1)}, f32[2,6,384]{2,0,1:T(2,128)}, u32[]{:S(2)}) copy-start(f32[2,6,384]{2,0,1:T(2,128)} %param.29) | copy-start | bytes 55300
  303.9 127.5 %copy-start.2 = (f32[2,6,768]{2,0,1:T(2,128)S(1)}, f32[2,6,768]{2,0,1:T(2,128)}, u32[]{:S(2)}) copy-start(f32[2,6,768]{2,0,1:T(2,128)} %param.25) | copy-start | bytes 110596
  303.9 127.5 %copy-start.3 = (f32[2,6,768]{2,0,1:T(2,128)S(1)}, f32[2,6,768]{2,0,1:T(2,128)}, u32[]{:S(2)}) copy-start(f32[2,6,768]{2,0,1:T(2,128)} %param.26) | copy-start | bytes 110596

commit v5 on v4

--- a/solution.py
+++ b/solution.py
@@ -120,15 +120,24 @@
     return jnp.concatenate([jnp.where(m, value, zero) for m in masks], axis=0)
 
 
-SAVED = ("a", "mixed", "c", "act", "dyr", "du", "dhr", "dqkv")
+def saved_columns(width, ratio):
+    left = (("a", 1), ("mixed", 1), ("c", 1), ("act", ratio))
+    right = (("dqkv", 3), ("dhr", 1), ("du", ratio), ("dyr", 1))
+    table = {}
+    for side, names in enumerate((left, right)):
+        start = 0
+        for name, size in names:
+            table[name] = (side, start * width, size * width)
+            start += size
+    return table, (3 + ratio) * width, (5 + ratio) * width
 
 
 def layers_kernel(layer_count, seq, rows, keys, meta, x_ref, dy_ref, hits_ref, shared_ref, split_ref, blocks, *rest):
-    outs = rest[: 8 * layer_count]
-    y_ref, dx_ref, vec_ref = rest[8 * layer_count : 8 * layer_count + 3]
-    rest = rest[8 * layer_count + 3 :]
-    saves = rest[: 8 * layer_count]
-    rest = rest[8 * layer_count :]
+    outs = rest[:2]
+    y_ref, dx_ref, vec_ref = rest[2:5]
+    rest = rest[5:]
+    saves = rest[: 2 * layer_count]
+    rest = rest[2 * layer_count :]
     weights = [rest[4 * n : 4 * n + 4] for n in range(layer_count)]
     rest = rest[4 * layer_count :]
     holds = [rest[7 * n : 7 * n + 7] for n in range(layer_count)]
@@ -141,24 +150,25 @@
     zero = jnp.zeros((), BF16)
     masks = head_masks()
 
-    def saving(layer, name, i):
-        n = layer * 8 + SAVED.index(name)
-        return pltpu.make_async_copy(saves[n], outs[n].at[i], save_sems.at[n])
-
-    def free(names):
+    columns, _, _ = saved_columns(width, ratio)
+
+    def saving(layer, side, i):
+        n = 2 * layer + side
+        return pltpu.make_async_copy(saves[n], outs[side].at[layer, i], save_sems.at[n])
+
+    def free(side):
         @pl.when(step > 0)
         def _():
             for n in range(layer_count):
-                for name in names:
-                    saving(n, name, step - 1).wait()
-
-    def send(names):
+                saving(n, side, step - 1).wait()
+
+    def send(side):
         for n in range(layer_count):
-            for name in names:
-                saving(n, name, step).start()
+            saving(n, side, step).start()
 
     def buffer(layer, name):
-        return saves[layer * 8 + SAVED.index(name)]
+        side, start, size = columns[name]
+        return saves[2 * layer + side].at[:, pl.ds(start, size)]
 
     jobs = [
         weight_copies(meta, n, blocks, *weights[n], weight_sems.at[n]) for n in range(layer_count)
@@ -187,7 +197,7 @@
             for ref in (hold[3], hold[4]):
                 ref[rows:keys, :] = jnp.zeros((keys - rows, width), BF16)
 
-    free(SAVED[:4])
+    free(0)
     holds[0][0][...] = x_ref[0].astype(F32)
     real = lax.broadcasted_iota(jnp.int32, (1, keys), 1) < seq
     for n in range(layer_count):
@@ -242,8 +252,8 @@
         else:
             y_ref[0] = y[0:seq, :]
 
-    send(SAVED[:4])
-    free(SAVED[4:])
+    send(0)
+    free(1)
     wanted = lax.broadcasted_iota(jnp.int32, (rows, 1), 0)
     hit = jnp.max(jnp.where(hits_ref[0] + 1 == wanted, 1.0, 0.0), axis=-1, keepdims=True)
     dy = dy_ref[0] * hit
@@ -302,13 +312,13 @@
         collect(1, da)
         dy = dh + norm_back(da, unit, inverse, shared_ref[n, 0:1, :])
     dx_ref[0] = dy[0:seq, :]
-    send(SAVED[4:])
+    send(1)
 
     @pl.when(step == pl.num_programs(0) - 1)
     def _():
         for n in range(layer_count):
-            for name in SAVED:
-                saving(n, name, step).wait()
+            for side in range(2):
+                saving(n, side, step).wait()
 
 
 def run_layers(count, seq, rows, keys, meta, place, stream, seed, hits, shared, split, blocks):
@@ -316,9 +326,9 @@
     ratio = split.shape[1] - 2
     heads = width // DH
     sd = jax.ShapeDtypeStruct
-    widths = [width, width, width, ratio * width, width, ratio * width, width, 3 * width] * layer_count
+    _, *widths = saved_columns(width, ratio)
     anyspace = pl.BlockSpec(memory_space=pl.ANY)
-    outs = [sd((count, rows, w), BF16) for w in widths]
+    outs = [sd((layer_count, count, rows, w), BF16) for w in widths]
     outs += [sd((2 * count, seq, width), F32)] * 2 + [sd((layer_count, 16, width), F32)]
     image = pl.BlockSpec((1, seq, width), lambda i, meta: (meta[place] * count + i, 0, 0))
 
@@ -329,7 +339,7 @@
         return pl.BlockSpec(tuple(shape), lambda i, meta: (0,) * len(shape))
 
     vmem = pltpu.VMEM
-    scratch = [vmem((rows, w), BF16) for w in widths]
+    scratch = [vmem((rows, w), BF16) for w in widths] * layer_count
     scratch += [
         vmem((width, 3 * width), BF16),
         vmem((width, width), BF16),
@@ -346,7 +356,7 @@
         vmem((rows, ratio * width), BF16),
     ] * layer_count
     scratch += [
-        pltpu.SemaphoreType.DMA((8 * layer_count,)),
+        pltpu.SemaphoreType.DMA((2 * layer_count,)),
         pltpu.SemaphoreType.DMA((layer_count, 4)),
     ]
     grid = pltpu.PrefetchScalarGridSpec(
@@ -370,37 +380,39 @@
         compiler_params=params(),
         name="layers",
     )(meta, stream, seed, hits, shared, split, blocks)
-    kept = [dict(zip(SAVED, res[8 * n : 8 * n + 8])) for n in range(layer_count)]
-    return kept, res[8 * layer_count], res[8 * layer_count + 1], res[8 * layer_count + 2]
-
-
-def gradient_kernel(
-    layer, pieces, ratio, meta, a_ref, dqkv_ref, mixed_ref, dhr_ref, c_ref, du_ref, act_ref,
-    dyr_ref, *rest,
-):
-    out_ref, turned, stage, sems = rest[-4:]
+    return res
+
+
+def gradient_step(s, ratio):
+    steps = 4 + 2 * ratio
+    q = s % steps
+    left = jnp.where(q < 3, 0, jnp.where(q < 4, 1, jnp.where(q < 4 + ratio, 2, q - 1 - ratio)))
+    right = jnp.minimum(q, 4 + ratio)
+    return s // steps, q, left, right
+
+
+def gradient_kernel(pieces, ratio, meta, left_ref, right_ref, out_ref, turned, stage, sems):
     side = out_ref.shape[-1]
-    shares = out_ref.shape[0]
     step = pl.program_id(0)
-    last = pl.num_programs(0) - 1
-    start_up = 4
-    start_down = 4 + ratio
+    layer, q, _, _ = gradient_step(step, ratio)
     base = layer * pieces * (4 + 2 * ratio)
     slot = step % 2
-
-    def saves(buffer, place):
-        out = []
-        for i in range(pieces):
-            for j in range(pieces):
-                block, share = place(i, j)
-                out.append(
-                    pltpu.make_async_copy(
-                        stage.at[buffer, pl.ds(i * side, side), pl.ds(j * side, side)],
-                        out_ref.at[share, meta[base + block]],
-                        sems.at[buffer],
-                    )
-                )
-        return out
+    by_rows = (q == 3) | (q >= 4 + ratio)
+
+    def block_of(i, j):
+        return base + jnp.where(
+            q < 3,
+            i * 3 + q,
+            jnp.where(
+                q < 4,
+                3 * pieces + j,
+                jnp.where(
+                    q < 4 + ratio,
+                    4 * pieces + i * ratio + q - 4,
+                    (4 + ratio) * pieces + (q - 4 - ratio) * pieces + j,
+                ),
+            ),
+        )
 
     def drain(buffer):
         pltpu.make_async_copy(stage.at[buffer], stage.at[buffer], sems.at[buffer]).wait()
@@ -409,43 +421,20 @@
     def _():
         drain(slot)
 
-    def work(lhs_ref, rhs_ref, first, place):
-        if first is None:
-            lhs = lhs_ref[...].T
-        else:
-
-            @pl.when(first)
-            def _():
-                turned[...] = lhs_ref[...].T
-
-            lhs = turned[...]
-        stage[slot] = nn(lhs, rhs_ref[...]).astype(BF16)
-        for save in saves(slot, place):
-            save.start()
-
-    @pl.when(step < 3)
+    @pl.when((q == 0) | ((q >= 3) & (q <= 4)) | (q >= 4 + ratio))
     def _():
-        work(a_ref, dqkv_ref, step == 0, lambda i, j: (i * 3 + step, j))
-
-    @pl.when(step == 3)
-    def _():
-        work(mixed_ref, dhr_ref, None, lambda i, j: (3 * pieces + j, i))
-
-    @pl.when((step >= start_up) & (step < start_down))
-    def _():
-        work(
-            c_ref, du_ref, step == start_up,
-            lambda i, j: (4 * pieces + i * ratio + step - start_up, j),
-        )
-
-    @pl.when(step >= start_down)
-    def _():
-        work(
-            act_ref, dyr_ref, None,
-            lambda i, j: ((4 + ratio) * pieces + (step - start_down) * pieces + j, i),
-        )
-
-    @pl.when(step == last)
+        turned[...] = left_ref[0].T
+
+    stage[slot] = nn(turned[...], right_ref[0]).astype(BF16)
+    for i in range(pieces):
+        for j in range(pieces):
+            pltpu.make_async_copy(
+                stage.at[slot, pl.ds(i * side, side), pl.ds(j * side, side)],
+                out_ref.at[jnp.where(by_rows, i, j), meta[block_of(i, j)]],
+                sems.at[slot],
+            ).start()
+
+    @pl.when(step == pl.num_programs(0) - 1)
     def _():
         drain(1 - slot)
         drain(slot)
@@ -875,37 +864,43 @@
             total = total + tile_pieces[riding.index(j)]
         tiles[at] = total
 
-    hops = []
-    for d in (2, 1, 0):
-        reach = 1
-        while reach < sizes[d]:
-            bit = place.at[d] // reach % 2
-            there = place.at[d] + reach * (1 - 2 * bit)
-            coords = [there if e == d else place.at[e] for e in range(3)]
-            stride = (sizes[1] * sizes[2], sizes[2], 1)[d]
-            low = dp // (stride * reach) * (stride * reach)
-            hops.append(((coords[0] * sizes[1] + coords[1]) * sizes[2] + coords[2], tp, stride * reach, low))
-            reach *= 2
-
-    def hop_copy(k):
-        far_dp, far_tp, span, low = hops[k]
-        region = full.at[:, pl.ds(low, span)]
+    plane = sizes[1] * sizes[2]
+    peers = [
+        (oy, ox, ot)
+        for oy in range(sizes[1])
+        for ox in range(sizes[2])
+        for ot in range(2)
+        if (oy, ox, ot) != (0, 0, 0)
+    ]
+
+    def peer(offsets, sign):
+        oy, ox, ot = offsets
+        return place.shifted((0, sign * oy, sign * ox)), (1 - tp if ot else tp)
+
+    def plane_copy(k, sign):
+        far_dp, far_tp = peer(peers[k], sign)
+        region = full.at[tp, dp] if sign > 0 else full.at[far_tp, far_dp]
         return remote(region, region, hop_send.at[k], hop_recv.at[k], far_dp, far_tp)
 
-    def hop_arrival(k):
-        far_dp, far_tp, span, low = hops[k]
-        region = full.at[:, pl.ds(far_dp // span * span, span)]
-        return remote(region, region, hop_send.at[k], hop_recv.at[k], far_dp, far_tp)
-
-    def swap_copy(share):
-        region = full.at[share, dp]
-        return remote(region, region, hop_send.at[len(hops)], hop_recv.at[len(hops)], dp, 1 - tp)
+    def line_copy(k, sign):
+        n = len(peers) + k - 1
+        far_dp = place.along(0, sign * k)
+        held = dp if sign > 0 else far_dp
+        region = full.at[:, pl.ds(held // plane * plane, plane)]
+        return remote(region, region, hop_send.at[n], hop_recv.at[n], far_dp, tp)
 
     tiles[...] = jnp.zeros_like(tiles)
     for r in range(vec_ref.shape[0]):
         for i in range(chunks):
             tiles[r, i : i + 1, :] = vec_ref[r : r + 1, i * lanes : (i + 1) * lanes]
-    greet(place)
+    barrier = pltpu.get_barrier_semaphore()
+    for far_dp, far_tp in [peer(p, 1) for p in peers] + [
+        (place.along(0, k), tp) for k in range(1, sizes[0])
+    ]:
+        pl.semaphore_signal(
+            barrier, inc=1, device_id=(far_dp, far_tp), device_id_type=pl.DeviceIdType.MESH
+        )
+    pl.semaphore_wait(barrier, len(peers) + sizes[0] - 1)
     tile_over().start()
     for item in order_used:
         loading(item).start()
@@ -950,11 +945,14 @@
     tile_combine((1, (0, 0, 0)))
     full[tp, dp] = tiles[tp * dp_count + dp]
     full[tp, dp, square_row : square_row + 1, :] = squares
-    swap_copy(tp).start()
-    swap_copy(1 - tp).wait_recv()
-    for k in range(len(hops)):
-        hop_copy(k).start()
-        hop_arrival(k).wait_recv()
+    for k in range(len(peers)):
+        plane_copy(k, 1).start()
+    for k in range(len(peers)):
+        plane_copy(k, -1).wait_recv()
+    for k in range(1, sizes[0]):
+        line_copy(k, 1).start()
+    for k in range(1, sizes[0]):
+        line_copy(k, -1).wait_recv()
     total = full[0, 0]
     for n in range(1, 2 * dp_count):
         total = total + full[n // dp_count, n % dp_count]
@@ -976,9 +974,10 @@
     tile_over().wait_send()
     for i in riding:
         tile_sending(i).wait_send()
-    swap_copy(tp).wait_send()
-    for k in range(len(hops)):
-        hop_copy(k).wait_send()
+    for k in range(len(peers)):
+        plane_copy(k, 1).wait_send()
+    for k in range(1, sizes[0]):
+        line_copy(k, 1).wait_send()
     for n, ref in enumerate((block_out, grad_out)):
         image_copy(n, ref, tp).wait_send()
         image_copy(n, ref, 1 - tp).wait_recv()
@@ -991,7 +990,7 @@
     target = target.reshape(2, dp_count * rows, side)
     parts = part_table(sizes, rows)
     plan = gather_plan(sizes, parts)
-    hops = 1 + sum(n.bit_length() - 1 for n in sizes)
+    hops = 2 * sizes[1] * sizes[2] + sizes[0] - 2
     riding = sum(1 for p, _, _ in plan if p == 1)
     units = 3 * dp_count
     landing = sum(parts[p][2] for p, _, _ in plan)
@@ -1048,37 +1047,24 @@
     return pltpu.CompilerParams(vmem_limit_bytes=VMEM_LIMIT, dimension_semantics=("arbitrary",))
 
 
-def layer_gradients(layer, meta, kept, target, slot_total, side, share_count):
-    names = ("a", "dqkv", "mixed", "dhr", "c", "du", "act", "dyr")
-    ops = [kept[name].reshape(-1, kept[name].shape[-1]) for name in names]
-    tokens, width = ops[0].shape
-    ratio = ops[5].shape[1] // width
-    pieces = width // side
-
-    def clip(s, low, count):
-        return jnp.minimum(jnp.maximum(s - low, 0), count - 1)
-
-    block = (tokens, width)
-    maps = [
-        lambda s, meta: (0, 0),
-        lambda s, meta: (0, clip(s, 0, 3)),
-        lambda s, meta: (0, 0),
-        lambda s, meta: (0, 0),
-        lambda s, meta: (0, 0),
-        lambda s, meta: (0, clip(s, 4, ratio)),
-        lambda s, meta: (0, clip(s, 4 + ratio, ratio)),
-        lambda s, meta: (0, 0),
-    ]
-    in_specs = [pl.BlockSpec(block, index) for index in maps]
-    alias = {}
-    if target is not None:
-        in_specs.append(pl.BlockSpec(memory_space=pl.ANY))
-        ops.append(target)
-        alias = {len(ops): 0}
+def weight_gradients(meta, left, right, width, slot_total, side, share_count):
+    layer_count, count, rows, _ = left.shape
+    tokens = count * rows
+    ratio = left.shape[3] // width - 3
+    block = (1, tokens, width)
+
+    def left_map(s, meta):
+        layer, _, at, _ = gradient_step(s, ratio)
+        return (layer, 0, at)
+
+    def right_map(s, meta):
+        layer, _, _, at = gradient_step(s, ratio)
+        return (layer, 0, at)
+
     grid = pltpu.PrefetchScalarGridSpec(
         num_scalar_prefetch=1,
-        grid=(4 + 2 * ratio,),
-        in_specs=in_specs,
+        grid=(layer_count * (4 + 2 * ratio),),
+        in_specs=[pl.BlockSpec(block, left_map), pl.BlockSpec(block, right_map)],
         out_specs=pl.BlockSpec(memory_space=pl.ANY),
         scratch_shapes=[
             pltpu.VMEM((width, tokens), BF16),
@@ -1087,13 +1073,12 @@
         ],
     )
     return pl.pallas_call(
-        functools.partial(gradient_kernel, layer, pieces, ratio),
+        functools.partial(gradient_kernel, width // side, ratio),
         grid_spec=grid,
         out_shape=jax.ShapeDtypeStruct((share_count, slot_total, side, side), BF16),
-        input_output_aliases=alias,
         compiler_params=params(),
-        name=f"gradients{layer}",
-    )(meta, *ops)
+        name="gradients",
+    )(meta, left.reshape(layer_count, tokens, -1), right.reshape(layer_count, tokens, -1))
 
 
 def adam(layer_count, step_rate, live, squares, gradient, weight, left, right, first, second):
@@ -1164,12 +1149,10 @@
     split_all = jnp.concatenate([split_pair[t] for t in range(tp_count)], axis=2)
     hits = mask_patches[:, None, :]
 
-    kept, output_own, grad_own, vectors = run_layers(
+    left, right, output_own, grad_own, vectors = run_layers(
         count, seq, rows, keys, meta, place, stream, seed, hits, shared_vectors, split_all, blocks
     )
-    target = None
-    for layer in reversed(range(layer_count)):
-        target = layer_gradients(layer, meta, kept[layer], target, slot_total, side, tp_count)
+    target = weight_gradients(meta, left, right, width, slot_total, side, tp_count)
     mine_ids = dp_rank * slot_count + jnp.arange(slot_count, dtype=jnp.int32)
     matches = slot_index[None, :] == mine_ids[:, None]
     live = jnp.any(matches, axis=1)

time: 459 us -> 430 us (0.937)
  Pallas kernels: 430 us -> 406 us
    pallas_call x1, Pallas kernels: 133 us -> 117 us  [run_layers(): pl.pallas_call(functools.partial(layers_kernel, layer_count, seq, rows, k...]
    pallas_call x1, Pallas kernels: 123 us -> 118 us  [reduce_gradients(): pl.pallas_call(functools.partial(reduce_kernel, sizes, parts, plan, layer...]
    pallas_call x2 -> x1, Pallas kernels: 50.2 us -> 47.2 us  [weight_gradients(): pl.pallas_call(functools.partial(gradient_kernel, width // side, ratio),...]
    unnamed x18 -> x22, local copies, waits for them, and re-layouts: 14.3 us -> 12 us
where the time goes in v5:
time: 430 us; the launch traced here: 429 us
  Pallas kernels  406 us (94%)
  local copies, waits for them, and re-layouts  13.7 us (3%)
  other arithmetic  6.19 us (1%)
    pallas_call x1, Pallas kernels, reduce_gradients(): pl.pallas_call(functools.partial(reduce_kernel, sizes, parts, plan, layer...  118 us
    pallas_call x1, Pallas kernels, run_layers(): pl.pallas_call(functools.partial(layers_kernel, layer_count, seq, rows, k...  117 us
    pallas_call x1, Pallas kernels, gather_weights(): pl.pallas_call(functools.partial(gather_kernel, sizes, parts, plan), in_s...  115 us
    pallas_call x1, Pallas kernels, weight_gradients(): pl.pallas_call(functools.partial(gradient_kernel, width // side, ratio),...  47.2 us
    unnamed x22, local copies, waits for them, and re-layouts  12 us
    pallas_call x1, Pallas kernels, adam(): pl.pallas_call(functools.partial(adam_kernel, layer_count, step_rate), gr...  8.96 us

profile of v5, /device:TPU:0, one launch (start us, length us, event | category | flops | bytes accessed | tf_op | source)
XLA Modules:
  0.0 429.0 jit_solution(14200514828953441705)
XLA Ops:
  0.6 1.3 copy.36.split_ref
  2.0 0.0 copy-start.6
  2.0 0.0 copy-start
  2.0 115.2 %gather_weights.1 = (bf16[2,18432,384]{2,1,0:T(8,128)(2,1)}, f32[2,2,6,384]{3,2,1,0:T(8,128)}, bf16[4,208,768]{2,1,0:T(8,128)(2,1)}, f32[4,208,768]{2,1,0:T(8,128)}) custom-call(f32[1152,384]{1,0:T(8,128)} %bitcast.28, f32[2,6,384]{2,1,0:T(8,128)} %copy.36.split_ref, bf16[1576,768]{1,0:T(8,128)(2,1)} %bitcast.30, f32[1576,768]{1,0:T(8,128)} %bitcast.29), custom_call_target="tpu_custom_call" | custom-call | tf_op jit(solution)/shard_map/gather_weights/pallas_call | solution.py:721
  117.2 0.8 slice_bitcast_fusion.1
  118.0 0.6 pad_maximum_fusion.split_ref
  118.6 0.0 copy-done.6
  118.6 0.2 convert_reduce_fusion
  118.8 0.6 pad_add_fusion.meta
  119.4 0.0 copy-done
  119.4 0.6 copy.37.shared_ref
  120.0 117.5 %layers.1 = (bf16[2,4,208,5376]{3,2,1,0:T(8,128)(2,1)}, bf16[2,4,208,6912]{3,2,1,0:T(8,128)(2,1)}, f32[8,197,768]{2,1,0:T(8,128)}, f32[8,197,768]{2,1,0:T(8,128)}, f32[2,16,768]{2,1,0:T(8,128)}) custom-call(s32[49]{0:T(128)} %pad_add_fusion.meta, bf16[4,208,768]{2,1,0:T(8,128)(2,1)} %get-tuple-element.30.x_ref, f32[4,208,768]{2,1,0:T(8,128)} %get-tuple-element.31.dy_ref, ...), custom_call_target="tpu_custom_call" | custom-call | tf_op jit(solution)/shard_map/layers/pallas_call | solution.py:376
  237.5 47.2 %gradients.1 = bf16[2,48,384,384]{3,2,1,0:T(8,128)(2,1)} custom-call(s32[49]{0:T(128)} %pad_add_fusion.meta, bf16[2,832,5376]{2,1,0:T(8,128)(2,1)} %bitcast.27, bf16[2,832,6912]{2,1,0:T(8,128)(2,1)} %bitcast.24), custom_call_target="tpu_custom_call" | custom-call | tf_op jit(solution)/shard_map/gradients/pallas_call | solution.py:1075
  284.8 0.2 fusion.5
  284.9 0.2 compare_reduce_fusion
  285.1 0.7 fusion.4.live_ref
  285.8 0.0 copy-start.1
  285.8 0.0 copy-start.4
  285.8 0.0 copy-start.5
  285.8 0.0 copy-start.2
  285.8 0.0 copy-start.3
  285.8 117.6 %reduce_gradients.1 = (f32[1152,384]{1,0:T(8,128)}, f32[32,768]{1,0:T(8,128)}, f32[8,128]{1,0:T(8,128)}, f32[8,197,768]{2,1,0:T(8,128)}, f32[8,197,768]{2,1,0:T(8,128)}) custom-call(bf16[2,18432,384]{2,1,0:T(8,128)(2,1)} %bitcast.22, f32[32,768]{1,0:T(8,128)} %bitcast.32, ...), custom_call_target="tpu_custom_call", output_to_operand_aliasing={{3}: (3, {}), {4}: (4, {})} | custom-call | tf_op jit(solution)/shard_map/reduce_gradients/pallas_call | solution.py:1001
  403.4 0.9 fusion.8
  404.4 1.8 sqrt_bitcast_fusion
  406.9 0.0 copy-done.1
  406.9 0.0 copy-done.4
  406.9 0.0 copy-done.5
  406.9 0.7 multiply_subtract_fusion.1
  407.6 0.0 copy-done.2
  407.6 0.0 copy-done.3
  407.6 0.7 multiply_subtract_fusion
  408.4 0.5 convert_element_type.7.live_ref
  408.9 9.0 %adam.1 = (f32[3,1,384,384]{3,2,1,0:T(8,128)}, f32[3,1,384,384]{3,2,1,0:T(8,128)}, f32[3,1,384,384]{3,2,1,0:T(8,128)}) custom-call(s32[3]{0:T(128)} %convert_element_type.7.live_ref, f32[8,128]{1,0:T(8,128)} %get-tuple-element.41.square_ref, f32[3,384,384]{2,1,0:T(8,128)} %bitcast.31, f32[3,1,384,384]{3,2,1,0:T(8,128)} %w_ref.1, f32[3,1,384,384]{3,2,1,0:T(8,128)} %l_ref.1, ...), custom_call_target="tpu_custom_call" | custom-call | tf_op jit(solution)/shard_map/adam/pallas_call | solution.py:1089
  417.8 0.0 slice-start
  417.9 0.0 slice-start.1
  417.9 6.3 %copy.40 = f32[8,197,768]{2,0,1:T(8,128)} copy(f32[8,197,768]{2,1,0:T(8,128)} %get-tuple-element.60) | data formatting | bytes 9682944
  424.2 0.0 slice-done
  424.2 0.0 slice-done.1
  424.2 3.7 copy.41
  (4 shorter events, 0.0 us)
Async XLA Ops:
  2.0 116.6 %copy-start.6 = (s32[48]{0:T(128)S(1)}, s32[48]{0:T(128)}, u32[]{:S(2)}) copy-start(s32[48]{0:T(128)} %param.18) | copy-start | bytes 580
  2.0 117.4 %copy-start = (f32[2,6,768]{2,0,1:T(2,128)S(1)}, f32[2,6,768]{2,0,1:T(2,128)}, u32[]{:S(2)}) copy-start(f32[2,6,768]{2,0,1:T(2,128)} %param.24) | copy-start | bytes 110596
  285.8 121.1 %copy-start.1 = (f32[2,6,384]{2,0,1:T(2,128)S(1)}, f32[2,6,384]{2,0,1:T(2,128)}, u32[]{:S(2)}) copy-start(f32[2,6,384]{2,0,1:T(2,128)} %param.27) | copy-start | bytes 55300
  285.8 121.1 %copy-start.4 = (f32[2,6,384]{2,0,1:T(2,128)S(1)}, f32[2,6,384]{2,0,1:T(2,128)}, u32[]{:S(2)}) copy-start(f32[2,6,384]{2,0,1:T(2,128)} %param.28) | copy-start | bytes 55300
  285.8 121.1 %copy-start.5 = (f32[2,6,384]{2,0,1:T(2,128)S(1)}, f32[2,6,384]{2,0,1:T(2,128)}, u32[]{:S(2)}) copy-start(f32[2,6,384]{2,0,1:T(2,128)} %param.29) | copy-start | bytes 55300
  285.8 121.8 %copy-start.2 = (f32[2,6,768]{2,0,1:T(2,128)S(1)}, f32[2,6,768]{2,0,1:T(2,128)}, u32[]{:S(2)}) copy-start(f32[2,6,768]{2,0,1:T(2,128)} %param.25) | copy-start | bytes 110596
  285.8 121.8 %copy-start.3 = (f32[2,6,768]{2,0,1:T(2,128)S(1)}, f32[2,6,768]{2,0,1:T(2,128)}, u32[]{:S(2)}) copy-start(f32[2,6,768]{2,0,1:T(2,128)} %param.26) | copy-start | bytes 110596
  417.8 6.4 %slice-start = ((s8[4915200]{0:T(1024)(128)(4,1)}), s8[4194304]{0:T(1024)(128)(4,1)S(1)}, s32[]{:S(2)}) async-start(s8[4915200]{0:T(1024)(128)(4,1)} %bitcast.25), calls=%async_computation | async-start | bytes 8388608
  417.9 6.3 %slice-start.1 = ((s8[4915200]{0:T(1024)(128)(4,1)}), s8[720896]{0:T(1024)(128)(4,1)S(1)}, s32[]{:S(2)}) async-start(s8[4915200]{0:T(1024)(128)(4,1)} %bitcast.25), calls=%async_computation.1 | async-start | bytes 1441792

commit v6 on v5

--- a/solution.py
+++ b/solution.py
@@ -118,6 +118,10 @@
 def spread_heads(masks, value):
     zero = jnp.zeros((), value.dtype)
     return jnp.concatenate([jnp.where(m, value, zero) for m in masks], axis=0)
+
+
+def beside(stack, rows):
+    return jnp.concatenate([stack[h * rows : (h + 1) * rows, :] for h in range(GROUP)], axis=1)
 
 
 def saved_columns(width, ratio):
@@ -223,10 +227,7 @@
             probs = (power * (1.0 / total)).astype(BF16)
             ps[g * GROUP * rows : (g + 1) * GROUP * rows, :] = probs
             v4 = vs[:, cols]
-            mix = None
-            for h in range(GROUP):
-                part = nn(probs[h * rows : (h + 1) * rows, :], jnp.where(masks[h], v4, zero))
-                mix = part if mix is None else mix + part
+            mix = nn(beside(probs, rows), spread_heads(masks, v4))
             mixed[:, cols] = mix.astype(BF16)
         if n == 0:
             ready([(0, 1), (0, 2), (0, 3)])
@@ -296,10 +297,7 @@
             ds = (both - wide * jnp.sum(both, axis=-1, keepdims=True)).astype(BF16)
             dv = tn(probs, dm)[0:rows, :].astype(BF16)
             dk = tn(ds, spread_heads(masks, qs[:, cols]))[0:rows, :].astype(BF16)
-            dq = None
-            for h in range(GROUP):
-                part = nn(ds[h * rows : (h + 1) * rows, :], jnp.where(masks[h], k4, zero))
-                dq = part if dq is None else dq + part
+            dq = nn(beside(ds, rows), spread_heads(masks, k4))
             back[:, cols] = (dq.astype(BF16).astype(F32) * scale).astype(BF16)
             back[:, width + g * LANES : width + (g + 1) * LANES] = dk
             back[:, 2 * width + g * LANES : 2 * width + (g + 1) * LANES] = dv
@@ -384,23 +382,21 @@
 
 
 def gradient_step(s, ratio):
-    steps = 4 + 2 * ratio
-    q = s % steps
-    left = jnp.where(q < 3, 0, jnp.where(q < 4, 1, jnp.where(q < 4 + ratio, 2, q - 1 - ratio)))
-    right = jnp.minimum(q, 4 + ratio)
-    return s // steps, q, left, right
-
-
-def gradient_kernel(pieces, ratio, meta, left_ref, right_ref, out_ref, turned, stage, sems):
+    left = jnp.where(s < 3, 0, jnp.where(s < 4, 1, jnp.where(s < 4 + ratio, 2, s - 1 - ratio)))
+    return left, jnp.minimum(s, 4 + ratio)
+
+
+def gradient_kernel(pieces, ratio, meta, left_ref, right_ref, out_ref, stage, sems):
     side = out_ref.shape[-1]
     step = pl.program_id(0)
-    layer, q, _, _ = gradient_step(step, ratio)
-    base = layer * pieces * (4 + 2 * ratio)
+    q = step
+    layer_count = left_ref.shape[0]
+    per_layer = pieces * (4 + 2 * ratio)
     slot = step % 2
     by_rows = (q == 3) | (q >= 4 + ratio)
 
     def block_of(i, j):
-        return base + jnp.where(
+        return jnp.where(
             q < 3,
             i * 3 + q,
             jnp.where(
@@ -421,18 +417,16 @@
     def _():
         drain(slot)
 
-    @pl.when((q == 0) | ((q >= 3) & (q <= 4)) | (q >= 4 + ratio))
-    def _():
-        turned[...] = left_ref[0].T
-
-    stage[slot] = nn(turned[...], right_ref[0]).astype(BF16)
-    for i in range(pieces):
-        for j in range(pieces):
-            pltpu.make_async_copy(
-                stage.at[slot, pl.ds(i * side, side), pl.ds(j * side, side)],
-                out_ref.at[jnp.where(by_rows, i, j), meta[block_of(i, j)]],
-                sems.at[slot],
-            ).start()
+    for n in range(layer_count):
+        stage[slot, n] = tn(left_ref[n], right_ref[n]).astype(BF16)
+    for n in range(layer_count):
+        for i in range(pieces):
+            for j in range(pieces):
+                pltpu.make_async_copy(
+                    stage.at[slot, n, pl.ds(i * side, side), pl.ds(j * side, side)],
+                    out_ref.at[jnp.where(by_rows, i, j), meta[n * per_layer + block_of(i, j)]],
+                    sems.at[slot],
+                ).start()
 
     @pl.when(step == pl.num_programs(0) - 1)
     def _():
@@ -1051,24 +1045,21 @@
     layer_count, count, rows, _ = left.shape
     tokens = count * rows
     ratio = left.shape[3] // width - 3
-    block = (1, tokens, width)
+    block = (layer_count, tokens, width)
 
     def left_map(s, meta):
-        layer, _, at, _ = gradient_step(s, ratio)
-        return (layer, 0, at)
+        return (0, 0, gradient_step(s, ratio)[0])
 
     def right_map(s, meta):
-        layer, _, _, at = gradient_step(s, ratio)
-        return (layer, 0, at)
+        return (0, 0, gradient_step(s, ratio)[1])
 
     grid = pltpu.PrefetchScalarGridSpec(
         num_scalar_prefetch=1,
-        grid=(layer_count * (4 + 2 * ratio),),
+        grid=(4 + 2 * ratio,),
         in_specs=[pl.BlockSpec(block, left_map), pl.BlockSpec(block, right_map)],
         out_specs=pl.BlockSpec(memory_space=pl.ANY),
         scratch_shapes=[
-            pltpu.VMEM((width, tokens), BF16),
-            pltpu.VMEM((2, width, width), BF16),
+            pltpu.VMEM((2, layer_count, width, width), BF16),
             pltpu.SemaphoreType.DMA((2,)),
         ],
     )

time: 430 us -> 434 us (level); the launches traced: 429 us -> 427 us
    pallas_call x1, Pallas kernels: 47.2 us -> 38.1 us  [weight_gradients(): pl.pallas_call(functools.partial(gradient_kernel, width // side, ratio),...]
    pallas_call x1, Pallas kernels: 117 us -> 124 us  [run_layers(): pl.pallas_call(functools.partial(layers_kernel, layer_count, seq, rows, k...]
where the time goes in v6:
time: 434 us; the launch traced here: 427 us
  Pallas kernels  404 us (93%)
  local copies, waits for them, and re-layouts  13.7 us (3%)
  other arithmetic  6.19 us (1%)
    pallas_call x1, Pallas kernels, run_layers(): pl.pallas_call(functools.partial(layers_kernel, layer_count, seq, rows, k...  124 us
    pallas_call x1, Pallas kernels, reduce_gradients(): pl.pallas_call(functools.partial(reduce_kernel, sizes, parts, plan, layer...  118 us
    pallas_call x1, Pallas kernels, gather_weights(): pl.pallas_call(functools.partial(gather_kernel, sizes, parts, plan), in_s...  115 us
    pallas_call x1, Pallas kernels, weight_gradients(): pl.pallas_call(functools.partial(gradient_kernel, width // side, ratio),...  38.1 us
    unnamed x22, local copies, waits for them, and re-layouts  12 us
    pallas_call x1, Pallas kernels, adam(): pl.pallas_call(functools.partial(adam_kernel, layer_count, step_rate), gr...  8.96 us

profile of v6, /device:TPU:0, one launch (start us, length us, event | category | flops | bytes accessed | tf_op | source)
XLA Modules:
  0.0 426.8 jit_solution(16192542395357657793)
XLA Ops:
  0.6 1.3 copy.36.split_ref
  2.0 0.0 copy-start.6
  2.0 0.0 copy-start
  2.0 115.2 %gather_weights.1 = (bf16[2,18432,384]{2,1,0:T(8,128)(2,1)}, f32[2,2,6,384]{3,2,1,0:T(8,128)}, bf16[4,208,768]{2,1,0:T(8,128)(2,1)}, f32[4,208,768]{2,1,0:T(8,128)}) custom-call(f32[1152,384]{1,0:T(8,128)} %bitcast.28, f32[2,6,384]{2,1,0:T(8,128)} %copy.36.split_ref, bf16[1576,768]{1,0:T(8,128)(2,1)} %bitcast.30, f32[1576,768]{1,0:T(8,128)} %bitcast.29), custom_call_target="tpu_custom_call" | custom-call | tf_op jit(solution)/shard_map/gather_weights/pallas_call | solution.py:715
  117.2 0.8 slice_bitcast_fusion.1
  118.0 0.6 pad_maximum_fusion.split_ref
  118.6 0.0 copy-done.6
  118.6 0.2 convert_reduce_fusion
  118.8 0.6 pad_add_fusion.meta
  119.4 0.0 copy-done
  119.4 0.6 copy.37.shared_ref
  120.0 124.3 %layers.1 = (bf16[2,4,208,5376]{3,2,1,0:T(8,128)(2,1)}, bf16[2,4,208,6912]{3,2,1,0:T(8,128)(2,1)}, f32[8,197,768]{2,1,0:T(8,128)}, f32[8,197,768]{2,1,0:T(8,128)}, f32[2,16,768]{2,1,0:T(8,128)}) custom-call(s32[49]{0:T(128)} %pad_add_fusion.meta, bf16[4,208,768]{2,1,0:T(8,128)(2,1)} %get-tuple-element.30.x_ref, f32[4,208,768]{2,1,0:T(8,128)} %get-tuple-element.31.dy_ref, ...), custom_call_target="tpu_custom_call" | custom-call | tf_op jit(solution)/shard_map/layers/pallas_call | solution.py:374
  244.3 38.1 %gradients.1 = bf16[2,48,384,384]{3,2,1,0:T(8,128)(2,1)} custom-call(s32[49]{0:T(128)} %pad_add_fusion.meta, bf16[2,832,5376]{2,1,0:T(8,128)(2,1)} %bitcast.27, bf16[2,832,6912]{2,1,0:T(8,128)(2,1)} %bitcast.24), custom_call_target="tpu_custom_call" | custom-call | tf_op jit(solution)/shard_map/gradients/pallas_call | solution.py:1066
  282.4 0.2 fusion.5
  282.6 0.2 compare_reduce_fusion
  282.7 0.7 fusion.4.live_ref
  283.4 0.0 copy-start.1
  283.4 0.0 copy-start.4
  283.4 0.0 copy-start.5
  283.4 0.0 copy-start.2
  283.4 0.0 copy-start.3
  283.4 117.6 %reduce_gradients.1 = (f32[1152,384]{1,0:T(8,128)}, f32[32,768]{1,0:T(8,128)}, f32[8,128]{1,0:T(8,128)}, f32[8,197,768]{2,1,0:T(8,128)}, f32[8,197,768]{2,1,0:T(8,128)}) custom-call(bf16[2,18432,384]{2,1,0:T(8,128)(2,1)} %bitcast.22, f32[32,768]{1,0:T(8,128)} %bitcast.32, ...), custom_call_target="tpu_custom_call", output_to_operand_aliasing={{3}: (3, {}), {4}: (4, {})} | custom-call | tf_op jit(solution)/shard_map/reduce_gradients/pallas_call | solution.py:995
  401.1 0.9 fusion.8
  402.0 1.8 sqrt_bitcast_fusion
  404.5 0.0 copy-done.1
  404.5 0.0 copy-done.4
  404.6 0.0 copy-done.5
  404.6 0.7 multiply_subtract_fusion.1
  405.2 0.0 copy-done.2
  405.2 0.0 copy-done.3
  405.2 0.7 multiply_subtract_fusion
  406.0 0.5 convert_element_type.7.live_ref
  406.5 9.0 %adam.1 = (f32[3,1,384,384]{3,2,1,0:T(8,128)}, f32[3,1,384,384]{3,2,1,0:T(8,128)}, f32[3,1,384,384]{3,2,1,0:T(8,128)}) custom-call(s32[3]{0:T(128)} %convert_element_type.7.live_ref, f32[8,128]{1,0:T(8,128)} %get-tuple-element.41.square_ref, f32[3,384,384]{2,1,0:T(8,128)} %bitcast.31, f32[3,1,384,384]{3,2,1,0:T(8,128)} %w_ref.1, f32[3,1,384,384]{3,2,1,0:T(8,128)} %l_ref.1, ...), custom_call_target="tpu_custom_call" | custom-call | tf_op jit(solution)/shard_map/adam/pallas_call | solution.py:1080
  415.5 0.0 slice-start
  415.5 0.0 slice-start.1
  415.5 6.3 %copy.40 = f32[8,197,768]{2,0,1:T(8,128)} copy(f32[8,197,768]{2,1,0:T(8,128)} %get-tuple-element.60) | data formatting | bytes 9682944
  421.8 0.0 slice-done
  421.8 0.0 slice-done.1
  421.8 3.7 copy.41
  (4 shorter events, 0.0 us)
Async XLA Ops:
  2.0 116.6 %copy-start.6 = (s32[48]{0:T(128)S(1)}, s32[48]{0:T(128)}, u32[]{:S(2)}) copy-start(s32[48]{0:T(128)} %param.18) | copy-start | bytes 580
  2.0 117.4 %copy-start = (f32[2,6,768]{2,0,1:T(2,128)S(1)}, f32[2,6,768]{2,0,1:T(2,128)}, u32[]{:S(2)}) copy-start(f32[2,6,768]{2,0,1:T(2,128)} %param.24) | copy-start | bytes 110596
  283.4 121.1 %copy-start.1 = (f32[2,6,384]{2,0,1:T(2,128)S(1)}, f32[2,6,384]{2,0,1:T(2,128)}, u32[]{:S(2)}) copy-start(f32[2,6,384]{2,0,1:T(2,128)} %param.27) | copy-start | bytes 55300
  283.4 121.1 %copy-start.4 = (f32[2,6,384]{2,0,1:T(2,128)S(1)}, f32[2,6,384]{2,0,1:T(2,128)}, u32[]{:S(2)}) copy-start(f32[2,6,384]{2,0,1:T(2,128)} %param.28) | copy-start | bytes 55300
  283.4 121.1 %copy-start.5 = (f32[2,6,384]{2,0,1:T(2,128)S(1)}, f32[2,6,384]{2,0,1:T(2,128)}, u32[]{:S(2)}) copy-start(f32[2,6,384]{2,0,1:T(2,128)} %param.29) | copy-start | bytes 55300
  283.4 121.8 %copy-start.2 = (f32[2,6,768]{2,0,1:T(2,128)S(1)}, f32[2,6,768]{2,0,1:T(2,128)}, u32[]{:S(2)}) copy-start(f32[2,6,768]{2,0,1:T(2,128)} %param.25) | copy-start | bytes 110596
  283.4 121.8 %copy-start.3 = (f32[2,6,768]{2,0,1:T(2,128)S(1)}, f32[2,6,768]{2,0,1:T(2,128)}, u32[]{:S(2)}) copy-start(f32[2,6,768]{2,0,1:T(2,128)} %param.26) | copy-start | bytes 110596
  415.5 6.4 %slice-start = ((s8[4915200]{0:T(1024)(128)(4,1)}), s8[4194304]{0:T(1024)(128)(4,1)S(1)}, s32[]{:S(2)}) async-start(s8[4915200]{0:T(1024)(128)(4,1)} %bitcast.25), calls=%async_computation | async-start | bytes 8388608
  415.5 6.3 %slice-start.1 = ((s8[4915200]{0:T(1024)(128)(4,1)}), s8[720896]{0:T(1024)(128)(4,1)S(1)}, s32[]{:S(2)}) async-start(s8[4915200]{0:T(1024)(128)(4,1)} %bitcast.25), calls=%async_computation.1 | async-start | bytes 1441792
